TPU v7x, 128 devices: a whole 4x4x4 slice. The times are simulated.
128 devices in a mesh: dp: 8 (over z, x_hi), chan: 16 (over x_lo, y, core).
Axes of the slice: x: 4 (x_hi: 2, x_lo: 2; x = x_hi * 2 + x_lo), y: 4, z: 4, core: 2. Of those that a mesh axis runs over, the one named last changes fastest.
Arguments:
- tokens: bfloat16 [8192, 8192], P('dp', 'chan'), may hold values from -6 to 6
- first_up: bfloat16 [32, 256, 256], P('chan'), may hold values from -0.375 to 0.375
- second_up: bfloat16 [32, 256, 1024], P('chan'), may hold values from -0.375 to 0.375
- first_down: bfloat16 [32, 1024, 256], P('chan'), may hold values from -0.1875 to 0.1875
- second_down: bfloat16 [32, 256, 256], P('chan'), may hold values from -0.375 to 0.375
- perm_up: int32 [8192], replicated, may hold values from 0 to 8191, as said below
- perm_down: int32 [8192], replicated, may hold values from 0 to 8191, as said below
- cotangent: bfloat16 [8192, 8192], P('dp', 'chan'), may hold values from -6 to 6
Outputs:
- mixed: bfloat16 [8192, 8192], P('dp', 'chan')
- input_grad: bfloat16 [8192, 8192], P('dp', 'chan')
- grad_first_up: float32 [32, 256, 256], P('chan')
- grad_second_up: float32 [32, 256, 1024], P('chan')
- grad_first_down: float32 [32, 1024, 256], P('chan')
- grad_second_down: float32 [32, 256, 256], P('chan')
Inputs may be any that keep to these rules, and one draw needn't show every extreme that they name: `perm_up`: A permutation of the channels; of the outputs j in one aligned group of 512 channels, exactly 32 take their source from each aligned group of 512 channels. `perm_down`: as perm_up, drawn independently.
All inputs are finite; a program needn't handle non-finite values.
Results may differ from a plain program's by a relative error of at most 0.007.
Values may be sent and summed in bfloat16 or wider, within the bound.
No kernel may reach another device: no remote copies, remote signals or barrier semaphores. Data moves between devices by JAX's collectives and lax.ppermute only.
A program may use at most 128 MiB of HBM per device.

v0:
```python
import jax
import jax.numpy as jnp
from jax import lax
from jax.sharding import PartitionSpec as P


def gelu_tanh(inputs):
    return jax.nn.gelu(inputs, approximate=True)


def block_apply(inputs, weight):
    row_count = inputs.shape[0]
    blocks = weight.shape[0]
    pieces = inputs.reshape(row_count, blocks, weight.shape[1])
    result = jnp.einsum("rki,kio->rko", pieces, weight, preferred_element_type=jnp.float32)
    return result.reshape(row_count, blocks * weight.shape[2])


def block_back(grads, weight):
    row_count = grads.shape[0]
    blocks = weight.shape[0]
    pieces = grads.reshape(row_count, blocks, weight.shape[2])
    result = jnp.einsum("rko,kio->rki", pieces, weight, preferred_element_type=jnp.float32)
    return result.reshape(row_count, blocks * weight.shape[1])


def block_grad(inputs, grads, weight):
    row_count = inputs.shape[0]
    blocks = weight.shape[0]
    left = inputs.reshape(row_count, blocks, weight.shape[1])
    right = grads.reshape(row_count, blocks, weight.shape[2])
    return jnp.einsum("rki,rko->kio", left, right, preferred_element_type=jnp.float32)


def prepare(routing):
    return (routing, jnp.argsort(routing))


def route(values, plan_tables, inverse):
    whole_rows = lax.all_to_all(values, "chan", split_axis=0, concat_axis=1, tiled=True)
    column_table = plan_tables[1] if inverse else plan_tables[0]
    shifted = whole_rows[:, column_table]
    return lax.all_to_all(shifted, "chan", split_axis=1, concat_axis=0, tiled=True)


def per_device(tokens, first_up, second_up, first_down, second_down, perm_up, perm_down, cotangent):
    plan_up = prepare(perm_up)
    plan_down = prepare(perm_down)
    first_act = block_apply(tokens, first_up).astype(jnp.bfloat16)
    mixed_in = route(first_act, plan_up, False)
    hidden = block_apply(mixed_in, second_up)
    activated, gelu_back = jax.vjp(gelu_tanh, hidden)
    act_low = activated.astype(jnp.bfloat16)
    narrowed = block_apply(act_low, first_down).astype(jnp.bfloat16)
    routed = route(narrowed, plan_down, False)
    mixed = block_apply(routed, second_down).astype(jnp.bfloat16)
    grad_sd = block_grad(routed, cotangent, second_down)
    routed_grad = block_back(cotangent, second_down).astype(jnp.bfloat16)
    narrowed_grad = route(routed_grad, plan_down, True)
    grad_fd = block_grad(act_low, narrowed_grad, first_down)
    act_grad = block_back(narrowed_grad, first_down)
    hidden_grad = gelu_back(act_grad)[0].astype(jnp.bfloat16)
    grad_su = block_grad(mixed_in, hidden_grad, second_up)
    mixed_grad = block_back(hidden_grad, second_up).astype(jnp.bfloat16)
    first_grad = route(mixed_grad, plan_up, True)
    grad_fu = block_grad(tokens, first_grad, first_up)
    input_grad = block_back(first_grad, first_up).astype(jnp.bfloat16)
    grad_fu, grad_su, grad_fd, grad_sd = lax.psum((grad_fu, grad_su, grad_fd, grad_sd), "dp")
    return (mixed, input_grad, grad_fu, grad_su, grad_fd, grad_sd)


def solution(mesh):
    placed = (
        P("dp", "chan"),
        P("chan", None, None),
        P("chan", None, None),
        P("chan", None, None),
        P("chan", None, None),
        P(),
        P(),
        P("dp", "chan"),
    )
    return jax.shard_map(
        per_device,
        mesh=mesh,
        in_specs=placed,
        out_specs=(
            P("dp", "chan"),
            P("dp", "chan"),
            P("chan", None, None),
            P("chan", None, None),
            P("chan", None, None),
            P("chan", None, None),
        ),
        check_vma=False,
    )
```

profile of v0, /device:TPU:24, one launch (start us, length us, event | category | flops | bytes accessed | tf_op | source)
XLA Modules:
  0.0 530.9 jit_solution(5941073909474705803)
XLA Ops:
  11.5 5.6 %all-to-all-start = ((bf16[16,64,512]{2,1,0:T(8,128)(2,1)}), bf16[16,64,512]{2,1,0:T(8,128)(2,1)S(1)}, u32[]{:S(2)}, u32[]{:S(2)}) async-start(bf16[16,64,512]{2,1,0:T(8,128)(2,1)} %convert_element_type.68), calls=%async_computation | async-start | bytes 2097152 | tf_op jit(solution)/shard_map/all_to_all | solution.py:40
  22.6 9.4 %all-to-all-done = bf16[16,64,512]{2,1,0:T(8,128)(2,1)S(1)} async-done(((bf16[16,64,512]{2,1,0:T(8,128)(2,1)}), bf16[16,64,512]{2,1,0:T(8,128)(2,1)S(1)}, u32[]{:S(2)}, u32[]{:S(2)}) %all-to-all-start) | async-done | bytes 1048608 | tf_op jit(solution)/shard_map/all_to_all | solution.py:40
  32.1 5.9 %all-to-all-start.4 = ((bf16[16,64,512]{2,1,0:T(8,128)(2,1)}), bf16[16,64,512]{2,1,0:T(8,128)(2,1)}, u32[]{:S(2)}, u32[]{:S(2)}) async-start(bf16[16,64,512]{2,1,0:T(8,128)(2,1)} %convert_element_type.78), calls=%async_computation.4 | async-start | bytes 2097152 | tf_op jit(solution)/shard_map/all_to_all | solution.py:40
  40.0 29.5 %gather_fusion = bf16[8192,64]{1,0:T(8,128)(2,1)} fusion(bf16[64,8192]{0,1:T(8,128)(2,1)S(1)} %bitcast.96, s32[8192]{0:T(1024)S(1)} %fusion.27), kind=kCustom, calls=%fused_computation | custom fusion | bytes 2129920 | tf_op jit(solution)/shard_map/gather | solution.py:42
  72.2 5.8 %all-to-all-start.1 = ((bf16[64,16,512]{2,0,1:T(8,128)(2,1)}), bf16[64,16,512]{2,0,1:T(8,128)(2,1)}, u32[]{:S(2)}, u32[]{:S(2)}) async-start(bf16[64,16,512]{2,0,1:T(8,128)(2,1)} %copy.33), calls=%async_computation.1 | async-start | bytes 2097152 | tf_op jit(solution)/shard_map/all_to_all | solution.py:43
  78.0 6.8 %sort.31 = (s32[8192]{0:T(1024)}, s32[8192]{0:T(1024)S(1)}) sort(s32[8192]{0:T(1024)S(1)} %copy-done.15, s32[8192]{0:T(1024)S(1)} %iota.7), dimensions={0}, to_apply=%region_0.0 | sort | flops 106496 | bytes 131072 | tf_op jit(solution)/shard_map/jit(argsort)/sort | solution.py:36
  86.8 29.5 %gather_fusion.2 = bf16[8192,64]{1,0:T(8,128)(2,1)} fusion(bf16[64,8192]{0,1:T(8,128)(2,1)S(1)} %bitcast.97, s32[8192]{0:T(1024)S(1)} %fusion.29), kind=kCustom, calls=%fused_computation.2 | custom fusion | bytes 2129920 | tf_op jit(solution)/shard_map/gather | solution.py:42
  119.0 5.7 %all-to-all-start.5 = ((bf16[64,16,512]{2,0,1:T(8,128)(2,1)}), bf16[64,16,512]{2,0,1:T(8,128)(2,1)S(1)}, u32[]{:S(2)}, u32[]{:S(2)}) async-start(bf16[64,16,512]{2,0,1:T(8,128)(2,1)} %copy.43), calls=%async_computation.5 | async-start | bytes 2097152 | tf_op jit(solution)/shard_map/all_to_all | solution.py:43
  129.3 10.3 %all-to-all-done.5 = bf16[64,16,512]{2,0,1:T(8,128)(2,1)S(1)} async-done(((bf16[64,16,512]{2,0,1:T(8,128)(2,1)}), bf16[64,16,512]{2,0,1:T(8,128)(2,1)S(1)}, u32[]{:S(2)}, u32[]{:S(2)}) %all-to-all-start.5) | async-done | bytes 1048608 | tf_op jit(solution)/shard_map/all_to_all | solution.py:43
  140.7 4.5 fusion.10
  145.2 6.8 %fusion.6 = bf16[1024,2,1024]{2,0,1:T(8,128)(2,1)S(1)} fusion(f32[2,1024,1024]{2,1,0:T(8,128)S(1)} %get-tuple-element.27, bf16[2,1024,256]{2,1,0:T(8,128)(2,1)S(1)} %copy-done.16, bf16[1024,2,256]{2,1,0:T(2,128)(2,1)S(1)} %copy-done.11), kind=kOutput, calls=%fused_computation.12 | convolution fusion | flops 1115684864 | bytes 14680064 | tf_op jit(solution)/shard_map/rko,kio->rki/dot_general | solution.py:23
  157.9 5.3 all-to-all-start.6
  163.2 3.4 fusion.12
  169.2 8.9 %all-to-all-done.6 = bf16[16,64,512]{2,1,0:T(8,128)(2,1)S(1)} async-done(((bf16[16,64,512]{2,1,0:T(8,128)(2,1)}), bf16[16,64,512]{2,1,0:T(8,128)(2,1)S(1)}, u32[]{:S(2)}, u32[]{:S(2)}) %all-to-all-start.6) | async-done | bytes 1048608 | tf_op jit(solution)/shard_map/all_to_all | solution.py:40
  178.1 5.3 all-to-all-start.2
  183.4 6.8 %sort.32 = (s32[8192]{0:T(1024)}, s32[8192]{0:T(1024)S(1)}) sort(s32[8192]{0:T(1024)S(1)} %copy-done.14, s32[8192]{0:T(1024)S(1)} %iota.8), dimensions={0}, to_apply=%region_1.2 | sort | flops 106496 | bytes 131072 | tf_op jit(solution)/shard_map/jit(argsort)/sort | solution.py:36
  192.2 29.5 %gather_fusion.3 = bf16[8192,64]{1,0:T(8,128)(2,1)} fusion(bf16[64,8192]{0,1:T(8,128)(2,1)S(1)} %bitcast.98, s32[8192]{0:T(1024)S(1)} %fusion.30), kind=kCustom, calls=%fused_computation.3 | custom fusion | bytes 2129920 | tf_op jit(solution)/shard_map/gather | solution.py:42
  224.4 5.8 %all-to-all-start.7 = ((bf16[64,16,512]{2,0,1:T(8,128)(2,1)}), bf16[64,16,512]{2,0,1:T(8,128)(2,1)}, u32[]{:S(2)}, u32[]{:S(2)}) async-start(bf16[64,16,512]{2,0,1:T(8,128)(2,1)} %copy.47), calls=%async_computation.7 | async-start | bytes 2097152 | tf_op jit(solution)/shard_map/all_to_all | solution.py:43
  231.3 29.5 %gather_fusion.1 = bf16[8192,64]{1,0:T(8,128)(2,1)} fusion(bf16[64,8192]{0,1:T(8,128)(2,1)S(1)} %bitcast.99, s32[8192]{0:T(1024)S(1)} %fusion.28), kind=kCustom, calls=%fused_computation.1 | custom fusion | bytes 2129920 | tf_op jit(solution)/shard_map/gather | solution.py:42
  263.5 5.7 %all-to-all-start.3 = ((bf16[64,16,512]{2,0,1:T(8,128)(2,1)}), bf16[64,16,512]{2,0,1:T(8,128)(2,1)S(1)}, u32[]{:S(2)}, u32[]{:S(2)}) async-start(bf16[64,16,512]{2,0,1:T(8,128)(2,1)} %copy.37), calls=%async_computation.3 | async-start | bytes 2097152 | tf_op jit(solution)/shard_map/all_to_all | solution.py:43
  269.3 4.9 fusion.31
  274.2 3.1 fusion.24
  293.0 223.5 %all-reduce.3.cloned.1.call-done = (f32[2,256,256]{1,2,0:T(8,128)}, f32[2,256,1024]{2,1,0:T(8,128)}, f32[2,1024,256]{2,1,0:T(8,128)}, f32[2,256,256]{2,1,0:T(8,128)}) async-done(((f32[2,256,256]{1,2,0:T(8,128)}, f32[2,256,1024]{2,1,0:T(8,128)}, f32[2,1024,256]{2,1,0:T(8,128)}, f32[2,256,256]{2,1,0:T(8,128)}), (f32[2,256,256]{1,2,0:T(8,128)}, f32[2,256,1024]{2,1,0:T(8,128)}, f32[2,1024,256]{2,1,0:T(8,128)}, ...) | async-done | bytes 5242896 | tf_op jit(solution)/shard_map/psum | solution.py:68
  518.6 3.3 copy.88
  (84 shorter events, 61.8 us)
Async XLA Ops:
  7.2 133.6 %copy-start = (bf16[2,256,1024]{2,1,0:T(8,128)(2,1)S(1)}, bf16[2,256,1024]{2,1,0:T(8,128)(2,1)}, u32[]{:S(2)}) copy-start(bf16[2,256,1024]{2,1,0:T(8,128)(2,1)} %param.10) | copy-start | bytes 3145732
  7.2 10.0 %copy-start.9 = (bf16[2,256,256]{2,1,0:T(8,128)(2,1)S(1)}, bf16[2,256,256]{2,1,0:T(8,128)(2,1)}, u32[]{:S(2)}) copy-start(bf16[2,256,256]{2,1,0:T(8,128)(2,1)} %param.12) | copy-start | bytes 786436
  10.0 7.1 %copy-start.10 = (bf16[1024,512]{1,0:T(8,128)(2,1)S(1)}, bf16[1024,512]{1,0:T(8,128)(2,1)}, u32[]{:S(2)}) copy-start(bf16[1024,512]{1,0:T(8,128)(2,1)} %param.15) | copy-start | bytes 3145732
  11.5 20.5 %all-to-all-start = ((bf16[16,64,512]{2,1,0:T(8,128)(2,1)}), bf16[16,64,512]{2,1,0:T(8,128)(2,1)S(1)}, u32[]{:S(2)}, u32[]{:S(2)}) async-start(bf16[16,64,512]{2,1,0:T(8,128)(2,1)} %convert_element_type.68), calls=%async_computation | async-start | bytes 2097152 | tf_op jit(solution)/shard_map/all_to_all | solution.py:40
  17.2 20.8 %copy-start.14 = (s32[8192]{0:T(1024)S(1)}, s32[8192]{0:T(1024)}, u32[]{:S(2)}) copy-start(s32[8192]{0:T(1024)} %param.13) | copy-start | bytes 98308
  32.1 5.9 %copy-start.6 = (bf16[16,64,512]{2,1,0:T(8,128)(2,1)}, bf16[16,64,512]{2,1,0:T(8,128)(2,1)S(1)}, u32[]{:S(2)}) copy-start(bf16[16,64,512]{2,1,0:T(8,128)(2,1)S(1)} %all-to-all-done) | copy-start | bytes 3145732
  32.1 40.1 %all-to-all-start.4 = ((bf16[16,64,512]{2,1,0:T(8,128)(2,1)}), bf16[16,64,512]{2,1,0:T(8,128)(2,1)}, u32[]{:S(2)}, u32[]{:S(2)}) async-start(bf16[16,64,512]{2,1,0:T(8,128)(2,1)} %convert_element_type.78), calls=%async_computation.4 | async-start | bytes 2097152 | tf_op jit(solution)/shard_map/all_to_all | solution.py:40
  69.5 8.5 %copy-start.15 = (s32[8192]{0:T(1024)S(1)}, s32[8192]{0:T(1024)}, u32[]{:S(2)}) copy-start(s32[8192]{0:T(1024)} %param.14) | copy-start | bytes 98308
  72.2 46.8 %all-to-all-start.1 = ((bf16[64,16,512]{2,0,1:T(8,128)(2,1)}), bf16[64,16,512]{2,0,1:T(8,128)(2,1)}, u32[]{:S(2)}, u32[]{:S(2)}) async-start(bf16[64,16,512]{2,0,1:T(8,128)(2,1)} %copy.33), calls=%async_computation.1 | async-start | bytes 2097152 | tf_op jit(solution)/shard_map/all_to_all | solution.py:43
  119.0 20.6 %all-to-all-start.5 = ((bf16[64,16,512]{2,0,1:T(8,128)(2,1)}), bf16[64,16,512]{2,0,1:T(8,128)(2,1)S(1)}, u32[]{:S(2)}, u32[]{:S(2)}) async-start(bf16[64,16,512]{2,0,1:T(8,128)(2,1)} %copy.43), calls=%async_computation.5 | async-start | bytes 2097152 | tf_op jit(solution)/shard_map/all_to_all | solution.py:43
  129.3 15.9 %copy-start.3 = (bf16[1024,2,256]{0,2,1:T(8,128)(2,1)}, bf16[1024,2,256]{0,2,1:T(8,128)(2,1)S(1)}, u32[]{:S(2)}) copy-start(bf16[1024,2,256]{0,2,1:T(8,128)(2,1)S(1)} %copy.51) | copy-start | bytes 3145732
  140.7 4.5 copy-start.16
  157.9 20.2 %all-to-all-start.6 = ((bf16[16,64,512]{2,1,0:T(8,128)(2,1)}), bf16[16,64,512]{2,1,0:T(8,128)(2,1)S(1)}, u32[]{:S(2)}, u32[]{:S(2)}) async-start(bf16[16,64,512]{2,1,0:T(8,128)(2,1)} %convert_element_type.82), calls=%async_computation.6 | async-start | bytes 2097152 | tf_op jit(solution)/shard_map/all_to_all | solution.py:40
  178.1 12.1 %copy-start.5 = (bf16[16,64,512]{2,1,0:T(8,128)(2,1)}, bf16[16,64,512]{2,1,0:T(8,128)(2,1)S(1)}, u32[]{:S(2)}) copy-start(bf16[16,64,512]{2,1,0:T(8,128)(2,1)S(1)} %all-to-all-done.6) | copy-start | bytes 3145732
  178.1 46.3 %all-to-all-start.2 = ((bf16[16,64,512]{2,1,0:T(8,128)(2,1)}), bf16[16,64,512]{2,1,0:T(8,128)(2,1)S(1)}, u32[]{:S(2)}, u32[]{:S(2)}) async-start(bf16[16,64,512]{2,1,0:T(8,128)(2,1)} %convert_element_type.72), calls=%async_computation.2 | async-start | bytes 2097152 | tf_op jit(solution)/shard_map/all_to_all | solution.py:40
  224.4 39.1 %all-to-all-start.7 = ((bf16[64,16,512]{2,0,1:T(8,128)(2,1)}), bf16[64,16,512]{2,0,1:T(8,128)(2,1)}, u32[]{:S(2)}, u32[]{:S(2)}) async-start(bf16[64,16,512]{2,0,1:T(8,128)(2,1)} %copy.47), calls=%async_computation.7 | async-start | bytes 2097152 | tf_op jit(solution)/shard_map/all_to_all | solution.py:43
  260.7 8.6 %copy-start.4 = (bf16[1024,2,256]{0,2,1:T(8,128)(2,1)S(1)}, bf16[1024,2,256]{0,2,1:T(8,128)(2,1)}, u32[]{:S(2)}) copy-start(bf16[1024,2,256]{0,2,1:T(8,128)(2,1)} %copy-done.3) | copy-start | bytes 3145732
  263.5 20.6 %all-to-all-start.3 = ((bf16[64,16,512]{2,0,1:T(8,128)(2,1)}), bf16[64,16,512]{2,0,1:T(8,128)(2,1)S(1)}, u32[]{:S(2)}, u32[]{:S(2)}) async-start(bf16[64,16,512]{2,0,1:T(8,128)(2,1)} %copy.37), calls=%async_computation.3 | async-start | bytes 2097152 | tf_op jit(solution)/shard_map/all_to_all | solution.py:43
  269.2 5.0 copy-start.12
  269.3 247.2 %all-reduce.3.cloned.1.call-start = ((), (), s32[]{:S(2)}) async-start(), calls=%async_computation.8 | async-start | bytes 10485760 | tf_op jit(solution)/shard_map/psum | solution.py:68
  269.3 4.9 copy-start.17
  516.4 5.5 %copy-start.7 = (f32[2,1024,256]{2,1,0:T(8,128)S(1)}, f32[2,1024,256]{2,1,0:T(8,128)}, u32[]{:S(2)}) copy-start(f32[2,1024,256]{2,1,0:T(8,128)} %get-tuple-element.32) | copy-start | bytes 6291460
  518.6 5.4 %copy-start.1 = (bf16[2,256,1024]{2,1,0:T(8,128)(2,1)S(1)}, bf16[2,256,1024]{2,1,0:T(8,128)(2,1)}, u32[]{:S(2)}) copy-start(bf16[2,256,1024]{2,1,0:T(8,128)(2,1)} %param.10) | copy-start | bytes 3145732
  518.6 4.6 copy-start.13
  (3 other events, 9.0 us)
Sparse Core Ops, SparseCore 0:
  288.6 227.8 all-reduce.2
where the time goes:
time: 533 us; the launch traced here: 531 us
  waiting for transfers between devices  254 us (48%)
  local copies, waits for them, and re-layouts  170 us (32%)
  starting transfers between devices  45.1 us (8%)
  matrix products  34.2 us (6%)
  between operations  14.3 us (3%)
  other arithmetic  13.6 us (3%)
    psum x1, waiting for transfers between devices, per_device(): lax.psum((grad_fu, grad_su, grad_fd, grad_sd), 'dp')  223 us
    gather x4, local copies, waits for them, and re-layouts, route(): shifted = whole_rows[:, column_table]  118 us
    all_to_all x4, starting transfers between devices, route(): lax.all_to_all(shifted, 'chan', split_axis=1, concat_axis=0, tiled=True)  23 us
    all_to_all x4, starting transfers between devices, route(): lax.all_to_all(values, 'chan', split_axis=0, concat_axis=1, tiled=True)  22.1 us
    all_to_all x4, waiting for transfers between devices, route(): lax.all_to_all(values, 'chan', split_axis=0, concat_axis=1, tiled=True)  18.4 us
    sort x2, other arithmetic, prepare(): return (routing, jnp.argsort(routing))  13.5 us
    dot_general x4, matrix products, block_grad(): jnp.einsum('rki,rko->kio', left, right, preferred_element_type=jnp.float32)  13 us
    unnamed x42, local copies, waits for them, and re-layouts  12.3 us
  transfers between devices with their start and end apart: 9, of which 5 were waited for; matrix products, arithmetic and copies ran while one was open for 35% of the time, Pallas kernels for 0%

commit v1 on v0

v1 whole, which is shorter than its diff:
```python
import jax
import jax.numpy as jnp
from jax import lax
from jax.experimental import pallas as pl
from jax.experimental.pallas import tpu as pltpu
from jax.sharding import PartitionSpec as P

BF = jnp.bfloat16
F32 = jnp.float32
GELU_C = 0.7978845608028654
GELU_A = 0.044715
VMEM_BYTES = 56 * 2**20


def nn(left, right):
    return lax.dot_general(left, right, (((1,), (0,)), ((), ())), preferred_element_type=F32)


def nt(left, right):
    return lax.dot_general(left, right, (((1,), (1,)), ((), ())), preferred_element_type=F32)


def tn(left, right):
    return lax.dot_general(left, right, (((0,), (0,)), ((), ())), preferred_element_type=F32)


def one_hots(perm_ref, me, before, source_ref, target_ref):
    perm = perm_ref[...]
    slot = lax.broadcasted_iota(jnp.int32, (32, 512), 0).astype(F32)
    lane = lax.broadcasted_iota(jnp.int32, (32, 512), 1).astype(F32)
    group = lax.shift_right_logical(perm, 9)
    mine = group == me
    rank = nn(jnp.where(mine, 1.0, 0.0).astype(BF), before)
    rank = jnp.where(mine, rank, -1.0)
    local = (perm & 511).astype(F32)
    for r in range(16):
        hit = rank[r : r + 1, :] == slot
        channel = jnp.sum(jnp.where(hit, local[r : r + 1, :], 0.0), axis=1, keepdims=True)
        source_ref[32 * r : 32 * r + 32, :] = jnp.where(channel == lane, 1.0, 0.0).astype(BF)
    row = lax.shift_right_logical(perm_ref[pl.ds(me, 1), :], 9)
    from_group = row == lax.broadcasted_iota(jnp.int32, (16, 512), 0)
    rank = nn(jnp.where(from_group, 1.0, 0.0).astype(BF), before)
    rank = jnp.where(from_group, rank, -1.0)
    for s in range(16):
        target_ref[32 * s : 32 * s + 32, :] = jnp.where(rank[s : s + 1, :] == slot, 1.0, 0.0).astype(BF)


def stage_one(tok_ref, cot_ref, fu_ref, sd_ref, pu_ref, pd_ref, out_ref, su_ref, tu_ref, sdn_ref, tdn_ref, wu_ref, wd_ref):
    me = lax.axis_index("chan")
    before = jnp.where(
        lax.broadcasted_iota(jnp.int32, (512, 512), 0) < lax.broadcasted_iota(jnp.int32, (512, 512), 1), 1.0, 0.0
    ).astype(BF)
    one_hots(pu_ref, me, before, su_ref, tu_ref)
    one_hots(pd_ref, me, before, sdn_ref, tdn_ref)
    for k in range(2):
        cols = slice(256 * k, 256 * k + 256)
        wu_ref[:, cols] = nt(su_ref[:, cols], fu_ref[k]).astype(BF)
        wd_ref[:, cols] = nn(tdn_ref[:, cols], sd_ref[k]).astype(BF)
    out_ref[:, 0:32, :] = nt(wu_ref[...], tok_ref[...]).astype(BF).reshape(16, 32, 1024)
    out_ref[:, 32:64, :] = nt(wd_ref[...], cot_ref[...]).astype(BF).reshape(16, 32, 1024)


def stage_two(r_ref, tu_ref, sdn_ref, su_ref, fd_ref, out_ref, g0, g1, g2, g3, act, hg, nar, mix, parts, sems):
    mixed_in = tn(tu_ref[...], r_ref[:, 0:32, :].reshape(512, 1024)).astype(BF)
    nar_grad = tn(sdn_ref[...], r_ref[:, 32:64, :].reshape(512, 1024)).astype(BF)
    for k in range(2):
        mi = mixed_in[256 * k : 256 * k + 256, :]
        ng = nar_grad[256 * k : 256 * k + 256, :]
        for c in range(4):
            units = slice(256 * c, 256 * c + 256)
            v = tn(su_ref[k, :, units], mi)
            up = nn(fd_ref[k, units, :], ng)
            sq = v * v
            h = 0.5 + 0.5 * jnp.tanh(v * (GELU_C + (GELU_C * GELU_A) * sq))
            a = (v * h).astype(BF)
            d = v * ((2 * GELU_C) + (6 * GELU_C * GELU_A) * sq)
            b = (up * (h * (1.0 + (1.0 - h) * d))).astype(BF)
            act[units, :] = a
            hg[units, :] = b
            gsu = nt(mi, b).astype(BF)
            gfd = nt(a, ng).astype(BF)
            for i in range(2):
                rows = slice(128 * i, 128 * i + 128)
                parts[2 * k + i, 0:128, units] = gsu[rows, :]
                at = (c % 2) * 512 + 256 * i
                parts[2 * k + c // 2, 128:256, at : at + 256] = gfd[rows, :]
        nar[256 * k : 256 * k + 256, :] = tn(fd_ref[k], act[...]).astype(BF)
        mix[256 * k : 256 * k + 256, :] = nn(su_ref[k], hg[...]).astype(BF)
    z = lax.shift_right_logical(lax.axis_index("dp"), 1)
    copies = [
        pltpu.make_async_copy(parts.at[(z + i) & 3], g, sems.at[i]) for i, g in enumerate((g0, g1, g2, g3))
    ]
    for copy in copies:
        copy.start()
    out_ref[:, 0:32, :] = nn(sdn_ref[...], nar[...]).astype(BF).reshape(16, 32, 1024)
    out_ref[:, 32:64, :] = nn(tu_ref[...], mix[...]).astype(BF).reshape(16, 32, 1024)
    for copy in copies:
        copy.wait()


def stage_three(r_ref, tok_ref, cot_ref, su_ref, tdn_ref, wu_ref, wd_ref, mixed_ref, ig_ref, t_ref):
    rc = r_ref[:, 0:32, :].reshape(512, 1024)
    rd = r_ref[:, 32:64, :].reshape(512, 1024)
    sd_slots = nn(rc, cot_ref[...]).astype(BF)
    fu_slots = nn(rd, tok_ref[...]).astype(BF)
    for k in range(2):
        cols = slice(256 * k, 256 * k + 256)
        gsd = tn(tdn_ref[:, cols], sd_slots[:, cols]).astype(BF)
        gfu = tn(fu_slots[:, cols], su_ref[:, cols]).astype(BF)
        for i in range(4):
            rows = slice(64 * i, 64 * i + 64)
            t_ref[4 * k + i, :, 0:256] = gsd[rows, :]
            t_ref[4 * k + i, :, 256:512] = gfu[rows, :]
    mixed_ref[...] = tn(rc, wd_ref[...]).astype(BF)
    ig_ref[...] = tn(rd, wu_ref[...]).astype(BF)


def finish(f0, f1, f2, f3, t_ref, gfu_ref, gsu_ref, gfd_ref, gsd_ref, parts, sems):
    z = lax.shift_right_logical(lax.axis_index("dp"), 1)
    copies = [
        pltpu.make_async_copy(f, parts.at[(z - i) & 3], sems.at[i]) for i, f in enumerate((f0, f1, f2, f3))
    ]
    for copy in copies:
        copy.start()
    for k in range(2):
        for i in range(4):
            rows = slice(64 * i, 64 * i + 64)
            gsd_ref[k, rows, :] = t_ref[4 * k + i, :, 0:256].astype(F32)
            gfu_ref[k, rows, :] = t_ref[4 * k + i, :, 256:512].astype(F32)
    for copy in copies:
        copy.wait()
    for c in range(4):
        k, half = c // 2, c % 2
        gsu_ref[k, 128 * half : 128 * half + 128, :] = parts[c, 0:128, :].astype(F32)
        for b in range(4):
            at = 512 * half + 128 * b
            gfd_ref[k, at : at + 128, :] = parts[c, 128:256, 256 * b : 256 * b + 256].astype(F32)


def like(*shape, dtype=BF):
    return jax.ShapeDtypeStruct(shape, dtype)


def whole(count):
    return [pl.BlockSpec(memory_space=pltpu.VMEM)] * count


def placed_anywhere(count):
    return [pl.BlockSpec(memory_space=pl.ANY)] * count


PARAMS = pltpu.CompilerParams(vmem_limit_bytes=VMEM_BYTES)


def shift_z(step):
    return [(2 * z + x, 2 * ((z + step) % 4) + x) for z in range(4) for x in range(2)]


SWAP_X = [(2 * z + x, 2 * z + 1 - x) for z in range(4) for x in range(2)]


def exchange(values, axis):
    return lax.all_to_all(values, axis, split_axis=0, concat_axis=0, tiled=True)


def per_device(tokens, first_up, second_up, first_down, second_down, perm_up, perm_down, cotangent):
    square = like(512, 512)
    sent, up_src, up_tgt, down_src, down_tgt, w_up, w_down = pl.pallas_call(
        stage_one,
        out_shape=(like(16, 64, 1024),) + (square,) * 6,
        in_specs=whole(6),
        out_specs=whole(7),
        compiler_params=PARAMS,
        name="stage_one",
    )(tokens, cotangent, first_up, second_down, perm_up.reshape(16, 512), perm_down.reshape(16, 512))
    got = exchange(sent, "chan")
    part = like(256, 1024)
    sent, g0, g1, g2, g3 = pl.pallas_call(
        stage_two,
        out_shape=(like(16, 64, 1024), part, part, part, part),
        in_specs=whole(5),
        out_specs=whole(1) + placed_anywhere(4),
        scratch_shapes=[
            pltpu.VMEM((1024, 1024), BF),
            pltpu.VMEM((1024, 1024), BF),
            pltpu.VMEM((512, 1024), BF),
            pltpu.VMEM((512, 1024), BF),
            pltpu.VMEM((4, 256, 1024), BF),
            pltpu.SemaphoreType.DMA((4,)),
        ],
        compiler_params=PARAMS,
        name="stage_two",
    )(got, up_tgt, down_src, second_up, first_down)
    near = [lax.ppermute(g, "dp", shift_z(i + 1)) for i, g in enumerate((g1, g2, g3))]
    got = exchange(sent, "chan")
    mixed, input_grad, tail = pl.pallas_call(
        stage_three,
        out_shape=(like(1024, 512), like(1024, 512), like(8, 64, 512)),
        in_specs=whole(7),
        out_specs=whole(3),
        compiler_params=PARAMS,
        name="stage_three",
    )(got, tokens, cotangent, up_src, down_tgt, w_up, w_down)
    mine = (g0.astype(F32) + near[0].astype(F32) + near[1].astype(F32) + near[2].astype(F32)).astype(BF)
    other = lax.ppermute(mine, "dp", SWAP_X)
    f0 = (mine.astype(F32) + other.astype(F32)).astype(BF)
    far = [lax.ppermute(f0, "dp", shift_z(i)) for i in (1, 2, 3)]
    tail = exchange(tail, "dp")
    tail = jnp.sum(tail.astype(F32), axis=0).astype(BF)
    tail = exchange(jnp.broadcast_to(tail[None], (8, 64, 512)), "dp")
    grad_fu, grad_su, grad_fd, grad_sd = pl.pallas_call(
        finish,
        out_shape=(
            like(2, 256, 256, dtype=F32),
            like(2, 256, 1024, dtype=F32),
            like(2, 1024, 256, dtype=F32),
            like(2, 256, 256, dtype=F32),
        ),
        in_specs=placed_anywhere(4) + whole(1),
        out_specs=whole(4),
        scratch_shapes=[pltpu.VMEM((4, 256, 1024), BF), pltpu.SemaphoreType.DMA((4,))],
        compiler_params=PARAMS,
        name="finish",
    )(f0, *far, tail)
    return (mixed, input_grad, grad_fu, grad_su, grad_fd, grad_sd)


def solution(mesh):
    placed = (
        P("dp", "chan"),
        P("chan", None, None),
        P("chan", None, None),
        P("chan", None, None),
        P("chan", None, None),
        P(),
        P(),
        P("dp", "chan"),
    )
    return jax.shard_map(
        per_device,
        mesh=mesh,
        in_specs=placed,
        out_specs=(
            P("dp", "chan"),
            P("dp", "chan"),
            P("chan", None, None),
            P("chan", None, None),
            P("chan", None, None),
            P("chan", None, None),
        ),
        check_vma=False,
    )
```

time: 533 us -> 150 us (0.28)
  waiting for transfers between devices: 254 us -> 42 us
  local copies, waits for them, and re-layouts: 170 us -> 5.71 us
  matrix products: 34.2 us -> 0 us
  Pallas kernels: 0 us -> 31.9 us
  blocking collectives: 0 us -> 31.3 us
  between operations: 14.3 us -> 0.91 us
  other arithmetic: 13.6 us -> 0.63 us
  starting transfers between devices: 45.1 us -> 37.3 us
    psum x1 -> x0, waiting for transfers between devices: 223 us -> none  [per_device(): lax.psum((grad_fu, grad_su, grad_fd, grad_sd), 'dp')]
    gather x4 -> x0, local copies, waits for them, and re-layouts: 118 us -> none  [route(): shifted = whole_rows[:, column_table]]
    dot_general x12 -> x0, matrix products: 34.2 us -> none  [the longest x4 13 us: block_grad(): jnp.einsum('rki,rko->kio', left, right, preferred_element_type=jnp.float32)]
    pallas_call x0 -> x4, Pallas kernels: none -> 31.9 us  [the longest x1 15.3 us: per_device(): pl.pallas_call(stage_two, out_shape=(like(16, 64, 1024), part, part, part...]
    all_to_all x0 -> x1, blocking collectives: none -> 31.3 us  [exchange(): return lax.all_to_all(values, axis, split_axis=0, concat_axis=0, tiled=True)]
    ppermute x0 -> x7, waiting for transfers between devices: none -> 30.7 us  [the longest x3 22.4 us: per_device(): lax.ppermute(g, 'dp', shift_z(i + 1))]
    all_to_all x8 -> x3, starting transfers between devices: 45.1 us -> 23 us  [exchange(): return lax.all_to_all(values, axis, split_axis=0, concat_axis=0, tiled=True)]
    all_to_all x8 -> x3, waiting for transfers between devices: 30.2 us -> 11.3 us  [exchange(): return lax.all_to_all(values, axis, split_axis=0, concat_axis=0, tiled=True)]
  transfers between devices with their start and end apart: 9 -> 10, of which waited for: 5 -> 5; matrix products, arithmetic and copies ran while one was open for 35% -> 1% of each run, Pallas kernels for 0% -> 4%
where the time goes in v1:
time: 150 us
  waiting for transfers between devices  42 us (28%)
  starting transfers between devices  37.3 us (25%)
  Pallas kernels  31.9 us (21%)
  blocking collectives  31.3 us (21%)
  local copies, waits for them, and re-layouts  5.71 us (4%)
    all_to_all x1, blocking collectives, exchange(): return lax.all_to_all(values, axis, split_axis=0, concat_axis=0, tiled=True)  31.3 us
    all_to_all x3, starting transfers between devices, exchange(): return lax.all_to_all(values, axis, split_axis=0, concat_axis=0, tiled=True)  23 us
    ppermute x3, waiting for transfers between devices, per_device(): lax.ppermute(g, 'dp', shift_z(i + 1))  22.4 us
    pallas_call x1, Pallas kernels, per_device(): pl.pallas_call(stage_two, out_shape=(like(16, 64, 1024), part, part, part...  15.3 us
    all_to_all x3, waiting for transfers between devices, exchange(): return lax.all_to_all(values, axis, split_axis=0, concat_axis=0, tiled=True)  11.3 us
    ppermute x3, waiting for transfers between devices, per_device(): far = [lax.ppermute(f0, 'dp', shift_z(i)) for i in (1, 2, 3)]  8.27 us
    pallas_call x1, Pallas kernels, per_device(): pl.pallas_call(stage_three, out_shape=(like(1024, 512), like(1024, 512),...  6.63 us
    ppermute x3, starting transfers between devices, per_device(): lax.ppermute(g, 'dp', shift_z(i + 1))  6.51 us
  transfers between devices with their start and end apart: 10, of which 5 were waited for; matrix products, arithmetic and copies ran while one was open for 1% of the time, Pallas kernels for 4%

profile of v1, /device:TPU:24, one launch (start us, length us, event | category | flops | bytes accessed | tf_op | source)
XLA Modules:
  0.0 149.8 jit_solution(9963963134608309883)
XLA Ops:
  0.6 1.4 reshape.19.pu_ref
  2.0 1.4 reshape.20.pd_ref
  3.4 5.1 %stage_one.1 = (bf16[16,64,1024]{2,1,0:T(8,128)(2,1)}, bf16[512,512]{1,0:T(8,128)(2,1)}, bf16[512,512]{1,0:T(8,128)(2,1)}, bf16[512,512]{1,0:T(8,128)(2,1)}, bf1...) custom-call(bf16[1024,512]{1,0:T(8,128)(2,1)} %tok_ref.3, bf16[1024,512]{1,0:T(8,128)(2,1)} %cot_ref.3, ...), custom_call_target="tpu_custom_call" | custom-call | tf_op jit(solution)/shard_map/stage_one/pallas_call | solution.py:168
  8.4 31.3 %all_to_all.20.r_ref = bf16[16,64,1024]{2,1,0:T(8,128)(2,1)} all-to-all(bf16[16,64,1024]{2,1,0:T(8,128)(2,1)} %get-tuple-element.25), channel_id=1, replica_groups=mesh['dp'=8,'chan'=16] {'chan'}, dimensions={0} | all-to-all | bytes 4194304 | tf_op jit(solution)/shard_map/all_to_all | solution.py:163
  39.7 15.3 %stage_two.1 = (bf16[16,64,1024]{2,1,0:T(8,128)(2,1)}, bf16[256,1024]{1,0:T(8,128)(2,1)}, bf16[256,1024]{1,0:T(8,128)(2,1)}, bf16[256,1024]{1,0:T(8,128)(2,1)}, bf16[256,1024]{1,0:T(8,128)(2,1)}) custom-call(bf16[16,64,1024]{2,1,0:T(8,128)(2,1)} %all_to_all.20.r_ref, bf16[512,512]{1,0:T(8,128)(2,1)} %get-tuple-element.26.tu_ref, ...), custom_call_target="tpu_custom_call" | custom-call | tf_op jit(solution)/shard_map/stage_two/pallas_call | solution.py:178
  55.0 6.0 %all-to-all-start.1 = ((bf16[16,64,1024]{2,1,0:T(8,128)(2,1)}), bf16[16,64,1024]{2,1,0:T(8,128)(2,1)S(1)}, u32[]{:S(2)}, u32[]{:S(2)}) async-start(bf16[16,64,1024]{2,1,0:T(8,128)(2,1)} %get-tuple-element.28), calls=%async_computation.1 | async-start | bytes 4194304 | tf_op jit(solution)/shard_map/all_to_all | solution.py:163
  61.0 1.9 %collective-permute-start = (bf16[256,1024]{1,0:T(8,128)(2,1)}, bf16[256,1024]{1,0:T(8,128)(2,1)S(1)}, u32[]{:S(2)}, u32[]{:S(2)}) collective-permute-start(bf16[256,1024]{1,0:T(8,128)(2,1)} %get-tuple-element.36), channel_id=1, source_target_pairs={{0,32},{16,48},{32,64},{48,80},{64,96},{80,112},{96,0},{112,16},{1... | collective-permute-start | bytes 1572872 | tf_op jit(solution)/shard_map/ppermute | solution.py:194
  62.9 3.6 %collective-permute-start.1 = (bf16[256,1024]{1,0:T(8,128)(2,1)}, bf16[256,1024]{1,0:T(8,128)(2,1)S(1)}, u32[]{:S(2)}, u32[]{:S(2)}) collective-permute-start(bf16[256,1024]{1,0:T(8,128)(2,1)} %get-tuple-element.37), channel_id=1, source_target_pairs={{0,64},{16,80},{32,96},{48,112},{64,0},{80,16},{96,32},{112,48},{1... | collective-permute-start | bytes 1572872 | tf_op jit(solution)/shard_map/ppermute | solution.py:194
  66.5 1.0 collective-permute-start.2
  67.5 10.0 %collective-permute-done = bf16[256,1024]{1,0:T(8,128)(2,1)S(1)} collective-permute-done((bf16[256,1024]{1,0:T(8,128)(2,1)}, bf16[256,1024]{1,0:T(8,128)(2,1)S(1)}, u32[]{:S(2)}, u32[]{:S(2)}) %collective-permute-start) | collective-permute-done | bytes 524320 | tf_op jit(solution)/shard_map/ppermute | solution.py:194
  77.5 12.4 %collective-permute-done.1 = bf16[256,1024]{1,0:T(8,128)(2,1)S(1)} collective-permute-done((bf16[256,1024]{1,0:T(8,128)(2,1)}, bf16[256,1024]{1,0:T(8,128)(2,1)S(1)}, u32[]{:S(2)}, u32[]{:S(2)}) %collective-permute-start.1) | collective-permute-done | bytes 524320 | tf_op jit(solution)/shard_map/ppermute | solution.py:194
  90.3 2.8 %collective-permute-start.3 = (bf16[256,1024]{1,0:T(8,128)(2,1)S(1)}, bf16[256,1024]{1,0:T(8,128)(2,1)S(1)}, u32[]{:S(2)}, u32[]{:S(2)}) collective-permute-start(bf16[256,1024]{1,0:T(8,128)(2,1)S(1)} %add_convert_fusion.1), channel_id=1, source_target_pairs={{0,16},{16,0},{32,48},{48,32},{64,80},{80,64},{96,112},{112,96},{1... | collective-permute-start | bytes 1572872 | tf_op jit(solution)/shard_map/ppermute | solution.py:205
  93.1 1.3 copy-done
  94.4 6.6 %stage_three.1 = (bf16[1024,512]{1,0:T(8,128)(2,1)}, bf16[1024,512]{1,0:T(8,128)(2,1)}, bf16[8,64,512]{2,1,0:T(8,128)(2,1)}) custom-call(bf16[16,64,1024]{2,1,0:T(8,128)(2,1)} %copy-done, bf16[1024,512]{1,0:T(8,128)(2,1)} %tok_ref.3, bf16[1024,512]{1,0:T(8,128)(2,1)} %cot_ref.3, bf16[512,512]{1,0:T(8,128)(2,1)} %get-tuple-element.29.su_ref, ...), custom_call_target="tpu_custom_call" | custom-call | tf_op jit(solution)/shard_map/stage_three/pallas_call | solution.py:196
  101.0 4.8 %all-to-all-start.2 = ((bf16[8,64,512]{2,1,0:T(8,128)(2,1)}), bf16[8,64,512]{2,1,0:T(8,128)(2,1)S(1)}, u32[]{:S(2)}, u32[]{:S(2)}) async-start(bf16[8,64,512]{2,1,0:T(8,128)(2,1)} %get-tuple-element.39), calls=%async_computation.2 | async-start | bytes 1048576 | tf_op jit(solution)/shard_map/all_to_all | solution.py:163
  106.0 3.3 %collective-permute-start.6 = (bf16[256,1024]{1,0:T(8,128)(2,1)S(1)}, bf16[256,1024]{1,0:T(8,128)(2,1)S(1)}, u32[]{:S(2)}, u32[]{:S(2)}) collective-permute-start(bf16[256,1024]{1,0:T(8,128)(2,1)S(1)} %add_convert_fusion.f0), channel_id=1, source_target_pairs={{0,96},{16,112},{32,0},{48,16},{64,32},{80,48},{96,64},{112,80},{1... | collective-permute-start | bytes 1572872 | tf_op jit(solution)/shard_map/ppermute | solution.py:207
  109.3 0.9 collective-permute-start.5
  110.2 0.9 collective-permute-start.4
  111.1 7.2 %all-to-all-done.2 = bf16[8,64,512]{2,1,0:T(8,128)(2,1)S(1)} async-done(((bf16[8,64,512]{2,1,0:T(8,128)(2,1)}), bf16[8,64,512]{2,1,0:T(8,128)(2,1)S(1)}, u32[]{:S(2)}, u32[]{:S(2)}) %all-to-all-start.2) | async-done | bytes 524320 | tf_op jit(solution)/shard_map/all_to_all | solution.py:163
  118.3 0.8 broadcast_in_dim.2
  119.1 12.3 %all-to-all-start.3 = ((bf16[8,64,512]{2,1,0:T(8,128)(2,1)}), bf16[8,64,512]{2,1,0:T(8,128)(2,1)S(1)}, u32[]{:S(2)}, u32[]{:S(2)}) async-start(bf16[8,64,512]{2,1,0:T(8,128)(2,1)} %broadcast_in_dim.2), calls=%async_computation.3 | async-start | bytes 1048576 | tf_op jit(solution)/shard_map/all_to_all | solution.py:163
  131.4 8.3 %collective-permute-done.4.f1 = bf16[256,1024]{1,0:T(8,128)(2,1)S(1)} collective-permute-done((bf16[256,1024]{1,0:T(8,128)(2,1)S(1)}, bf16[256,1024]{1,0:T(8,128)(2,1)S(1)}, u32[]{:S(2)}, u32[]{:S(2)}) %collective-permute-start.4) | collective-permute-done | bytes 524320 | tf_op jit(solution)/shard_map/ppermute | solution.py:207
  139.7 4.2 %all-to-all-done.3.t_ref = bf16[8,64,512]{2,1,0:T(8,128)(2,1)S(1)} async-done(((bf16[8,64,512]{2,1,0:T(8,128)(2,1)}), bf16[8,64,512]{2,1,0:T(8,128)(2,1)S(1)}, u32[]{:S(2)}, u32[]{:S(2)}) %all-to-all-start.3) | async-done | bytes 524320 | tf_op jit(solution)/shard_map/all_to_all | solution.py:163
  144.7 5.0 %finish.1 = (f32[2,256,256]{2,1,0:T(8,128)}, f32[2,256,1024]{2,1,0:T(8,128)}, f32[2,1024,256]{2,1,0:T(8,128)}, f32[2,256,256]{2,1,0:T(8,128)}) custom-call(bf16[256,1024]{1,0:T(8,128)(2,1)} %copy-done.1, bf16[256,1024]{1,0:T(8,128)(2,1)} %copy-done.5, bf16[256,1024]{1,0:T(8,128)(2,1)} %copy-done.4, bf16[256,1024]{1,0:T(8,128)(2,1)} %copy-done.3, ...), custom_call_target="tpu_custom_call" | custom-call | tf_op jit(solution)/shard_map/finish/pallas_call | solution.py:211
  (23 shorter events, 1.4 us)
Async XLA Ops:
  55.0 11.5 %copy-start.7 = (bf16[256,1024]{1,0:T(8,128)(2,1)S(1)}, bf16[256,1024]{1,0:T(8,128)(2,1)}, u32[]{:S(2)}) copy-start(bf16[256,1024]{1,0:T(8,128)(2,1)} %get-tuple-element.38) | copy-start | bytes 1572868
  55.0 34.9 %copy-start.6 = (bf16[256,1024]{1,0:T(8,128)(2,1)S(1)}, bf16[256,1024]{1,0:T(8,128)(2,1)}, u32[]{:S(2)}) copy-start(bf16[256,1024]{1,0:T(8,128)(2,1)} %get-tuple-element.35) | copy-start | bytes 1572868
  55.0 38.0 %all-to-all-start.1 = ((bf16[16,64,1024]{2,1,0:T(8,128)(2,1)}), bf16[16,64,1024]{2,1,0:T(8,128)(2,1)S(1)}, u32[]{:S(2)}, u32[]{:S(2)}) async-start(bf16[16,64,1024]{2,1,0:T(8,128)(2,1)} %get-tuple-element.28), calls=%async_computation.1 | async-start | bytes 4194304 | tf_op jit(solution)/shard_map/all_to_all | solution.py:163
  61.0 16.5 %collective-permute-start = (bf16[256,1024]{1,0:T(8,128)(2,1)}, bf16[256,1024]{1,0:T(8,128)(2,1)S(1)}, u32[]{:S(2)}, u32[]{:S(2)}) collective-permute-start(bf16[256,1024]{1,0:T(8,128)(2,1)} %get-tuple-element.36), channel_id=1, source_target_pairs={{0,32},{16,48},{32,64},{48,80},{64,96},{80,112},{96,0},{112,16},{1... | collective-permute-start | bytes 1572872 | tf_op jit(solution)/shard_map/ppermute | solution.py:194
  62.9 27.0 %collective-permute-start.1 = (bf16[256,1024]{1,0:T(8,128)(2,1)}, bf16[256,1024]{1,0:T(8,128)(2,1)S(1)}, u32[]{:S(2)}, u32[]{:S(2)}) collective-permute-start(bf16[256,1024]{1,0:T(8,128)(2,1)} %get-tuple-element.37), channel_id=1, source_target_pairs={{0,64},{16,80},{32,96},{48,112},{64,0},{80,16},{96,32},{112,48},{1... | collective-permute-start | bytes 1572872 | tf_op jit(solution)/shard_map/ppermute | solution.py:194
  66.5 23.4 %collective-permute-start.2 = (bf16[256,1024]{1,0:T(8,128)(2,1)S(1)}, bf16[256,1024]{1,0:T(8,128)(2,1)S(1)}, u32[]{:S(2)}, u32[]{:S(2)}) collective-permute-start(bf16[256,1024]{1,0:T(8,128)(2,1)S(1)} %copy-done.7), channel_id=1, source_target_pairs={{0,96},{16,112},{32,0},{48,16},{64,32},{80,48},{96,64},{112,80},{1... | collective-permute-start | bytes 1572872 | tf_op jit(solution)/shard_map/ppermute | solution.py:194
  90.3 15.6 %collective-permute-start.3 = (bf16[256,1024]{1,0:T(8,128)(2,1)S(1)}, bf16[256,1024]{1,0:T(8,128)(2,1)S(1)}, u32[]{:S(2)}, u32[]{:S(2)}) collective-permute-start(bf16[256,1024]{1,0:T(8,128)(2,1)S(1)} %add_convert_fusion.1), channel_id=1, source_target_pairs={{0,16},{16,0},{32,48},{48,32},{64,80},{80,64},{96,112},{112,96},{1... | collective-permute-start | bytes 1572872 | tf_op jit(solution)/shard_map/ppermute | solution.py:205
  93.1 1.3 copy-start
  101.0 17.2 %all-to-all-start.2 = ((bf16[8,64,512]{2,1,0:T(8,128)(2,1)}), bf16[8,64,512]{2,1,0:T(8,128)(2,1)S(1)}, u32[]{:S(2)}, u32[]{:S(2)}) async-start(bf16[8,64,512]{2,1,0:T(8,128)(2,1)} %get-tuple-element.39), calls=%async_computation.2 | async-start | bytes 1048576 | tf_op jit(solution)/shard_map/all_to_all | solution.py:163
  106.0 37.8 %copy-start.1 = (bf16[256,1024]{1,0:T(8,128)(2,1)}, bf16[256,1024]{1,0:T(8,128)(2,1)S(1)}, u32[]{:S(2)}) copy-start(bf16[256,1024]{1,0:T(8,128)(2,1)S(1)} %add_convert_fusion.f0) | copy-start | bytes 1572868
  106.0 25.3 %collective-permute-start.6 = (bf16[256,1024]{1,0:T(8,128)(2,1)S(1)}, bf16[256,1024]{1,0:T(8,128)(2,1)S(1)}, u32[]{:S(2)}, u32[]{:S(2)}) collective-permute-start(bf16[256,1024]{1,0:T(8,128)(2,1)S(1)} %add_convert_fusion.f0), channel_id=1, source_target_pairs={{0,96},{16,112},{32,0},{48,16},{64,32},{80,48},{96,64},{112,80},{1... | collective-permute-start | bytes 1572872 | tf_op jit(solution)/shard_map/ppermute | solution.py:207
  109.3 22.1 %collective-permute-start.5 = (bf16[256,1024]{1,0:T(8,128)(2,1)S(1)}, bf16[256,1024]{1,0:T(8,128)(2,1)S(1)}, u32[]{:S(2)}, u32[]{:S(2)}) collective-permute-start(bf16[256,1024]{1,0:T(8,128)(2,1)S(1)} %add_convert_fusion.f0), channel_id=1, source_target_pairs={{0,64},{16,80},{32,96},{48,112},{64,0},{80,16},{96,32},{112,48},{1... | collective-permute-start | bytes 1572872 | tf_op jit(solution)/shard_map/ppermute | solution.py:207
  110.2 29.5 %collective-permute-start.4 = (bf16[256,1024]{1,0:T(8,128)(2,1)S(1)}, bf16[256,1024]{1,0:T(8,128)(2,1)S(1)}, u32[]{:S(2)}, u32[]{:S(2)}) collective-permute-start(bf16[256,1024]{1,0:T(8,128)(2,1)S(1)} %add_convert_fusion.f0), channel_id=1, source_target_pairs={{0,32},{16,48},{32,64},{48,80},{64,96},{80,112},{96,0},{112,16},{1... | collective-permute-start | bytes 1572872 | tf_op jit(solution)/shard_map/ppermute | solution.py:207
  119.1 24.7 %all-to-all-start.3 = ((bf16[8,64,512]{2,1,0:T(8,128)(2,1)}), bf16[8,64,512]{2,1,0:T(8,128)(2,1)S(1)}, u32[]{:S(2)}, u32[]{:S(2)}) async-start(bf16[8,64,512]{2,1,0:T(8,128)(2,1)} %broadcast_in_dim.2), calls=%async_computation.3 | async-start | bytes 1048576 | tf_op jit(solution)/shard_map/all_to_all | solution.py:163
  131.4 12.5 %copy-start.3 = (bf16[256,1024]{1,0:T(8,128)(2,1)}, bf16[256,1024]{1,0:T(8,128)(2,1)S(1)}, u32[]{:S(2)}) copy-start(bf16[256,1024]{1,0:T(8,128)(2,1)S(1)} %collective-permute-done.6.f3) | copy-start | bytes 1572868
  131.4 12.4 %copy-start.4 = (bf16[256,1024]{1,0:T(8,128)(2,1)}, bf16[256,1024]{1,0:T(8,128)(2,1)S(1)}, u32[]{:S(2)}) copy-start(bf16[256,1024]{1,0:T(8,128)(2,1)S(1)} %collective-permute-done.5.f2) | copy-start | bytes 1572868
  139.7 4.2 %copy-start.5 = (bf16[256,1024]{1,0:T(8,128)(2,1)}, bf16[256,1024]{1,0:T(8,128)(2,1)S(1)}, u32[]{:S(2)}) copy-start(bf16[256,1024]{1,0:T(8,128)(2,1)S(1)} %collective-permute-done.4.f1) | copy-start | bytes 1572868
  143.9 0.8 copy-start.2

commit v2 on v0

v2 whole, which is shorter than its diff:
```python
import jax
import jax.numpy as jnp
from jax import lax
from jax.experimental import pallas as pl
from jax.experimental.pallas import tpu as pltpu
from jax.sharding import PartitionSpec as P

BF = jnp.bfloat16
F32 = jnp.float32
GELU_C = 0.7978845608028654
GELU_A = 0.044715


def nn(left, right):
    return lax.dot_general(left, right, (((1,), (0,)), ((), ())), preferred_element_type=F32)


def nt(left, right):
    return lax.dot_general(left, right, (((1,), (1,)), ((), ())), preferred_element_type=F32)


def tn(left, right):
    return lax.dot_general(left, right, (((0,), (0,)), ((), ())), preferred_element_type=F32)


def slot_order(perm_ref, me):
    rows, mine = [], []
    for i in range(4):
        rows.append(perm_ref[pl.ds(i, 16, stride=4), :])
        mine.append(perm_ref[pl.ds(4 * me + i, 1), :])
    perm = jnp.concatenate(rows, axis=1)
    own = jnp.concatenate(mine, axis=1)
    from_here = lax.shift_right_logical(perm, 9) == me
    from_group = lax.shift_right_logical(own, 9) == lax.broadcasted_iota(jnp.int32, (16, 512), 0)
    return from_here, (perm & 511).astype(F32), from_group


def ranks(hits):
    before = jnp.where(
        lax.broadcasted_iota(jnp.int32, (512, 512), 0) < lax.broadcasted_iota(jnp.int32, (512, 512), 1), 1.0, 0.0
    ).astype(BF)
    return jnp.where(hits, nn(jnp.where(hits, 1.0, 0.0).astype(BF), before), -1.0)


def source_matrix(perm_ref, me, ref):
    from_here, channel, _ = slot_order(perm_ref, me)
    rank = ranks(from_here)
    slot = lax.broadcasted_iota(jnp.int32, (32, 512), 0).astype(F32)
    lane = lax.broadcasted_iota(jnp.int32, (32, 512), 1).astype(F32)
    for r in range(16):
        hit = rank[r : r + 1, :] == slot
        source = jnp.sum(jnp.where(hit, channel[r : r + 1, :], 0.0), axis=1, keepdims=True)
        ref[32 * r : 32 * r + 32, :] = jnp.where(source == lane, 1.0, 0.0).astype(BF)


def target_matrix(perm_ref, me, ref):
    _, _, from_group = slot_order(perm_ref, me)
    rank = ranks(from_group)
    slot = lax.broadcasted_iota(jnp.int32, (32, 512), 0).astype(F32)
    for s in range(16):
        ref[32 * s : 32 * s + 32, :] = jnp.where(rank[s : s + 1, :] == slot, 1.0, 0.0).astype(BF)


def fold_up(source_ref, fu_ref, ref):
    for k in range(2):
        cols = slice(256 * k, 256 * k + 256)
        ref[:, cols] = nt(source_ref[:, cols], fu_ref[k]).astype(BF)


def fold_down(target_ref, sd_ref, ref):
    for k in range(2):
        cols = slice(256 * k, 256 * k + 256)
        ref[:, cols] = nn(target_ref[:, cols], sd_ref[k]).astype(BF)


def start(pairs, sems):
    copies = [pltpu.make_async_copy(source, target, sems.at[i]) for i, (source, target) in enumerate(pairs)]
    for copy in copies:
        copy.start()
    return copies


def send(source, target, sem):
    copy = pltpu.make_async_copy(source, target, sem)
    copy.start()
    return copy


def stage_one(
    tok_hbm, cot_hbm, fu_hbm, sd_hbm, pu_hbm, pd_hbm, out_hbm, tok, cot, fu, sd, pu, pd, matrix, weight, out, sems, out_sems
):
    pairs = ((pu_hbm, pu), (fu_hbm, fu), (tok_hbm, tok), (pd_hbm, pd), (sd_hbm, sd), (cot_hbm, cot))
    copies = start(pairs, sems)
    me = lax.axis_index("chan")
    copies[0].wait()
    source_matrix(pu, me, matrix.at[0])
    copies[1].wait()
    fold_up(matrix.at[0], fu, weight.at[0])
    copies[3].wait()
    target_matrix(pd, me, matrix.at[1])
    copies[4].wait()
    fold_down(matrix.at[1], sd, weight.at[1])
    sent = []
    for i, (wait, rows) in enumerate(((copies[2], tok), (copies[5], cot))):
        wait.wait()
        for j in range(2):
            groups = slice(8 * j, 8 * j + 8)
            part = nt(weight[i, 256 * j : 256 * j + 256, :], rows[...]).astype(BF)
            out[groups, 32 * i : 32 * i + 32, :] = part.reshape(8, 32, 1024)
            at = (groups, slice(32 * i, 32 * i + 32))
            sent.append(send(out.at[at], out_hbm.at[at], out_sems.at[2 * i + j]))
    for copy in sent:
        copy.wait()


def prepare(fu_ref, sd_ref, pu_ref, pd_ref, mark, up_src, up_tgt, down_src, down_tgt, w_up, w_down):
    me = lax.axis_index("chan")
    source_matrix(pu_ref, me, up_src)
    target_matrix(pu_ref, me, up_tgt)
    source_matrix(pd_ref, me, down_src)
    target_matrix(pd_ref, me, down_tgt)
    fold_up(up_src, fu_ref, w_up)
    fold_down(down_tgt, sd_ref, w_down)


def stage_two(
    tgt_hbm, src_hbm, su_hbm, fd_hbm, r_ref, out_hbm, f0, f1, f2, f3, s0, s1, s2, s3,
    up_tgt, down_src, su, fd, act, hg, nar, mix, pfd, psu, out, sems, out_sems,
):
    copies = start(((tgt_hbm, up_tgt), (src_hbm, down_src), (su_hbm, su), (fd_hbm, fd)), sems)
    copies[0].wait()
    mixed_in = tn(up_tgt[...], r_ref[:, 0:32, :].reshape(512, 1024)).astype(BF)
    copies[1].wait()
    nar_grad = tn(down_src[...], r_ref[:, 32:64, :].reshape(512, 1024)).astype(BF)
    copies[2].wait()
    copies[3].wait()
    z = lax.shift_right_logical(lax.axis_index("dp"), 1)
    sent = []
    for k in range(2):
        mi = mixed_in[256 * k : 256 * k + 256, :]
        ng = nar_grad[256 * k : 256 * k + 256, :]
        for c in range(2):
            units = slice(512 * c, 512 * c + 512)
            v = tn(su[k, :, units], mi)
            up = nn(fd[k, units, :], ng)
            sq = v * v
            h = 0.5 + 0.5 * jnp.tanh(v * (GELU_C + (GELU_C * GELU_A) * sq))
            a = (v * h).astype(BF)
            d = v * ((2 * GELU_C) + (6 * GELU_C * GELU_A) * sq)
            b = (up * (h * (1.0 + (1.0 - h) * d))).astype(BF)
            act[k, units, :] = a
            hg[k, units, :] = b
            gsu = nt(mi, b).astype(BF)
            gfd = nt(a, ng).astype(BF)
            for i in range(2):
                psu[2 * k + i, :, units] = gsu[128 * i : 128 * i + 128, :]
            for i in range(4):
                pfd[2 * k + c, :, 256 * i : 256 * i + 256] = gfd[128 * i : 128 * i + 128, :]
        if k == 1:
            for i, (f, s) in enumerate(((f0, s0), (f1, s1), (f2, s2), (f3, s3))):
                sent.append(send(pfd.at[(z + i) & 3], f, out_sems.at[i]))
                sent.append(send(psu.at[(z + i) & 3], s, out_sems.at[4 + i]))
        nar[256 * k : 256 * k + 256, :] = tn(fd[k], act[k]).astype(BF)
        mix[256 * k : 256 * k + 256, :] = nn(su[k], hg[k]).astype(BF)
    for i, (matrix, rows) in enumerate(((down_src, nar), (up_tgt, mix))):
        for j in range(2):
            groups = slice(8 * j, 8 * j + 8)
            part = nn(matrix[256 * j : 256 * j + 256, :], rows[...]).astype(BF)
            out[groups, 32 * i : 32 * i + 32, :] = part.reshape(8, 32, 1024)
            at = (groups, slice(32 * i, 32 * i + 32))
            sent.append(send(out.at[at], out_hbm.at[at], out_sems.at[8 + 2 * i + j]))
    for copy in sent:
        copy.wait()


def square_grads(
    tok_hbm, cot_hbm, src_hbm, tgt_hbm, r_ref, after, t_hbm, tok, cot, up_src, down_tgt, t, sems, out_sems
):
    top, low = slice(0, 512), slice(512, 1024)
    pairs = (
        (cot_hbm.at[top], cot.at[top]),
        (cot_hbm.at[low], cot.at[low]),
        (tgt_hbm, down_tgt),
        (tok_hbm.at[top], tok.at[top]),
        (tok_hbm.at[low], tok.at[low]),
        (src_hbm, up_src),
    )
    copies = start(pairs, sems)
    sent = []
    for n, rows in enumerate((cot, tok)):
        slots = r_ref[:, 32 * n : 32 * n + 32, :].reshape(512, 1024)
        copies[3 * n].wait()
        sums = nn(slots[:, top], rows[top, :])
        copies[3 * n + 1].wait()
        sums = (sums + nn(slots[:, low], rows[low, :])).astype(BF)
        copies[3 * n + 2].wait()
        for k in range(2):
            cols = slice(256 * k, 256 * k + 256)
            grad = tn(down_tgt[:, cols], sums[:, cols]) if n == 0 else tn(sums[:, cols], up_src[:, cols])
            grad = grad.astype(BF)
            for i in range(4):
                t[4 * k + i, :, 256 * n : 256 * n + 256] = grad[64 * i : 64 * i + 64, :]
        at = (slice(0, 8), slice(0, 64), slice(256 * n, 256 * n + 256))
        sent.append(send(t.at[at], t_hbm.at[at], out_sems.at[n]))
    for copy in sent:
        copy.wait()


def outputs(up_hbm, down_hbm, r_ref, after, mixed_ref, ig_ref, w_up, w_down, sems):
    copies = start(((down_hbm, w_down), (up_hbm, w_up)), sems)
    copies[0].wait()
    mixed_ref[...] = tn(r_ref[:, 0:32, :].reshape(512, 1024), w_down[...]).astype(BF)
    copies[1].wait()
    ig_ref[...] = tn(r_ref[:, 32:64, :].reshape(512, 1024), w_up[...]).astype(BF)


def total(t_ref, after, out_ref):
    sums = t_ref[0].astype(F32)
    for i in range(1, 8):
        sums = sums + t_ref[i].astype(F32)
    sums = sums.astype(BF)
    for i in range(8):
        out_ref[i] = sums


def finish_down(f0, f1, f2, f3, out_ref):
    z = lax.shift_right_logical(lax.axis_index("dp"), 1)
    for i, f in enumerate((f0, f1, f2, f3)):
        c = (z - i) & 3
        for b in range(4):
            out_ref[c >> 1, pl.ds((c & 1) * 512 + 128 * b, 128), :] = f[:, 256 * b : 256 * b + 256].astype(F32)


def finish_up(f0, f1, f2, f3, out_ref):
    z = lax.shift_right_logical(lax.axis_index("dp"), 1)
    for i, f in enumerate((f0, f1, f2, f3)):
        c = (z - i) & 3
        out_ref[c >> 1, pl.ds((c & 1) * 128, 128), :] = f[...].astype(F32)


def finish_square(t_ref, gfu_ref, gsd_ref):
    for k in range(2):
        for i in range(4):
            rows = slice(64 * i, 64 * i + 64)
            gsd_ref[k, rows, :] = t_ref[4 * k + i, :, 0:256].astype(F32)
            gfu_ref[k, rows, :] = t_ref[4 * k + i, :, 256:512].astype(F32)


def like(*shape, dtype=BF):
    return jax.ShapeDtypeStruct(shape, dtype)


def far(*shape):
    return pltpu.HBM(shape, BF)


def near(*shape):
    return pltpu.VMEM(shape, BF)


def placed(space, count):
    return [pl.BlockSpec(memory_space=space)] * count


def run(kernel, args, out_shape, mega, hbm=0, after=(), out_space=pltpu.VMEM, scratch=(), sems=(), flops=0, moved=0):
    args = tuple(pltpu.with_memory_space_constraint(x, pltpu.HBM) if i < hbm else x for i, x in enumerate(args))
    return pl.pallas_call(
        kernel,
        out_shape=out_shape,
        in_specs=placed(pltpu.HBM, hbm) + placed(pltpu.VMEM, len(args) - hbm) + placed(pl.ANY, len(after)),
        out_specs=placed(out_space, len(out_shape)),
        scratch_shapes=list(scratch) + [pltpu.SemaphoreType.DMA((n,)) for n in sems],
        compiler_params=pltpu.CompilerParams(vmem_limit_bytes=mega * 2**20),
        cost_estimate=pl.CostEstimate(flops=flops, bytes_accessed=moved, transcendentals=0),
        name=kernel.__name__,
    )(*args, *after)


def shift_z(step):
    return [(2 * z + x, 2 * ((z + step) % 4) + x) for z in range(4) for x in range(2)]


SWAP_X = [(2 * z + x, 2 * z + 1 - x) for z in range(4) for x in range(2)]


def exchange(values, axis):
    return lax.all_to_all(values, axis, split_axis=0, concat_axis=0, tiled=True)


def z_sum(parts):
    got = [lax.ppermute(part, "dp", shift_z(i)) for i, part in enumerate(parts) if i]
    sums = parts[0].astype(F32)
    for part in got:
        sums = sums + part.astype(F32)
    return sums.astype(BF)


def x_sum(part):
    return (part.astype(F32) + lax.ppermute(part, "dp", SWAP_X).astype(F32)).astype(BF)


def z_gather(part):
    return [part] + [lax.ppermute(part, "dp", shift_z(i)) for i in (1, 2, 3)]


def per_device(tokens, first_up, second_up, first_down, second_down, perm_up, perm_down, cotangent):
    perms = (perm_up.reshape(64, 128), perm_down.reshape(64, 128))
    square = near(512, 512)
    (sent,) = run(
        stage_one,
        (tokens, cotangent, first_up, second_down) + perms,
        (far(16, 64, 1024),),
        20,
        hbm=6,
        out_space=pltpu.HBM,
        scratch=[near(1024, 512)] * 2
        + [near(2, 256, 256)] * 2
        + [pltpu.VMEM((64, 128), jnp.int32)] * 2
        + [near(2, 512, 512)] * 2
        + [near(16, 64, 1024)],
        sems=(6, 4),
        flops=2 * 10**9,
        moved=5 * 10**6,
    )
    got = exchange(sent, "chan")
    up_src, up_tgt, down_src, down_tgt, w_up, w_down = run(
        prepare,
        (first_up, second_down) + perms,
        (far(512, 512),) * 6,
        20,
        after=(sent,),
        flops=2 * 10**9,
        moved=4 * 10**6,
    )
    sent, *grads = run(
        stage_two,
        (up_tgt, down_src, second_up, first_down, got),
        (far(16, 64, 1024),) + (far(128, 1024),) * 8,
        32,
        hbm=4,
        out_space=pltpu.HBM,
        scratch=[square, square, near(2, 256, 1024), near(2, 1024, 256)]
        + [near(2, 1024, 1024)] * 2
        + [near(512, 1024)] * 2
        + [near(4, 128, 1024)] * 2
        + [near(16, 64, 1024)],
        sems=(4, 12),
        flops=85 * 10**8,
        moved=9 * 10**6,
    )
    got = exchange(sent, "chan")
    down_part = z_sum(grads[:4])
    up_part = z_sum(grads[4:])
    (tail,) = run(
        square_grads,
        (tokens, cotangent, up_src, down_tgt, got),
        (far(8, 64, 512),),
        20,
        hbm=4,
        after=(up_part,),
        out_space=pltpu.HBM,
        scratch=[near(1024, 512)] * 2 + [square, square, near(8, 64, 512)],
        sems=(6, 2),
        flops=16 * 10**8,
        moved=5 * 10**6,
    )
    down_all = z_gather(x_sum(down_part))
    up_all = z_gather(x_sum(up_part))
    tail_parts = exchange(tail, "dp")
    mixed, input_grad = run(
        outputs,
        (w_up, w_down, got),
        (like(1024, 512),) * 2,
        20,
        hbm=2,
        after=(tail,),
        scratch=[square, square],
        sems=(2,),
        flops=10**9,
        moved=5 * 10**6,
    )
    (tail_sums,) = run(
        total, (tail_parts,), (far(8, 64, 512),), 20, after=(mixed,), flops=10**6, moved=10**6
    )
    tail_all = exchange(tail_sums, "dp")
    (grad_fd,) = run(finish_down, down_all, (like(2, 1024, 256, dtype=F32),), 20, flops=10**6, moved=3 * 10**6)
    (grad_su,) = run(finish_up, up_all, (like(2, 256, 1024, dtype=F32),), 20, flops=10**6, moved=3 * 10**6)
    grad_fu, grad_sd = run(
        finish_square, (tail_all,), (like(2, 256, 256, dtype=F32),) * 2, 20, flops=10**6, moved=2 * 10**6
    )
    return (mixed, input_grad, grad_fu, grad_su, grad_fd, grad_sd)


def solution(mesh):
    layout = (
        P("dp", "chan"),
        P("chan", None, None),
        P("chan", None, None),
        P("chan", None, None),
        P("chan", None, None),
        P(),
        P(),
        P("dp", "chan"),
    )
    return jax.shard_map(
        per_device,
        mesh=mesh,
        in_specs=layout,
        out_specs=(
            P("dp", "chan"),
            P("dp", "chan"),
            P("chan", None, None),
            P("chan", None, None),
            P("chan", None, None),
            P("chan", None, None),
        ),
        check_vma=False,
    )
```

time: 533 us -> 144 us (0.27)
  waiting for transfers between devices: 254 us -> 54.4 us
  local copies, waits for them, and re-layouts: 170 us -> 3.93 us
  matrix products: 34.2 us -> 0 us
  Pallas kernels: 0 us -> 33.6 us
  between operations: 14.3 us -> 0.83 us
  other arithmetic: 13.6 us -> 2.37 us
    psum x1 -> x0, waiting for transfers between devices: 223 us -> none  [per_device(): lax.psum((grad_fu, grad_su, grad_fd, grad_sd), 'dp')]
    gather x4 -> x0, local copies, waits for them, and re-layouts: 118 us -> none  [route(): shifted = whole_rows[:, column_table]]
    dot_general x12 -> x0, matrix products: 34.2 us -> none  [the longest x4 13 us: block_grad(): jnp.einsum('rki,rko->kio', left, right, preferred_element_type=jnp.float32)]
    pallas_call x0 -> x9, Pallas kernels: none -> 33.6 us  [run(): pl.pallas_call(kernel, out_shape=out_shape, in_specs=placed(pltpu.HBM, hb...]
    ppermute x0 -> x14, waiting for transfers between devices: none -> 28.6 us  [the longest x6 16 us: z_sum(): lax.ppermute(part, 'dp', shift_z(i))]
    ppermute x0 -> x14, starting transfers between devices: none -> 25.8 us  [the longest x6 9.95 us: z_sum(): lax.ppermute(part, 'dp', shift_z(i))]
    all_to_all x8 -> x4, starting transfers between devices: 45.1 us -> 21.9 us  [exchange(): return lax.all_to_all(values, axis, split_axis=0, concat_axis=0, tiled=True)]
    all_to_all x8 -> x0, local copies, waits for them, and re-layouts: 18 us -> none  [the longest x4 10.8 us: route(): lax.all_to_all(shifted, 'chan', split_axis=1, concat_axis=0, tiled=True)]
  transfers between devices with their start and end apart: 9 -> 18, of which waited for: 5 -> 9; matrix products, arithmetic and copies ran while one was open for 35% -> 2% of each run, Pallas kernels for 0% -> 10%
where the time goes in v2:
time: 144 us; the launch traced here: 143 us
  waiting for transfers between devices  54.4 us (38%)
  starting transfers between devices  47.7 us (33%)
  Pallas kernels  33.6 us (23%)
  local copies, waits for them, and re-layouts  3.93 us (3%)
  other arithmetic  2.37 us (2%)
    pallas_call x9, Pallas kernels, run(): pl.pallas_call(kernel, out_shape=out_shape, in_specs=placed(pltpu.HBM, hb...  33.6 us
    all_to_all x4, waiting for transfers between devices, exchange(): return lax.all_to_all(values, axis, split_axis=0, concat_axis=0, tiled=True)  25.8 us
    all_to_all x4, starting transfers between devices, exchange(): return lax.all_to_all(values, axis, split_axis=0, concat_axis=0, tiled=True)  21.9 us
    ppermute x6, waiting for transfers between devices, z_sum(): lax.ppermute(part, 'dp', shift_z(i))  16 us
    ppermute x6, waiting for transfers between devices, z_gather(): return [part] + [lax.ppermute(part, 'dp', shift_z(i)) for i in (1, 2, 3)]  12.6 us
    ppermute x6, starting transfers between devices, z_sum(): lax.ppermute(part, 'dp', shift_z(i))  9.95 us
    ppermute x6, starting transfers between devices, z_gather(): return [part] + [lax.ppermute(part, 'dp', shift_z(i)) for i in (1, 2, 3)]  9.47 us
    ppermute x2, starting transfers between devices, x_sum(): lax.ppermute(part, 'dp', SWAP_X).astype(F32)  6.33 us
  transfers between devices with their start and end apart: 18, of which 9 were waited for; matrix products, arithmetic and copies ran while one was open for 2% of the time, Pallas kernels for 10%

profile of v2, /device:TPU:24, one launch (start us, length us, event | category | flops | bytes accessed | tf_op | source)
XLA Modules:
  0.0 142.8 jit_solution(9775434443403796450)
XLA Ops:
  0.6 4.3 %stage_one.1.mark = bf16[16,64,1024]{2,1,0:T(8,128)(2,1)} custom-call(bf16[1024,512]{1,0:T(8,128)(2,1)} %tok_hbm.3, bf16[1024,512]{1,0:T(8,128)(2,1)} %cot_hbm.3, bf16[2,256,256]{2,1,0:T(8,128)(2,1)} %fu_ref.1, bf16[2,256,256]{2,1,0:T(8,128)(2,1)} %sd_ref.1, s32[64,128]{1,0:T(8,128)} %bitcast.2, s32[64,128]{1,0:T(8,128)} %bitcast.4), custom_call_target="tpu_custom_call" | custom-call | flops 2000000000 | bytes 5000000 | tf_op jit(solution)/shard_map/stage_one/pallas_call | solution.py:267
  5.0 5.8 %all-to-all-start = ((bf16[16,64,1024]{2,1,0:T(8,128)(2,1)}), bf16[16,64,1024]{2,1,0:T(8,128)(2,1)S(1)}, u32[]{:S(2)}, u32[]{:S(2)}) async-start(bf16[16,64,1024]{2,1,0:T(8,128)(2,1)} %stage_one.1.mark), calls=%async_computation | async-start | bytes 4194304 | tf_op jit(solution)/shard_map/all_to_all | solution.py:287
  10.8 1.6 %copy-done.1 = bf16[16,64,1024]{2,1,0:T(8,128)(2,1)S(1)} copy-done((bf16[16,64,1024]{2,1,0:T(8,128)(2,1)S(1)}, bf16[16,64,1024]{2,1,0:T(8,128)(2,1)}, u32[]{:S(2)}) %copy-start.1) | copy-done | bytes 2097176
  12.5 2.2 %prepare.1 = (bf16[512,512]{1,0:T(8,128)(2,1)}, bf16[512,512]{1,0:T(8,128)(2,1)}, bf16[512,512]{1,0:T(8,128)(2,1)}, bf16[512,512]{1,0:T(8,128)(2,1)}, bf16[512,5...) custom-call(bf16[2,256,256]{2,1,0:T(8,128)(2,1)S(1)} %copy-done.3, bf16[2,256,256]{2,1,0:T(8,128)(2,1)S(1)} %copy-done.4, ...), custom_call_target="tpu_custom_call" | custom-call | flops 2000000000 | bytes 4000000 | tf_op jit(solution)/shard_map/prepare/pallas_call | solution.py:267
  14.6 25.5 %all-to-all-done.r_ref = bf16[16,64,1024]{2,1,0:T(8,128)(2,1)S(1)} async-done(((bf16[16,64,1024]{2,1,0:T(8,128)(2,1)}), bf16[16,64,1024]{2,1,0:T(8,128)(2,1)S(1)}, u32[]{:S(2)}, u32[]{:S(2)}) %all-to-all-start) | async-done | bytes 2097184 | tf_op jit(solution)/shard_map/all_to_all | solution.py:287
  40.2 13.5 %stage_two.1 = (bf16[16,64,1024]{2,1,0:T(8,128)(2,1)}, bf16[128,1024]{1,0:T(8,128)(2,1)}, bf16[128,1024]{1,0:T(8,128)(2,1)}, bf16[128,1024]{1,0:T(8,128)(2,1)}, ...) custom-call(bf16[512,512]{1,0:T(8,128)(2,1)} %get-tuple-element.27.t, ...), custom_call_target="tpu_custom_call" | custom-call | flops 8499999744 | bytes 9000000 | tf_op jit(solution)/shard_map/stage_two/pallas_call | solution.py:267
  53.7 5.0 %all-to-all-start.1 = ((bf16[16,64,1024]{2,1,0:T(8,128)(2,1)}), bf16[16,64,1024]{2,1,0:T(8,128)(2,1)S(1)}, u32[]{:S(2)}, u32[]{:S(2)}) async-start(bf16[16,64,1024]{2,1,0:T(8,128)(2,1)} %get-tuple-element.29), calls=%async_computation.1 | async-start | bytes 4194304 | tf_op jit(solution)/shard_map/all_to_all | solution.py:287
  58.8 1.9 %collective-permute-start.7 = (bf16[128,1024]{1,0:T(8,128)(2,1)}, bf16[128,1024]{1,0:T(8,128)(2,1)S(1)}, u32[]{:S(2)}, u32[]{:S(2)}) collective-permute-start(bf16[128,1024]{1,0:T(8,128)(2,1)} %get-tuple-element.40), channel_id=1, source_target_pairs={{0,32},{16,48},{32,64},{48,80},{64,96},{80,112},{96,0},{112,16},{1... | collective-permute-start | bytes 786440 | tf_op jit(solution)/shard_map/ppermute | solution.py:291
  60.7 3.6 %collective-permute-start.8 = (bf16[128,1024]{1,0:T(8,128)(2,1)}, bf16[128,1024]{1,0:T(8,128)(2,1)S(1)}, u32[]{:S(2)}, u32[]{:S(2)}) collective-permute-start(bf16[128,1024]{1,0:T(8,128)(2,1)} %get-tuple-element.41), channel_id=1, source_target_pairs={{0,64},{16,80},{32,96},{48,112},{64,0},{80,16},{96,32},{112,48},{1... | collective-permute-start | bytes 786440 | tf_op jit(solution)/shard_map/ppermute | solution.py:291
  66.7 3.4 %collective-permute-done.7 = bf16[128,1024]{1,0:T(8,128)(2,1)S(1)} collective-permute-done((bf16[128,1024]{1,0:T(8,128)(2,1)}, bf16[128,1024]{1,0:T(8,128)(2,1)S(1)}, u32[]{:S(2)}, u32[]{:S(2)}) %collective-permute-start.7) | collective-permute-done | bytes 262176 | tf_op jit(solution)/shard_map/ppermute | solution.py:291
  70.2 2.0 %collective-permute-start.2 = (bf16[128,1024]{1,0:T(8,128)(2,1)S(1)}, bf16[128,1024]{1,0:T(8,128)(2,1)S(1)}, u32[]{:S(2)}, u32[]{:S(2)}) collective-permute-start(bf16[128,1024]{1,0:T(8,128)(2,1)S(1)} %copy-done.9), channel_id=1, source_target_pairs={{0,96},{16,112},{32,0},{48,16},{64,32},{80,48},{96,64},{112,80},{1... | collective-permute-start | bytes 786440 | tf_op jit(solution)/shard_map/ppermute | solution.py:291
  72.2 5.1 %collective-permute-done.8 = bf16[128,1024]{1,0:T(8,128)(2,1)S(1)} collective-permute-done((bf16[128,1024]{1,0:T(8,128)(2,1)}, bf16[128,1024]{1,0:T(8,128)(2,1)S(1)}, u32[]{:S(2)}, u32[]{:S(2)}) %collective-permute-start.8) | collective-permute-done | bytes 262176 | tf_op jit(solution)/shard_map/ppermute | solution.py:291
  77.5 2.8 %collective-permute-start.10 = (bf16[128,1024]{1,0:T(8,128)(2,1)S(1)}, bf16[128,1024]{1,0:T(8,128)(2,1)}, u32[]{:S(2)}, u32[]{:S(2)}) collective-permute-start(bf16[128,1024]{1,0:T(8,128)(2,1)S(1)} %add_convert_fusion.1), channel_id=1, source_target_pairs={{0,16},{16,0},{32,48},{48,32},{64,80},{80,64},{96,112},{112,96},{1... | collective-permute-start | bytes 786440 | tf_op jit(solution)/shard_map/ppermute | solution.py:299
  80.9 6.8 %collective-permute-done.1 = bf16[128,1024]{1,0:T(8,128)(2,1)S(1)} collective-permute-done((bf16[128,1024]{1,0:T(8,128)(2,1)S(1)}, bf16[128,1024]{1,0:T(8,128)(2,1)S(1)}, u32[]{:S(2)}, u32[]{:S(2)}) %collective-permute-start.1) | collective-permute-done | bytes 262176 | tf_op jit(solution)/shard_map/ppermute | solution.py:291
  88.1 4.2 %square_grads.1.after = bf16[8,64,512]{2,1,0:T(8,128)(2,1)} custom-call(bf16[1024,512]{1,0:T(8,128)(2,1)} %tok_hbm.3, bf16[1024,512]{1,0:T(8,128)(2,1)} %cot_hbm.3, bf16[512,512]{1,0:T(8,128)(2,1)} %get-tuple-element.30.src_hbm, bf16[512,512]{1,0:T(8,128)(2,1)} %get-tuple-element.31.tgt_hbm, bf16[16,64,1024]{2,1,0:T(8,128)(2,1)S(1)} %all-to-all-done.1.r_ref, ...), custom_call_target="tpu_custom_call" | custom-call | flops 1600000000 | bytes 5000000 | tf_op jit(solution)/shard_map/square_grads/pallas_call | solution.py:267
  92.4 7.5 %all-to-all-start.2 = ((bf16[8,64,512]{2,1,0:T(8,128)(2,1)}), bf16[8,64,512]{2,1,0:T(8,128)(2,1)S(1)}, u32[]{:S(2)}, u32[]{:S(2)}) async-start(bf16[8,64,512]{2,1,0:T(8,128)(2,1)} %square_grads.1.after), calls=%async_computation.2 | async-start | bytes 1048576 | tf_op jit(solution)/shard_map/all_to_all | solution.py:287
  99.8 3.5 %collective-permute-start.3 = (bf16[128,1024]{1,0:T(8,128)(2,1)S(1)}, bf16[128,1024]{1,0:T(8,128)(2,1)}, u32[]{:S(2)}, u32[]{:S(2)}) collective-permute-start(bf16[128,1024]{1,0:T(8,128)(2,1)S(1)} %add_convert_fusion.3.after), channel_id=1, source_target_pairs={{0,16},{16,0},{32,48},{48,32},{64,80},{80,64},{96,112},{112,96},{1... | collective-permute-start | bytes 786440 | tf_op jit(solution)/shard_map/ppermute | solution.py:299
  104.4 2.7 %collective-permute-start.13 = (bf16[128,1024]{1,0:T(8,128)(2,1)S(1)}, bf16[128,1024]{1,0:T(8,128)(2,1)S(1)}, u32[]{:S(2)}, u32[]{:S(2)}) collective-permute-start(bf16[128,1024]{1,0:T(8,128)(2,1)S(1)} %add_convert_fusion.f0), channel_id=1, source_target_pairs={{0,96},{16,112},{32,0},{48,16},{64,32},{80,48},{96,64},{112,80},{1... | collective-permute-start | bytes 786440 | tf_op jit(solution)/shard_map/ppermute | solution.py:303
  109.9 3.5 %outputs.1 = (bf16[1024,512]{1,0:T(8,128)(2,1)}, bf16[1024,512]{1,0:T(8,128)(2,1)}) custom-call(bf16[512,512]{1,0:T(8,128)(2,1)} %get-tuple-element.25.up_hbm, bf16[512,512]{1,0:T(8,128)(2,1)} %get-tuple-element.26.down_hbm, bf16[16,64,1024]{2,1,0:T(8,128)(2,1)S(1)} %all-to-all-done.1.r_ref, bf16[8,64,512]{2,1,0:T(8,128)(2,1)S(1)} %copy-done), custom_call_target="tpu_custom_call" | custom-call | flops 1000000000 | bytes 5000000 | tf_op jit(solution)/shard_map/outputs/pallas_call | solution.py:267
  115.5 3.7 %all-to-all-start.3 = ((bf16[8,64,512]{2,1,0:T(8,128)(2,1)}), bf16[8,64,512]{2,1,0:T(8,128)(2,1)S(1)}, u32[]{:S(2)}, u32[]{:S(2)}) async-start(bf16[8,64,512]{2,1,0:T(8,128)(2,1)} %total.1), calls=%async_computation.3 | async-start | bytes 1048576 | tf_op jit(solution)/shard_map/all_to_all | solution.py:287
  120.2 3.3 %collective-permute-start.6 = (bf16[128,1024]{1,0:T(8,128)(2,1)S(1)}, bf16[128,1024]{1,0:T(8,128)(2,1)S(1)}, u32[]{:S(2)}, u32[]{:S(2)}) collective-permute-start(bf16[128,1024]{1,0:T(8,128)(2,1)S(1)} %add_convert_fusion.2.f0), channel_id=1, source_target_pairs={{0,96},{16,112},{32,0},{48,16},{64,32},{80,48},{96,64},{112,80},{1... | collective-permute-start | bytes 786440 | tf_op jit(solution)/shard_map/ppermute | solution.py:303
  125.2 2.5 %finish_down.1 = f32[2,1024,256]{2,1,0:T(8,128)} custom-call(bf16[128,1024]{1,0:T(8,128)(2,1)S(1)} %add_convert_fusion.f0, bf16[128,1024]{1,0:T(8,128)(2,1)} %collective-permute-done.11.f1, bf16[128,1024]{1,0:T(8,128)(2,1)} %collective-permute-done.12.f2, bf16[128,1024]{1,0:T(8,128)(2,1)S(1)} %collective-permute-done.13.f3), custom_call_target="tpu_custom_call" | custom-call | flops 1000000 | bytes 3000000 | tf_op jit(solution)/shard_map/finish_down/pallas_call | solution.py:267
  127.7 6.5 %collective-permute-done.6.f3 = bf16[128,1024]{1,0:T(8,128)(2,1)S(1)} collective-permute-done((bf16[128,1024]{1,0:T(8,128)(2,1)S(1)}, bf16[128,1024]{1,0:T(8,128)(2,1)S(1)}, u32[]{:S(2)}, u32[]{:S(2)}) %collective-permute-start.6) | collective-permute-done | bytes 262176 | tf_op jit(solution)/shard_map/ppermute | solution.py:303
  135.4 4.9 %collective-permute-done.4.f1 = bf16[128,1024]{1,0:T(8,128)(2,1)S(1)} collective-permute-done((bf16[128,1024]{1,0:T(8,128)(2,1)S(1)}, bf16[128,1024]{1,0:T(8,128)(2,1)S(1)}, u32[]{:S(2)}, u32[]{:S(2)}) %collective-permute-start.4) | collective-permute-done | bytes 262176 | tf_op jit(solution)/shard_map/ppermute | solution.py:303
  (49 shorter events, 16.0 us)
Async XLA Ops:
  5.0 5.8 %copy-start.3 = (bf16[2,256,256]{2,1,0:T(8,128)(2,1)S(1)}, bf16[2,256,256]{2,1,0:T(8,128)(2,1)}, u32[]{:S(2)}) copy-start(bf16[2,256,256]{2,1,0:T(8,128)(2,1)} %fu_ref.1) | copy-start | bytes 786436
  5.0 35.2 %all-to-all-start = ((bf16[16,64,1024]{2,1,0:T(8,128)(2,1)}), bf16[16,64,1024]{2,1,0:T(8,128)(2,1)S(1)}, u32[]{:S(2)}, u32[]{:S(2)}) async-start(bf16[16,64,1024]{2,1,0:T(8,128)(2,1)} %stage_one.1.mark), calls=%async_computation | async-start | bytes 4194304 | tf_op jit(solution)/shard_map/all_to_all | solution.py:287
  53.7 10.6 %copy-start.11 = (bf16[128,1024]{1,0:T(8,128)(2,1)S(1)}, bf16[128,1024]{1,0:T(8,128)(2,1)}, u32[]{:S(2)}) copy-start(bf16[128,1024]{1,0:T(8,128)(2,1)} %get-tuple-element.42) | copy-start | bytes 786436
  53.7 12.6 %copy-start.10 = (bf16[128,1024]{1,0:T(8,128)(2,1)S(1)}, bf16[128,1024]{1,0:T(8,128)(2,1)}, u32[]{:S(2)}) copy-start(bf16[128,1024]{1,0:T(8,128)(2,1)} %get-tuple-element.34) | copy-start | bytes 786436
  53.7 16.5 %copy-start.9 = (bf16[128,1024]{1,0:T(8,128)(2,1)S(1)}, bf16[128,1024]{1,0:T(8,128)(2,1)}, u32[]{:S(2)}) copy-start(bf16[128,1024]{1,0:T(8,128)(2,1)} %get-tuple-element.35) | copy-start | bytes 786436
  53.7 23.6 %copy-start.8 = (bf16[128,1024]{1,0:T(8,128)(2,1)S(1)}, bf16[128,1024]{1,0:T(8,128)(2,1)}, u32[]{:S(2)}) copy-start(bf16[128,1024]{1,0:T(8,128)(2,1)} %get-tuple-element.39) | copy-start | bytes 786436
  53.7 34.0 %copy-start.7 = (bf16[128,1024]{1,0:T(8,128)(2,1)S(1)}, bf16[128,1024]{1,0:T(8,128)(2,1)}, u32[]{:S(2)}) copy-start(bf16[128,1024]{1,0:T(8,128)(2,1)} %get-tuple-element.32) | copy-start | bytes 786436
  53.7 34.4 %all-to-all-start.1 = ((bf16[16,64,1024]{2,1,0:T(8,128)(2,1)}), bf16[16,64,1024]{2,1,0:T(8,128)(2,1)S(1)}, u32[]{:S(2)}, u32[]{:S(2)}) async-start(bf16[16,64,1024]{2,1,0:T(8,128)(2,1)} %get-tuple-element.29), calls=%async_computation.1 | async-start | bytes 4194304 | tf_op jit(solution)/shard_map/all_to_all | solution.py:287
  58.8 11.4 %collective-permute-start.7 = (bf16[128,1024]{1,0:T(8,128)(2,1)}, bf16[128,1024]{1,0:T(8,128)(2,1)S(1)}, u32[]{:S(2)}, u32[]{:S(2)}) collective-permute-start(bf16[128,1024]{1,0:T(8,128)(2,1)} %get-tuple-element.40), channel_id=1, source_target_pairs={{0,32},{16,48},{32,64},{48,80},{64,96},{80,112},{96,0},{112,16},{1... | collective-permute-start | bytes 786440 | tf_op jit(solution)/shard_map/ppermute | solution.py:291
  60.7 16.6 %collective-permute-start.8 = (bf16[128,1024]{1,0:T(8,128)(2,1)}, bf16[128,1024]{1,0:T(8,128)(2,1)S(1)}, u32[]{:S(2)}, u32[]{:S(2)}) collective-permute-start(bf16[128,1024]{1,0:T(8,128)(2,1)} %get-tuple-element.41), channel_id=1, source_target_pairs={{0,64},{16,80},{32,96},{48,112},{64,0},{80,16},{96,32},{112,48},{1... | collective-permute-start | bytes 786440 | tf_op jit(solution)/shard_map/ppermute | solution.py:291
  64.3 13.0 %collective-permute-start.9 = (bf16[128,1024]{1,0:T(8,128)(2,1)S(1)}, bf16[128,1024]{1,0:T(8,128)(2,1)S(1)}, u32[]{:S(2)}, u32[]{:S(2)}) collective-permute-start(bf16[128,1024]{1,0:T(8,128)(2,1)S(1)} %copy-done.11), channel_id=1, source_target_pairs={{0,96},{16,112},{32,0},{48,16},{64,32},{80,48},{96,64},{112,80},{1... | collective-permute-start | bytes 786440 | tf_op jit(solution)/shard_map/ppermute | solution.py:291
  65.3 15.6 %collective-permute-start = (bf16[128,1024]{1,0:T(8,128)(2,1)}, bf16[128,1024]{1,0:T(8,128)(2,1)S(1)}, u32[]{:S(2)}, u32[]{:S(2)}) collective-permute-start(bf16[128,1024]{1,0:T(8,128)(2,1)} %get-tuple-element.33), channel_id=1, source_target_pairs={{0,32},{16,48},{32,64},{48,80},{64,96},{80,112},{96,0},{112,16},{1... | collective-permute-start | bytes 786440 | tf_op jit(solution)/shard_map/ppermute | solution.py:291
  66.3 21.4 %collective-permute-start.1 = (bf16[128,1024]{1,0:T(8,128)(2,1)S(1)}, bf16[128,1024]{1,0:T(8,128)(2,1)S(1)}, u32[]{:S(2)}, u32[]{:S(2)}) collective-permute-start(bf16[128,1024]{1,0:T(8,128)(2,1)S(1)} %copy-done.10), channel_id=1, source_target_pairs={{0,64},{16,80},{32,96},{48,112},{64,0},{80,16},{96,32},{112,48},{1... | collective-permute-start | bytes 786440 | tf_op jit(solution)/shard_map/ppermute | solution.py:291
  70.2 17.5 %collective-permute-start.2 = (bf16[128,1024]{1,0:T(8,128)(2,1)S(1)}, bf16[128,1024]{1,0:T(8,128)(2,1)S(1)}, u32[]{:S(2)}, u32[]{:S(2)}) collective-permute-start(bf16[128,1024]{1,0:T(8,128)(2,1)S(1)} %copy-done.9), channel_id=1, source_target_pairs={{0,96},{16,112},{32,0},{48,16},{64,32},{80,48},{96,64},{112,80},{1... | collective-permute-start | bytes 786440 | tf_op jit(solution)/shard_map/ppermute | solution.py:291
  77.5 25.9 %collective-permute-start.10 = (bf16[128,1024]{1,0:T(8,128)(2,1)S(1)}, bf16[128,1024]{1,0:T(8,128)(2,1)}, u32[]{:S(2)}, u32[]{:S(2)}) collective-permute-start(bf16[128,1024]{1,0:T(8,128)(2,1)S(1)} %add_convert_fusion.1), channel_id=1, source_target_pairs={{0,16},{16,0},{32,48},{48,32},{64,80},{80,64},{96,112},{112,96},{1... | collective-permute-start | bytes 786440 | tf_op jit(solution)/shard_map/ppermute | solution.py:299
  92.4 21.1 %all-to-all-start.2 = ((bf16[8,64,512]{2,1,0:T(8,128)(2,1)}), bf16[8,64,512]{2,1,0:T(8,128)(2,1)S(1)}, u32[]{:S(2)}, u32[]{:S(2)}) async-start(bf16[8,64,512]{2,1,0:T(8,128)(2,1)} %square_grads.1.after), calls=%async_computation.2 | async-start | bytes 1048576 | tf_op jit(solution)/shard_map/all_to_all | solution.py:287
  99.8 19.4 %collective-permute-start.3 = (bf16[128,1024]{1,0:T(8,128)(2,1)S(1)}, bf16[128,1024]{1,0:T(8,128)(2,1)}, u32[]{:S(2)}, u32[]{:S(2)}) collective-permute-start(bf16[128,1024]{1,0:T(8,128)(2,1)S(1)} %add_convert_fusion.3.after), channel_id=1, source_target_pairs={{0,16},{16,0},{32,48},{48,32},{64,80},{80,64},{96,112},{112,96},{1... | collective-permute-start | bytes 786440 | tf_op jit(solution)/shard_map/ppermute | solution.py:299
  104.4 20.0 %collective-permute-start.13 = (bf16[128,1024]{1,0:T(8,128)(2,1)S(1)}, bf16[128,1024]{1,0:T(8,128)(2,1)S(1)}, u32[]{:S(2)}, u32[]{:S(2)}) collective-permute-start(bf16[128,1024]{1,0:T(8,128)(2,1)S(1)} %add_convert_fusion.f0), channel_id=1, source_target_pairs={{0,96},{16,112},{32,0},{48,16},{64,32},{80,48},{96,64},{112,80},{1... | collective-permute-start | bytes 786440 | tf_op jit(solution)/shard_map/ppermute | solution.py:303
  107.1 18.1 %collective-permute-start.12 = (bf16[128,1024]{1,0:T(8,128)(2,1)S(1)}, bf16[128,1024]{1,0:T(8,128)(2,1)}, u32[]{:S(2)}, u32[]{:S(2)}) collective-permute-start(bf16[128,1024]{1,0:T(8,128)(2,1)S(1)} %add_convert_fusion.f0), channel_id=1, source_target_pairs={{0,64},{16,80},{32,96},{48,112},{64,0},{80,16},{96,32},{112,48},{1... | collective-permute-start | bytes 786440 | tf_op jit(solution)/shard_map/ppermute | solution.py:303
  108.0 17.3 %collective-permute-start.11 = (bf16[128,1024]{1,0:T(8,128)(2,1)S(1)}, bf16[128,1024]{1,0:T(8,128)(2,1)}, u32[]{:S(2)}, u32[]{:S(2)}) collective-permute-start(bf16[128,1024]{1,0:T(8,128)(2,1)S(1)} %add_convert_fusion.f0), channel_id=1, source_target_pairs={{0,32},{16,48},{32,64},{48,80},{64,96},{80,112},{96,0},{112,16},{1... | collective-permute-start | bytes 786440 | tf_op jit(solution)/shard_map/ppermute | solution.py:303
  115.5 26.3 %all-to-all-start.3 = ((bf16[8,64,512]{2,1,0:T(8,128)(2,1)}), bf16[8,64,512]{2,1,0:T(8,128)(2,1)S(1)}, u32[]{:S(2)}, u32[]{:S(2)}) async-start(bf16[8,64,512]{2,1,0:T(8,128)(2,1)} %total.1), calls=%async_computation.3 | async-start | bytes 1048576 | tf_op jit(solution)/shard_map/all_to_all | solution.py:287
  120.2 14.0 %collective-permute-start.6 = (bf16[128,1024]{1,0:T(8,128)(2,1)S(1)}, bf16[128,1024]{1,0:T(8,128)(2,1)S(1)}, u32[]{:S(2)}, u32[]{:S(2)}) collective-permute-start(bf16[128,1024]{1,0:T(8,128)(2,1)S(1)} %add_convert_fusion.2.f0), channel_id=1, source_target_pairs={{0,96},{16,112},{32,0},{48,16},{64,32},{80,48},{96,64},{112,80},{1... | collective-permute-start | bytes 786440 | tf_op jit(solution)/shard_map/ppermute | solution.py:303
  123.5 11.9 %collective-permute-start.5 = (bf16[128,1024]{1,0:T(8,128)(2,1)S(1)}, bf16[128,1024]{1,0:T(8,128)(2,1)S(1)}, u32[]{:S(2)}, u32[]{:S(2)}) collective-permute-start(bf16[128,1024]{1,0:T(8,128)(2,1)S(1)} %add_convert_fusion.2.f0), channel_id=1, source_target_pairs={{0,64},{16,80},{32,96},{48,112},{64,0},{80,16},{96,32},{112,48},{1... | collective-permute-start | bytes 786440 | tf_op jit(solution)/shard_map/ppermute | solution.py:303
  124.4 15.9 %collective-permute-start.4 = (bf16[128,1024]{1,0:T(8,128)(2,1)S(1)}, bf16[128,1024]{1,0:T(8,128)(2,1)S(1)}, u32[]{:S(2)}, u32[]{:S(2)}) collective-permute-start(bf16[128,1024]{1,0:T(8,128)(2,1)S(1)} %add_convert_fusion.2.f0), channel_id=1, source_target_pairs={{0,32},{16,48},{32,64},{48,80},{64,96},{80,112},{96,0},{112,16},{1... | collective-permute-start | bytes 786440 | tf_op jit(solution)/shard_map/ppermute | solution.py:303
  (6 other events, 21.4 us)

commit v3 on v2

--- a/solution.py
+++ b/solution.py
@@ -127,8 +127,9 @@
     tgt_hbm, src_hbm, su_hbm, fd_hbm, r_ref, out_hbm, f0, f1, f2, f3, s0, s1, s2, s3,
     up_tgt, down_src, su, fd, act, hg, nar, mix, pfd, psu, out, sems, out_sems,
 ):
-    copies = start(((tgt_hbm, up_tgt), (src_hbm, down_src), (su_hbm, su), (fd_hbm, fd)), sems)
+    copies = start(((tgt_hbm, up_tgt), (src_hbm, down_src)), sems)
     copies[0].wait()
+    copies += [send(su_hbm, su, sems.at[2]), send(fd_hbm, fd, sems.at[3])]
     mixed_in = tn(up_tgt[...], r_ref[:, 0:32, :].reshape(512, 1024)).astype(BF)
     copies[1].wait()
     nar_grad = tn(down_src[...], r_ref[:, 32:64, :].reshape(512, 1024)).astype(BF)
@@ -174,7 +175,7 @@
 
 
 def square_grads(
-    tok_hbm, cot_hbm, src_hbm, tgt_hbm, r_ref, after, t_hbm, tok, cot, up_src, down_tgt, t, sems, out_sems
+    tok_hbm, cot_hbm, src_hbm, tgt_hbm, r_ref, t_hbm, tok, cot, up_src, down_tgt, t, sems, out_sems
 ):
     top, low = slice(0, 512), slice(512, 1024)
     pairs = (
@@ -223,27 +224,35 @@
         out_ref[i] = sums
 
 
-def finish_down(f0, f1, f2, f3, out_ref):
-    z = lax.shift_right_logical(lax.axis_index("dp"), 1)
-    for i, f in enumerate((f0, f1, f2, f3)):
-        c = (z - i) & 3
-        for b in range(4):
-            out_ref[c >> 1, pl.ds((c & 1) * 512 + 128 * b, 128), :] = f[:, 256 * b : 256 * b + 256].astype(F32)
-
-
-def finish_up(f0, f1, f2, f3, out_ref):
-    z = lax.shift_right_logical(lax.axis_index("dp"), 1)
-    for i, f in enumerate((f0, f1, f2, f3)):
-        c = (z - i) & 3
-        out_ref[c >> 1, pl.ds((c & 1) * 128, 128), :] = f[...].astype(F32)
-
-
-def finish_square(t_ref, gfu_ref, gsd_ref):
+def place(part_f, part_s, step, fd, su, fd_hbm, su_hbm, sems):
+    for b in range(4):
+        fd[128 * b : 128 * b + 128, :] = part_f[:, 256 * b : 256 * b + 256].astype(F32)
+    su[...] = part_s[...].astype(F32)
+    c = (lax.shift_right_logical(lax.axis_index("dp"), 1) - step) & 3
+    fd_at = fd_hbm.at[c >> 1, pl.ds(pl.multiple_of((c & 1) * 512, 512), 512)]
+    su_at = su_hbm.at[c >> 1, pl.ds(pl.multiple_of((c & 1) * 128, 128), 128)]
+    return start(((fd, fd_at), (su, su_at)), sems)
+
+
+def place_near(own, left, right, fd_hbm, su_hbm, fd, su, sems):
+    sent = []
+    for n, (part, step) in enumerate(((own, 0), (left, 1), (right, 3))):
+        halves = (part.at[0:128], part.at[128:256])
+        sent += place(*halves, step, fd.at[n], su.at[n], fd_hbm, su_hbm, sems.at[n])
+    for copy in sent:
+        copy.wait()
+
+
+def finish(f_far, s_far, t_ref, fd_in, su_in, fd_hbm, su_hbm, gfu_hbm, gsd_hbm, fd, su, gfu, gsd, sems, more_sems):
+    sent = place(f_far, s_far, 2, fd, su, fd_hbm, su_hbm, sems)
     for k in range(2):
         for i in range(4):
             rows = slice(64 * i, 64 * i + 64)
-            gsd_ref[k, rows, :] = t_ref[4 * k + i, :, 0:256].astype(F32)
-            gfu_ref[k, rows, :] = t_ref[4 * k + i, :, 256:512].astype(F32)
+            gsd[k, rows, :] = t_ref[4 * k + i, :, 0:256].astype(F32)
+            gfu[k, rows, :] = t_ref[4 * k + i, :, 256:512].astype(F32)
+    sent += start(((gfu, gfu_hbm), (gsd, gsd_hbm)), more_sems)
+    for copy in sent:
+        copy.wait()
 
 
 def like(*shape, dtype=BF):
@@ -262,14 +271,17 @@
     return [pl.BlockSpec(memory_space=space)] * count
 
 
-def run(kernel, args, out_shape, mega, hbm=0, after=(), out_space=pltpu.VMEM, scratch=(), sems=(), flops=0, moved=0):
+def run(kernel, args, out_shape, mega, hbm=0, after=(), out_space=pltpu.VMEM, aliases=None, scratch=(), sems=(), flops=0, moved=0):
     args = tuple(pltpu.with_memory_space_constraint(x, pltpu.HBM) if i < hbm else x for i, x in enumerate(args))
+    if not aliases:
+        after = tuple(pltpu.with_memory_space_constraint(x, pltpu.HBM) for x in after)
     return pl.pallas_call(
         kernel,
         out_shape=out_shape,
-        in_specs=placed(pltpu.HBM, hbm) + placed(pltpu.VMEM, len(args) - hbm) + placed(pl.ANY, len(after)),
+        in_specs=placed(pltpu.HBM, hbm) + placed(pltpu.VMEM, len(args) - hbm) + placed(pl.ANY if aliases else pltpu.HBM, len(after)),
         out_specs=placed(out_space, len(out_shape)),
-        scratch_shapes=list(scratch) + [pltpu.SemaphoreType.DMA((n,)) for n in sems],
+        input_output_aliases=aliases or {},
+        scratch_shapes=list(scratch) + [pltpu.SemaphoreType.DMA(n if isinstance(n, tuple) else (n,)) for n in sems],
         compiler_params=pltpu.CompilerParams(vmem_limit_bytes=mega * 2**20),
         cost_estimate=pl.CostEstimate(flops=flops, bytes_accessed=moved, transcendentals=0),
         name=kernel.__name__,
@@ -287,20 +299,25 @@
     return lax.all_to_all(values, axis, split_axis=0, concat_axis=0, tiled=True)
 
 
-def z_sum(parts):
-    got = [lax.ppermute(part, "dp", shift_z(i)) for i, part in enumerate(parts) if i]
+def shifted(part, step):
+    return lax.ppermute(part, "dp", shift_z(step))
+
+
+def added(*parts):
     sums = parts[0].astype(F32)
-    for part in got:
+    for part in parts[1:]:
         sums = sums + part.astype(F32)
     return sums.astype(BF)
 
 
-def x_sum(part):
-    return (part.astype(F32) + lax.ppermute(part, "dp", SWAP_X).astype(F32)).astype(BF)
-
-
-def z_gather(part):
-    return [part] + [lax.ppermute(part, "dp", shift_z(i)) for i in (1, 2, 3)]
+def z_sums(f, s):
+    f_on = shifted(f[2], 1)
+    s_on = shifted(s[2], 3)
+    s_got = shifted(s[1], 1)
+    f_got = shifted(f[3], 3)
+    f_far = shifted(added(f[1], f_on), 1)
+    s_far = shifted(added(s[3], s_on), 3)
+    return added(f[0], f_got, f_far), added(s[0], s_got, s_far)
 
 
 def per_device(tokens, first_up, second_up, first_down, second_down, perm_up, perm_down, cotangent):
@@ -349,23 +366,22 @@
         moved=9 * 10**6,
     )
     got = exchange(sent, "chan")
-    down_part = z_sum(grads[:4])
-    up_part = z_sum(grads[4:])
+    part = jnp.concatenate(z_sums(grads[:4], grads[4:]))
+    chunk = added(part, lax.ppermute(part, "dp", SWAP_X))
+    left, right = shifted(chunk, 1), shifted(chunk, 3)
+    f_far, s_far = shifted(left[:128], 1), shifted(right[128:], 3)
     (tail,) = run(
         square_grads,
         (tokens, cotangent, up_src, down_tgt, got),
         (far(8, 64, 512),),
         20,
         hbm=4,
-        after=(up_part,),
         out_space=pltpu.HBM,
         scratch=[near(1024, 512)] * 2 + [square, square, near(8, 64, 512)],
         sems=(6, 2),
         flops=16 * 10**8,
         moved=5 * 10**6,
     )
-    down_all = z_gather(x_sum(down_part))
-    up_all = z_gather(x_sum(up_part))
     tail_parts = exchange(tail, "dp")
     mixed, input_grad = run(
         outputs,
@@ -383,10 +399,31 @@
         total, (tail_parts,), (far(8, 64, 512),), 20, after=(mixed,), flops=10**6, moved=10**6
     )
     tail_all = exchange(tail_sums, "dp")
-    (grad_fd,) = run(finish_down, down_all, (like(2, 1024, 256, dtype=F32),), 20, flops=10**6, moved=3 * 10**6)
-    (grad_su,) = run(finish_up, up_all, (like(2, 256, 1024, dtype=F32),), 20, flops=10**6, moved=3 * 10**6)
-    grad_fu, grad_sd = run(
-        finish_square, (tail_all,), (like(2, 256, 256, dtype=F32),) * 2, 20, flops=10**6, moved=2 * 10**6
+    wide = (like(2, 1024, 256, dtype=F32), like(2, 256, 1024, dtype=F32))
+    held = run(
+        place_near,
+        (chunk, left, right),
+        wide,
+        24,
+        out_space=pl.ANY,
+        scratch=[pltpu.VMEM((3, 512, 256), F32), pltpu.VMEM((3, 128, 1024), F32)],
+        sems=((3, 2),),
+        flops=10**6,
+        moved=5 * 10**6,
+    )
+    small = like(2, 256, 256, dtype=F32)
+    grad_fd, grad_su, grad_fu, grad_sd = run(
+        finish,
+        (f_far, s_far, tail_all),
+        wide + (small, small),
+        24,
+        after=tuple(held),
+        out_space=pl.ANY,
+        aliases={3: 0, 4: 1},
+        scratch=[pltpu.VMEM((512, 256), F32), pltpu.VMEM((128, 1024), F32)] + [pltpu.VMEM((2, 256, 256), F32)] * 2,
+        sems=((2,), (2,)),
+        flops=10**6,
+        moved=4 * 10**6,
     )
     return (mixed, input_grad, grad_fu, grad_su, grad_fd, grad_sd)
 

time: 144 us -> 137 us (0.951)
  starting transfers between devices: 47.7 us -> 40.9 us
  waiting for transfers between devices: 54.4 us -> 56.3 us
    ppermute x14 -> x11, starting transfers between devices: 25.8 us -> 19.1 us  [the longest x10 16.4 us: shifted(): return lax.ppermute(part, 'dp', shift_z(step))]
    all_to_all x4, waiting for transfers between devices: 25.8 us -> 31.6 us  [exchange(): return lax.all_to_all(values, axis, split_axis=0, concat_axis=0, tiled=True)]
    ppermute x14 -> x11, waiting for transfers between devices: 28.6 us -> 24.7 us  [the longest x10 24.7 us: shifted(): return lax.ppermute(part, 'dp', shift_z(step))]
    unnamed x24 -> x22, local copies, waits for them, and re-layouts: 3.93 us -> 0.7 us
    slice x0 -> x2, local copies, waits for them, and re-layouts: none -> 1.94 us  [per_device(): f_far, s_far = (shifted(left[:128], 1), shifted(right[128:], 3))]
    pallas_call x9 -> x8, Pallas kernels: 33.6 us -> 33.1 us  [run(): pl.pallas_call(kernel, out_shape=out_shape, in_specs=placed(pltpu.HBM, hb...]
  transfers between devices with their start and end apart: 18 -> 15, of which waited for: 9 -> 9; matrix products, arithmetic and copies ran while one was open for 2% -> 3% of each run, Pallas kernels for 10% -> 10%
where the time goes in v3:
time: 137 us; the launch traced here: 136 us
  waiting for transfers between devices  56.3 us (41%)
  starting transfers between devices  40.9 us (30%)
  Pallas kernels  33.1 us (24%)
  local copies, waits for them, and re-layouts  2.64 us (2%)
  other arithmetic  1.72 us (1%)
    pallas_call x8, Pallas kernels, run(): pl.pallas_call(kernel, out_shape=out_shape, in_specs=placed(pltpu.HBM, hb...  33.1 us
    all_to_all x4, waiting for transfers between devices, exchange(): return lax.all_to_all(values, axis, split_axis=0, concat_axis=0, tiled=True)  31.6 us
    ppermute x10, waiting for transfers between devices, shifted(): return lax.ppermute(part, 'dp', shift_z(step))  24.7 us
    all_to_all x4, starting transfers between devices, exchange(): return lax.all_to_all(values, axis, split_axis=0, concat_axis=0, tiled=True)  21.8 us
    ppermute x10, starting transfers between devices, shifted(): return lax.ppermute(part, 'dp', shift_z(step))  16.4 us
    ppermute x1, starting transfers between devices, per_device(): chunk = added(part, lax.ppermute(part, 'dp', SWAP_X))  2.74 us
  transfers between devices with their start and end apart: 15, of which 9 were waited for; matrix products, arithmetic and copies ran while one was open for 3% of the time, Pallas kernels for 10%

profile of v3, /device:TPU:24, one launch (start us, length us, event | category | flops | bytes accessed | tf_op | source)
XLA Modules:
  0.0 135.7 jit_solution(1931572549002071929)
XLA Ops:
  0.6 4.3 %stage_one.1.mark = bf16[16,64,1024]{2,1,0:T(8,128)(2,1)} custom-call(bf16[1024,512]{1,0:T(8,128)(2,1)} %tok_hbm.3, bf16[1024,512]{1,0:T(8,128)(2,1)} %cot_hbm.3, bf16[2,256,256]{2,1,0:T(8,128)(2,1)} %fu_ref.1, bf16[2,256,256]{2,1,0:T(8,128)(2,1)} %sd_ref.1, s32[64,128]{1,0:T(8,128)} %bitcast.2, s32[64,128]{1,0:T(8,128)} %bitcast.4), custom_call_target="tpu_custom_call" | custom-call | flops 2000000000 | bytes 5000000 | tf_op jit(solution)/shard_map/stage_one/pallas_call | solution.py:278
  5.0 5.8 %all-to-all-start = ((bf16[16,64,1024]{2,1,0:T(8,128)(2,1)}), bf16[16,64,1024]{2,1,0:T(8,128)(2,1)S(1)}, u32[]{:S(2)}, u32[]{:S(2)}) async-start(bf16[16,64,1024]{2,1,0:T(8,128)(2,1)} %stage_one.1.mark), calls=%async_computation | async-start | bytes 4194304 | tf_op jit(solution)/shard_map/all_to_all | solution.py:299
  10.8 2.2 %prepare.1 = (bf16[512,512]{1,0:T(8,128)(2,1)}, bf16[512,512]{1,0:T(8,128)(2,1)}, bf16[512,512]{1,0:T(8,128)(2,1)}, bf16[512,512]{1,0:T(8,128)(2,1)}, bf16[512,5...) custom-call(bf16[2,256,256]{2,1,0:T(8,128)(2,1)S(1)} %copy-done, bf16[2,256,256]{2,1,0:T(8,128)(2,1)S(1)} %copy-done.1, ...), custom_call_target="tpu_custom_call" | custom-call | flops 2000000000 | bytes 4000000 | tf_op jit(solution)/shard_map/prepare/pallas_call | solution.py:278
  13.0 27.1 %all-to-all-done.r_ref = bf16[16,64,1024]{2,1,0:T(8,128)(2,1)S(1)} async-done(((bf16[16,64,1024]{2,1,0:T(8,128)(2,1)}), bf16[16,64,1024]{2,1,0:T(8,128)(2,1)S(1)}, u32[]{:S(2)}, u32[]{:S(2)}) %all-to-all-start) | async-done | bytes 2097184 | tf_op jit(solution)/shard_map/all_to_all | solution.py:299
  40.2 13.6 %stage_two.1 = (bf16[16,64,1024]{2,1,0:T(8,128)(2,1)}, bf16[128,1024]{1,0:T(8,128)(2,1)}, bf16[128,1024]{1,0:T(8,128)(2,1)}, bf16[128,1024]{1,0:T(8,128)(2,1)}, ...) custom-call(bf16[512,512]{1,0:T(8,128)(2,1)} %get-tuple-element.31.t, ...), custom_call_target="tpu_custom_call" | custom-call | flops 8499999744 | bytes 9000000 | tf_op jit(solution)/shard_map/stage_two/pallas_call | solution.py:278
  53.8 5.0 %all-to-all-start.1 = ((bf16[16,64,1024]{2,1,0:T(8,128)(2,1)}), bf16[16,64,1024]{2,1,0:T(8,128)(2,1)S(1)}, u32[]{:S(2)}, u32[]{:S(2)}) async-start(bf16[16,64,1024]{2,1,0:T(8,128)(2,1)} %get-tuple-element.33), calls=%async_computation.1 | async-start | bytes 4194304 | tf_op jit(solution)/shard_map/all_to_all | solution.py:299
  58.9 2.0 %collective-permute-start.1 = (bf16[128,1024]{1,0:T(8,128)(2,1)}, bf16[128,1024]{1,0:T(8,128)(2,1)S(1)}, u32[]{:S(2)}, u32[]{:S(2)}) collective-permute-start(bf16[128,1024]{1,0:T(8,128)(2,1)} %get-tuple-element.41), channel_id=1, source_target_pairs={{0,32},{16,48},{32,64},{48,80},{64,96},{80,112},{96,0},{112,16},{1... | collective-permute-start | bytes 786440 | tf_op jit(solution)/shard_map/ppermute | solution.py:303
  60.9 2.4 %collective-permute-start.4 = (bf16[128,1024]{1,0:T(8,128)(2,1)}, bf16[128,1024]{1,0:T(8,128)(2,1)S(1)}, u32[]{:S(2)}, u32[]{:S(2)}) collective-permute-start(bf16[128,1024]{1,0:T(8,128)(2,1)} %get-tuple-element.45), channel_id=1, source_target_pairs={{0,96},{16,112},{32,0},{48,16},{64,32},{80,48},{96,64},{112,80},{1... | collective-permute-start | bytes 786440 | tf_op jit(solution)/shard_map/ppermute | solution.py:303
  65.0 4.8 %collective-permute-done.1 = bf16[128,1024]{1,0:T(8,128)(2,1)S(1)} collective-permute-done((bf16[128,1024]{1,0:T(8,128)(2,1)}, bf16[128,1024]{1,0:T(8,128)(2,1)S(1)}, u32[]{:S(2)}, u32[]{:S(2)}) %collective-permute-start.1) | collective-permute-done | bytes 262176 | tf_op jit(solution)/shard_map/ppermute | solution.py:303
  71.6 2.4 %collective-permute-start.5 = (bf16[128,1024]{1,0:T(8,128)(2,1)S(1)}, bf16[128,1024]{1,0:T(8,128)(2,1)S(1)}, u32[]{:S(2)}, u32[]{:S(2)}) collective-permute-start(bf16[128,1024]{1,0:T(8,128)(2,1)S(1)} %add_convert_fusion.2), channel_id=1, source_target_pairs={{0,96},{16,112},{32,0},{48,16},{64,32},{80,48},{96,64},{112,80},{1... | collective-permute-start | bytes 786440 | tf_op jit(solution)/shard_map/ppermute | solution.py:303
  75.8 4.5 %collective-permute-done.2 = bf16[128,1024]{1,0:T(8,128)(2,1)S(1)} collective-permute-done((bf16[128,1024]{1,0:T(8,128)(2,1)S(1)}, bf16[128,1024]{1,0:T(8,128)(2,1)S(1)}, u32[]{:S(2)}, u32[]{:S(2)}) %collective-permute-start.2) | collective-permute-done | bytes 262176 | tf_op jit(solution)/shard_map/ppermute | solution.py:303
  80.5 4.1 %collective-permute-done.3 = bf16[128,1024]{1,0:T(8,128)(2,1)S(1)} collective-permute-done((bf16[128,1024]{1,0:T(8,128)(2,1)S(1)}, bf16[128,1024]{1,0:T(8,128)(2,1)S(1)}, u32[]{:S(2)}, u32[]{:S(2)}) %collective-permute-start.3) | collective-permute-done | bytes 262176 | tf_op jit(solution)/shard_map/ppermute | solution.py:303
  85.5 2.7 %collective-permute-start.6 = (bf16[256,1024]{1,0:T(8,128)(2,1)S(1)}, bf16[256,1024]{1,0:T(8,128)(2,1)}, u32[]{:S(2)}, u32[]{:S(2)}) collective-permute-start(bf16[256,1024]{1,0:T(8,128)(2,1)S(1)} %pad_maximum_fusion), channel_id=1, source_target_pairs={{0,16},{16,0},{32,48},{48,32},{64,80},{80,64},{96,112},{112,96},{1... | collective-permute-start | bytes 1572872 | tf_op jit(solution)/shard_map/ppermute | solution.py:370
  88.2 4.2 %square_grads.1.after = bf16[8,64,512]{2,1,0:T(8,128)(2,1)} custom-call(bf16[1024,512]{1,0:T(8,128)(2,1)} %tok_hbm.3, bf16[1024,512]{1,0:T(8,128)(2,1)} %cot_hbm.3, bf16[512,512]{1,0:T(8,128)(2,1)} %get-tuple-element.34.src_hbm, bf16[512,512]{1,0:T(8,128)(2,1)} %get-tuple-element.35.tgt_hbm, bf16[16,64,1024]{2,1,0:T(8,128)(2,1)S(1)} %all-to-all-done.1.r_ref), custom_call_target="tpu_custom_call" | custom-call | flops 1600000000 | bytes 5000000 | tf_op jit(solution)/shard_map/square_grads/pallas_call | solution.py:278
  92.4 7.5 %all-to-all-start.2 = ((bf16[8,64,512]{2,1,0:T(8,128)(2,1)}), bf16[8,64,512]{2,1,0:T(8,128)(2,1)S(1)}, u32[]{:S(2)}, u32[]{:S(2)}) async-start(bf16[8,64,512]{2,1,0:T(8,128)(2,1)} %square_grads.1.after), calls=%async_computation.2 | async-start | bytes 1048576 | tf_op jit(solution)/shard_map/all_to_all | solution.py:299
  101.3 3.3 %collective-permute-start.9 = (bf16[256,1024]{1,0:T(8,128)(2,1)S(1)}, bf16[256,1024]{1,0:T(8,128)(2,1)}, u32[]{:S(2)}, u32[]{:S(2)}) collective-permute-start(bf16[256,1024]{1,0:T(8,128)(2,1)S(1)} %add_convert_fusion.own), channel_id=1, source_target_pairs={{0,96},{16,112},{32,0},{48,16},{64,32},{80,48},{96,64},{112,80},{1... | collective-permute-start | bytes 1572872 | tf_op jit(solution)/shard_map/ppermute | solution.py:303
  104.6 3.5 %outputs.1 = (bf16[1024,512]{1,0:T(8,128)(2,1)}, bf16[1024,512]{1,0:T(8,128)(2,1)}) custom-call(bf16[512,512]{1,0:T(8,128)(2,1)} %get-tuple-element.29.up_hbm, bf16[512,512]{1,0:T(8,128)(2,1)} %get-tuple-element.30.down_hbm, bf16[16,64,1024]{2,1,0:T(8,128)(2,1)S(1)} %all-to-all-done.1.r_ref, bf16[8,64,512]{2,1,0:T(8,128)(2,1)} %square_grads.1.after), custom_call_target="tpu_custom_call" | custom-call | flops 1000000000 | bytes 5000000 | tf_op jit(solution)/shard_map/outputs/pallas_call | solution.py:278
  108.1 4.4 %all-to-all-done.2.t_ref = bf16[8,64,512]{2,1,0:T(8,128)(2,1)S(1)} async-done(((bf16[8,64,512]{2,1,0:T(8,128)(2,1)}), bf16[8,64,512]{2,1,0:T(8,128)(2,1)S(1)}, u32[]{:S(2)}, u32[]{:S(2)}) %all-to-all-start.2) | async-done | bytes 524320 | tf_op jit(solution)/shard_map/all_to_all | solution.py:299
  113.4 3.5 %all-to-all-start.3 = ((bf16[8,64,512]{2,1,0:T(8,128)(2,1)}), bf16[8,64,512]{2,1,0:T(8,128)(2,1)S(1)}, u32[]{:S(2)}, u32[]{:S(2)}) async-start(bf16[8,64,512]{2,1,0:T(8,128)(2,1)} %total.1), calls=%async_computation.3 | async-start | bytes 1048576 | tf_op jit(solution)/shard_map/all_to_all | solution.py:299
  116.9 3.7 %collective-permute-done.9.right = bf16[256,1024]{1,0:T(8,128)(2,1)} collective-permute-done((bf16[256,1024]{1,0:T(8,128)(2,1)S(1)}, bf16[256,1024]{1,0:T(8,128)(2,1)}, u32[]{:S(2)}, u32[]{:S(2)}) %collective-permute-start.9) | collective-permute-done | bytes 524320 | tf_op jit(solution)/shard_map/ppermute | solution.py:303
  121.6 2.9 %collective-permute-start.10 = (bf16[128,1024]{1,0:T(8,128)(2,1)S(1)}, bf16[128,1024]{1,0:T(8,128)(2,1)S(1)}, u32[]{:S(2)}, u32[]{:S(2)}) collective-permute-start(bf16[128,1024]{1,0:T(8,128)(2,1)S(1)} %slice.9), channel_id=1, source_target_pairs={{0,96},{16,112},{32,0},{48,16},{64,32},{80,48},{96,64},{112,80},{1... | collective-permute-start | bytes 786440 | tf_op jit(solution)/shard_map/ppermute | solution.py:303
  125.5 2.9 %place_near.1 = (f32[2,1024,256]{2,1,0:T(8,128)}, f32[2,256,1024]{2,1,0:T(8,128)}) custom-call(bf16[256,1024]{1,0:T(8,128)(2,1)S(1)} %add_convert_fusion.own, bf16[256,1024]{1,0:T(8,128)(2,1)} %collective-permute-done.7.left, bf16[256,1024]{1,0:T(8,128)(2,1)} %collective-permute-done.9.right), custom_call_target="tpu_custom_call" | custom-call | flops 1000000 | bytes 5000000 | tf_op jit(solution)/shard_map/place_near/pallas_call | solution.py:278
  128.5 2.9 %collective-permute-done.10.s_far = bf16[128,1024]{1,0:T(8,128)(2,1)S(1)} collective-permute-done((bf16[128,1024]{1,0:T(8,128)(2,1)S(1)}, bf16[128,1024]{1,0:T(8,128)(2,1)S(1)}, u32[]{:S(2)}, u32[]{:S(2)}) %collective-permute-start.10) | collective-permute-done | bytes 262176 | tf_op jit(solution)/shard_map/ppermute | solution.py:303
  131.4 2.8 %collective-permute-done.8.f_far = bf16[128,1024]{1,0:T(8,128)(2,1)S(1)} collective-permute-done((bf16[128,1024]{1,0:T(8,128)(2,1)S(1)}, bf16[128,1024]{1,0:T(8,128)(2,1)S(1)}, u32[]{:S(2)}, u32[]{:S(2)}) %collective-permute-start.8) | collective-permute-done | bytes 262176 | tf_op jit(solution)/shard_map/ppermute | solution.py:303
  (44 shorter events, 12.0 us)
Async XLA Ops:
  5.0 5.8 %copy-start = (bf16[2,256,256]{2,1,0:T(8,128)(2,1)S(1)}, bf16[2,256,256]{2,1,0:T(8,128)(2,1)}, u32[]{:S(2)}) copy-start(bf16[2,256,256]{2,1,0:T(8,128)(2,1)} %fu_ref.1) | copy-start | bytes 786436
  5.0 5.8 %copy-start.1 = (bf16[2,256,256]{2,1,0:T(8,128)(2,1)S(1)}, bf16[2,256,256]{2,1,0:T(8,128)(2,1)}, u32[]{:S(2)}) copy-start(bf16[2,256,256]{2,1,0:T(8,128)(2,1)} %sd_ref.1) | copy-start | bytes 786436
  5.0 5.8 %copy-start.2 = (s32[8192]{0:T(1024)S(1)}, s32[8192]{0:T(1024)}, u32[]{:S(2)}) copy-start(s32[8192]{0:T(1024)} %param.13) | copy-start | bytes 98308
  5.0 35.2 %all-to-all-start = ((bf16[16,64,1024]{2,1,0:T(8,128)(2,1)}), bf16[16,64,1024]{2,1,0:T(8,128)(2,1)S(1)}, u32[]{:S(2)}, u32[]{:S(2)}) async-start(bf16[16,64,1024]{2,1,0:T(8,128)(2,1)} %stage_one.1.mark), calls=%async_computation | async-start | bytes 4194304 | tf_op jit(solution)/shard_map/all_to_all | solution.py:299
  53.8 9.5 %copy-start.10 = (bf16[128,1024]{1,0:T(8,128)(2,1)S(1)}, bf16[128,1024]{1,0:T(8,128)(2,1)}, u32[]{:S(2)}) copy-start(bf16[128,1024]{1,0:T(8,128)(2,1)} %get-tuple-element.39) | copy-start | bytes 786436
  53.8 16.0 %copy-start.6 = (bf16[128,1024]{1,0:T(8,128)(2,1)S(1)}, bf16[128,1024]{1,0:T(8,128)(2,1)}, u32[]{:S(2)}) copy-start(bf16[128,1024]{1,0:T(8,128)(2,1)} %get-tuple-element.40) | copy-start | bytes 786436
  53.8 16.2 %copy-start.9 = (bf16[128,1024]{1,0:T(8,128)(2,1)S(1)}, bf16[128,1024]{1,0:T(8,128)(2,1)}, u32[]{:S(2)}) copy-start(bf16[128,1024]{1,0:T(8,128)(2,1)} %get-tuple-element.43) | copy-start | bytes 786436
  53.8 17.7 %copy-start.5 = (bf16[128,1024]{1,0:T(8,128)(2,1)S(1)}, bf16[128,1024]{1,0:T(8,128)(2,1)}, u32[]{:S(2)}) copy-start(bf16[128,1024]{1,0:T(8,128)(2,1)} %get-tuple-element.44) | copy-start | bytes 786436
  53.8 26.6 %copy-start.8 = (bf16[128,1024]{1,0:T(8,128)(2,1)S(1)}, bf16[128,1024]{1,0:T(8,128)(2,1)}, u32[]{:S(2)}) copy-start(bf16[128,1024]{1,0:T(8,128)(2,1)} %get-tuple-element.38) | copy-start | bytes 786436
  53.8 34.4 %all-to-all-start.1 = ((bf16[16,64,1024]{2,1,0:T(8,128)(2,1)}), bf16[16,64,1024]{2,1,0:T(8,128)(2,1)S(1)}, u32[]{:S(2)}, u32[]{:S(2)}) async-start(bf16[16,64,1024]{2,1,0:T(8,128)(2,1)} %get-tuple-element.33), calls=%async_computation.1 | async-start | bytes 4194304 | tf_op jit(solution)/shard_map/all_to_all | solution.py:299
  58.9 25.8 %copy-start.7 = (bf16[128,1024]{1,0:T(8,128)(2,1)S(1)}, bf16[128,1024]{1,0:T(8,128)(2,1)}, u32[]{:S(2)}) copy-start(bf16[128,1024]{1,0:T(8,128)(2,1)} %get-tuple-element.42) | copy-start | bytes 786436
  58.9 10.9 %collective-permute-start.1 = (bf16[128,1024]{1,0:T(8,128)(2,1)}, bf16[128,1024]{1,0:T(8,128)(2,1)S(1)}, u32[]{:S(2)}, u32[]{:S(2)}) collective-permute-start(bf16[128,1024]{1,0:T(8,128)(2,1)} %get-tuple-element.41), channel_id=1, source_target_pairs={{0,32},{16,48},{32,64},{48,80},{64,96},{80,112},{96,0},{112,16},{1... | collective-permute-start | bytes 786440 | tf_op jit(solution)/shard_map/ppermute | solution.py:303
  60.9 10.7 %collective-permute-start.4 = (bf16[128,1024]{1,0:T(8,128)(2,1)}, bf16[128,1024]{1,0:T(8,128)(2,1)S(1)}, u32[]{:S(2)}, u32[]{:S(2)}) collective-permute-start(bf16[128,1024]{1,0:T(8,128)(2,1)} %get-tuple-element.45), channel_id=1, source_target_pairs={{0,96},{16,112},{32,0},{48,16},{64,32},{80,48},{96,64},{112,80},{1... | collective-permute-start | bytes 786440 | tf_op jit(solution)/shard_map/ppermute | solution.py:303
  63.2 12.6 %collective-permute-start = (bf16[128,1024]{1,0:T(8,128)(2,1)S(1)}, bf16[128,1024]{1,0:T(8,128)(2,1)S(1)}, u32[]{:S(2)}, u32[]{:S(2)}) collective-permute-start(bf16[128,1024]{1,0:T(8,128)(2,1)S(1)} %copy-done.10), channel_id=1, source_target_pairs={{0,96},{16,112},{32,0},{48,16},{64,32},{80,48},{96,64},{112,80},{1... | collective-permute-start | bytes 786440 | tf_op jit(solution)/shard_map/ppermute | solution.py:303
  69.9 10.5 %collective-permute-start.2 = (bf16[128,1024]{1,0:T(8,128)(2,1)S(1)}, bf16[128,1024]{1,0:T(8,128)(2,1)S(1)}, u32[]{:S(2)}, u32[]{:S(2)}) collective-permute-start(bf16[128,1024]{1,0:T(8,128)(2,1)S(1)} %add_convert_fusion.4), channel_id=1, source_target_pairs={{0,32},{16,48},{32,64},{48,80},{64,96},{80,112},{96,0},{112,16},{1... | collective-permute-start | bytes 786440 | tf_op jit(solution)/shard_map/ppermute | solution.py:303
  70.0 14.7 %collective-permute-start.3 = (bf16[128,1024]{1,0:T(8,128)(2,1)S(1)}, bf16[128,1024]{1,0:T(8,128)(2,1)S(1)}, u32[]{:S(2)}, u32[]{:S(2)}) collective-permute-start(bf16[128,1024]{1,0:T(8,128)(2,1)S(1)} %copy-done.9), channel_id=1, source_target_pairs={{0,32},{16,48},{32,64},{48,80},{64,96},{80,112},{96,0},{112,16},{1... | collective-permute-start | bytes 786440 | tf_op jit(solution)/shard_map/ppermute | solution.py:303
  71.6 13.0 %collective-permute-start.5 = (bf16[128,1024]{1,0:T(8,128)(2,1)S(1)}, bf16[128,1024]{1,0:T(8,128)(2,1)S(1)}, u32[]{:S(2)}, u32[]{:S(2)}) collective-permute-start(bf16[128,1024]{1,0:T(8,128)(2,1)S(1)} %add_convert_fusion.2), channel_id=1, source_target_pairs={{0,96},{16,112},{32,0},{48,16},{64,32},{80,48},{96,64},{112,80},{1... | collective-permute-start | bytes 786440 | tf_op jit(solution)/shard_map/ppermute | solution.py:303
  85.5 14.5 %collective-permute-start.6 = (bf16[256,1024]{1,0:T(8,128)(2,1)S(1)}, bf16[256,1024]{1,0:T(8,128)(2,1)}, u32[]{:S(2)}, u32[]{:S(2)}) collective-permute-start(bf16[256,1024]{1,0:T(8,128)(2,1)S(1)} %pad_maximum_fusion), channel_id=1, source_target_pairs={{0,16},{16,0},{32,48},{48,32},{64,80},{80,64},{96,112},{112,96},{1... | collective-permute-start | bytes 1572872 | tf_op jit(solution)/shard_map/ppermute | solution.py:370
  92.4 20.1 %all-to-all-start.2 = ((bf16[8,64,512]{2,1,0:T(8,128)(2,1)}), bf16[8,64,512]{2,1,0:T(8,128)(2,1)S(1)}, u32[]{:S(2)}, u32[]{:S(2)}) async-start(bf16[8,64,512]{2,1,0:T(8,128)(2,1)} %square_grads.1.after), calls=%async_computation.2 | async-start | bytes 1048576 | tf_op jit(solution)/shard_map/all_to_all | solution.py:299
  101.3 19.3 %collective-permute-start.9 = (bf16[256,1024]{1,0:T(8,128)(2,1)S(1)}, bf16[256,1024]{1,0:T(8,128)(2,1)}, u32[]{:S(2)}, u32[]{:S(2)}) collective-permute-start(bf16[256,1024]{1,0:T(8,128)(2,1)S(1)} %add_convert_fusion.own), channel_id=1, source_target_pairs={{0,96},{16,112},{32,0},{48,16},{64,32},{80,48},{96,64},{112,80},{1... | collective-permute-start | bytes 1572872 | tf_op jit(solution)/shard_map/ppermute | solution.py:303
  104.6 19.9 %collective-permute-start.7 = (bf16[256,1024]{1,0:T(8,128)(2,1)S(1)}, bf16[256,1024]{1,0:T(8,128)(2,1)}, u32[]{:S(2)}, u32[]{:S(2)}) collective-permute-start(bf16[256,1024]{1,0:T(8,128)(2,1)S(1)} %add_convert_fusion.own), channel_id=1, source_target_pairs={{0,32},{16,48},{32,64},{48,80},{64,96},{80,112},{96,0},{112,16},{1... | collective-permute-start | bytes 1572872 | tf_op jit(solution)/shard_map/ppermute | solution.py:303
  113.4 20.7 %all-to-all-start.3 = ((bf16[8,64,512]{2,1,0:T(8,128)(2,1)}), bf16[8,64,512]{2,1,0:T(8,128)(2,1)S(1)}, u32[]{:S(2)}, u32[]{:S(2)}) async-start(bf16[8,64,512]{2,1,0:T(8,128)(2,1)} %total.1), calls=%async_computation.3 | async-start | bytes 1048576 | tf_op jit(solution)/shard_map/all_to_all | solution.py:299
  121.6 9.8 %collective-permute-start.10 = (bf16[128,1024]{1,0:T(8,128)(2,1)S(1)}, bf16[128,1024]{1,0:T(8,128)(2,1)S(1)}, u32[]{:S(2)}, u32[]{:S(2)}) collective-permute-start(bf16[128,1024]{1,0:T(8,128)(2,1)S(1)} %slice.9), channel_id=1, source_target_pairs={{0,96},{16,112},{32,0},{48,16},{64,32},{80,48},{96,64},{112,80},{1... | collective-permute-start | bytes 786440 | tf_op jit(solution)/shard_map/ppermute | solution.py:303
  125.5 8.7 %collective-permute-start.8 = (bf16[128,1024]{1,0:T(8,128)(2,1)S(1)}, bf16[128,1024]{1,0:T(8,128)(2,1)S(1)}, u32[]{:S(2)}, u32[]{:S(2)}) collective-permute-start(bf16[128,1024]{1,0:T(8,128)(2,1)S(1)} %slice.8), channel_id=1, source_target_pairs={{0,32},{16,48},{32,64},{48,80},{64,96},{80,112},{96,0},{112,16},{1... | collective-permute-start | bytes 786440 | tf_op jit(solution)/shard_map/ppermute | solution.py:303
  (2 other events, 6.5 us)

commit v4 on v3

--- a/solution.py
+++ b/solution.py
@@ -124,17 +124,15 @@
 
 
 def stage_two(
-    tgt_hbm, src_hbm, su_hbm, fd_hbm, r_ref, out_hbm, f0, f1, f2, f3, s0, s1, s2, s3,
-    up_tgt, down_src, su, fd, act, hg, nar, mix, pfd, psu, out, sems, out_sems,
+    src_hbm, su_hbm, fd_hbm, up_tgt, r_ref, out_hbm, f0, f1, f2, f3, s0, s1, s2, s3,
+    down_src, su, fd, act, hg, nar, mix, pfd, psu, out, sems, out_sems,
 ):
-    copies = start(((tgt_hbm, up_tgt), (src_hbm, down_src)), sems)
+    copies = start(((src_hbm, down_src), (su_hbm, su), (fd_hbm, fd)), sems)
+    mixed_in = tn(up_tgt[...], r_ref[:, 0:32, :].reshape(512, 1024)).astype(BF)
     copies[0].wait()
-    copies += [send(su_hbm, su, sems.at[2]), send(fd_hbm, fd, sems.at[3])]
-    mixed_in = tn(up_tgt[...], r_ref[:, 0:32, :].reshape(512, 1024)).astype(BF)
+    nar_grad = tn(down_src[...], r_ref[:, 32:64, :].reshape(512, 1024)).astype(BF)
     copies[1].wait()
-    nar_grad = tn(down_src[...], r_ref[:, 32:64, :].reshape(512, 1024)).astype(BF)
     copies[2].wait()
-    copies[3].wait()
     z = lax.shift_right_logical(lax.axis_index("dp"), 1)
     sent = []
     for k in range(2):
@@ -164,12 +162,12 @@
         nar[256 * k : 256 * k + 256, :] = tn(fd[k], act[k]).astype(BF)
         mix[256 * k : 256 * k + 256, :] = nn(su[k], hg[k]).astype(BF)
     for i, (matrix, rows) in enumerate(((down_src, nar), (up_tgt, mix))):
-        for j in range(2):
-            groups = slice(8 * j, 8 * j + 8)
-            part = nn(matrix[256 * j : 256 * j + 256, :], rows[...]).astype(BF)
-            out[groups, 32 * i : 32 * i + 32, :] = part.reshape(8, 32, 1024)
+        for j in range(4):
+            groups = slice(4 * j, 4 * j + 4)
+            part = nn(matrix[128 * j : 128 * j + 128, :], rows[...]).astype(BF)
+            out[groups, 32 * i : 32 * i + 32, :] = part.reshape(4, 32, 1024)
             at = (groups, slice(32 * i, 32 * i + 32))
-            sent.append(send(out.at[at], out_hbm.at[at], out_sems.at[8 + 2 * i + j]))
+            sent.append(send(out.at[at], out_hbm.at[at], out_sems.at[8 + 4 * i + j]))
     for copy in sent:
         copy.wait()
 
@@ -224,6 +222,20 @@
         out_ref[i] = sums
 
 
+def join(f0, f1, f2, s0, s1, s2, out_ref):
+    out_ref[0:128, :] = (f0[...].astype(F32) + f1[...].astype(F32) + f2[...].astype(F32)).astype(BF)
+    out_ref[128:256, :] = (s0[...].astype(F32) + s1[...].astype(F32) + s2[...].astype(F32)).astype(BF)
+
+
+def pair(mine, other, out_ref):
+    out_ref[...] = (mine[...].astype(F32) + other[...].astype(F32)).astype(BF)
+
+
+def halves(left, right, f_out, s_out):
+    f_out[...] = left[0:128, :]
+    s_out[...] = right[128:256, :]
+
+
 def place(part_f, part_s, step, fd, su, fd_hbm, su_hbm, sems):
     for b in range(4):
         fd[128 * b : 128 * b + 128, :] = part_f[:, 256 * b : 256 * b + 256].astype(F32)
@@ -317,7 +329,8 @@
     f_got = shifted(f[3], 3)
     f_far = shifted(added(f[1], f_on), 1)
     s_far = shifted(added(s[3], s_on), 3)
-    return added(f[0], f_got, f_far), added(s[0], s_got, s_far)
+    (part,) = run(join, (f[0], f_got, f_far, s[0], s_got, s_far), (like(256, 1024),), 16, flops=1, moved=2 * 10**6)
+    return part
 
 
 def per_device(tokens, first_up, second_up, first_down, second_down, perm_up, perm_down, cotangent):
@@ -343,7 +356,7 @@
     up_src, up_tgt, down_src, down_tgt, w_up, w_down = run(
         prepare,
         (first_up, second_down) + perms,
-        (far(512, 512),) * 6,
+        (far(512, 512), square) + (far(512, 512),) * 4,
         20,
         after=(sent,),
         flops=2 * 10**9,
@@ -351,25 +364,27 @@
     )
     sent, *grads = run(
         stage_two,
-        (up_tgt, down_src, second_up, first_down, got),
+        (down_src, second_up, first_down, pltpu.with_memory_space_constraint(up_tgt, pltpu.VMEM), got),
         (far(16, 64, 1024),) + (far(128, 1024),) * 8,
         32,
-        hbm=4,
+        hbm=3,
         out_space=pltpu.HBM,
-        scratch=[square, square, near(2, 256, 1024), near(2, 1024, 256)]
+        scratch=[square, near(2, 256, 1024), near(2, 1024, 256)]
         + [near(2, 1024, 1024)] * 2
         + [near(512, 1024)] * 2
         + [near(4, 128, 1024)] * 2
         + [near(16, 64, 1024)],
-        sems=(4, 12),
+        sems=(3, 16),
         flops=85 * 10**8,
         moved=9 * 10**6,
     )
     got = exchange(sent, "chan")
-    part = jnp.concatenate(z_sums(grads[:4], grads[4:]))
-    chunk = added(part, lax.ppermute(part, "dp", SWAP_X))
+    part = z_sums(grads[:4], grads[4:])
+    other = lax.ppermute(part, "dp", SWAP_X)
+    (chunk,) = run(pair, (part, other), (like(256, 1024),), 16, flops=1, moved=2 * 10**6)
     left, right = shifted(chunk, 1), shifted(chunk, 3)
-    f_far, s_far = shifted(left[:128], 1), shifted(right[128:], 3)
+    f_on, s_on = run(halves, (left, right), (like(128, 1024),) * 2, 16, flops=1, moved=10**6)
+    f_far, s_far = shifted(f_on, 1), shifted(s_on, 3)
     (tail,) = run(
         square_grads,
         (tokens, cotangent, up_src, down_tgt, got),

time: 137 us -> 135 us (0.985)
  waiting for transfers between devices: 56.3 us -> 58.9 us
  other arithmetic: 1.72 us -> 0.14 us
    all_to_all x4, waiting for transfers between devices: 31.6 us -> 35.5 us  [exchange(): return lax.all_to_all(values, axis, split_axis=0, concat_axis=0, tiled=True)]
    slice x2 -> x0, local copies, waits for them, and re-layouts: 1.94 us -> none  [per_device(): f_far, s_far = (shifted(left[:128], 1), shifted(right[128:], 3))]
    convert_element_type x5 -> x2, other arithmetic: 1.68 us -> 0.14 us  [added(): return sums.astype(BF)]
    pallas_call x8 -> x11, Pallas kernels: 33.1 us -> 31.9 us  [run(): pl.pallas_call(kernel, out_shape=out_shape, in_specs=placed(pltpu.HBM, hb...]
  transfers between devices with their start and end apart: 15 -> 15, of which waited for: 9 -> 9; matrix products, arithmetic and copies ran while one was open for 3% -> 0% of each run, Pallas kernels for 10% -> 10%
where the time goes in v4:
time: 135 us; the launch traced here: 134 us
  waiting for transfers between devices  58.9 us (44%)
  starting transfers between devices  40.7 us (30%)
  Pallas kernels  31.9 us (24%)
  local copies, waits for them, and re-layouts  1.64 us (1%)
    all_to_all x4, waiting for transfers between devices, exchange(): return lax.all_to_all(values, axis, split_axis=0, concat_axis=0, tiled=True)  35.5 us
    pallas_call x11, Pallas kernels, run(): pl.pallas_call(kernel, out_shape=out_shape, in_specs=placed(pltpu.HBM, hb...  31.9 us
    ppermute x10, waiting for transfers between devices, shifted(): return lax.ppermute(part, 'dp', shift_z(step))  23.4 us
    all_to_all x4, starting transfers between devices, exchange(): return lax.all_to_all(values, axis, split_axis=0, concat_axis=0, tiled=True)  21.8 us
    ppermute x10, starting transfers between devices, shifted(): return lax.ppermute(part, 'dp', shift_z(step))  16.1 us
    ppermute x1, starting transfers between devices, per_device(): other = lax.ppermute(part, 'dp', SWAP_X)  2.81 us
  transfers between devices with their start and end apart: 15, of which 9 were waited for; matrix products, arithmetic and copies ran while one was open for 0% of the time, Pallas kernels for 10%

profile of v4, /device:TPU:24, one launch (start us, length us, event | category | flops | bytes accessed | tf_op | source)
XLA Modules:
  0.0 134.4 jit_solution(4344083981008147403)
XLA Ops:
  0.6 4.3 %stage_one.1.mark = bf16[16,64,1024]{2,1,0:T(8,128)(2,1)} custom-call(bf16[1024,512]{1,0:T(8,128)(2,1)} %tok_hbm.3, bf16[1024,512]{1,0:T(8,128)(2,1)} %cot_hbm.3, bf16[2,256,256]{2,1,0:T(8,128)(2,1)} %fu_ref.1, bf16[2,256,256]{2,1,0:T(8,128)(2,1)} %sd_ref.1, s32[64,128]{1,0:T(8,128)} %bitcast.2, s32[64,128]{1,0:T(8,128)} %bitcast.4), custom_call_target="tpu_custom_call" | custom-call | flops 2000000000 | bytes 5000000 | tf_op jit(solution)/shard_map/stage_one/pallas_call | solution.py:290
  5.0 5.8 %all-to-all-start = ((bf16[16,64,1024]{2,1,0:T(8,128)(2,1)}), bf16[16,64,1024]{2,1,0:T(8,128)(2,1)S(1)}, u32[]{:S(2)}, u32[]{:S(2)}) async-start(bf16[16,64,1024]{2,1,0:T(8,128)(2,1)} %stage_one.1.mark), calls=%async_computation | async-start | bytes 4194304 | tf_op jit(solution)/shard_map/all_to_all | solution.py:311
  10.8 2.1 %prepare.1 = (bf16[512,512]{1,0:T(8,128)(2,1)}, bf16[512,512]{1,0:T(8,128)(2,1)S(1)}, bf16[512,512]{1,0:T(8,128)(2,1)}, bf16[512,512]{1,0:T(8,128)(2,1)}, bf16[5...) custom-call(bf16[2,256,256]{2,1,0:T(8,128)(2,1)S(1)} %copy-done.4, bf16[2,256,256]{2,1,0:T(8,128)(2,1)S(1)} %copy-done.5, ...), custom_call_target="tpu_custom_call" | custom-call | flops 2000000000 | bytes 4000000 | tf_op jit(solution)/shard_map/prepare/pallas_call | solution.py:290
  12.9 27.3 %all-to-all-done.r_ref = bf16[16,64,1024]{2,1,0:T(8,128)(2,1)S(1)} async-done(((bf16[16,64,1024]{2,1,0:T(8,128)(2,1)}), bf16[16,64,1024]{2,1,0:T(8,128)(2,1)S(1)}, u32[]{:S(2)}, u32[]{:S(2)}) %all-to-all-start) | async-done | bytes 2097184 | tf_op jit(solution)/shard_map/all_to_all | solution.py:311
  40.2 12.7 %stage_two.1 = (bf16[16,64,1024]{2,1,0:T(8,128)(2,1)}, bf16[128,1024]{1,0:T(8,128)(2,1)}, bf16[128,1024]{1,0:T(8,128)(2,1)}, bf16[128,1024]{1,0:T(8,128)(2,1)}, ...) custom-call(bf16[512,512]{1,0:T(8,128)(2,1)} %get-tuple-element.33.s, ...), custom_call_target="tpu_custom_call" | custom-call | flops 8499999744 | bytes 9000000 | tf_op jit(solution)/shard_map/stage_two/pallas_call | solution.py:290
  52.9 5.0 %all-to-all-start.1 = ((bf16[16,64,1024]{2,1,0:T(8,128)(2,1)}), bf16[16,64,1024]{2,1,0:T(8,128)(2,1)S(1)}, u32[]{:S(2)}, u32[]{:S(2)}) async-start(bf16[16,64,1024]{2,1,0:T(8,128)(2,1)} %get-tuple-element.35), calls=%async_computation.1 | async-start | bytes 4194304 | tf_op jit(solution)/shard_map/all_to_all | solution.py:311
  58.0 1.9 %collective-permute-start.1 = (bf16[128,1024]{1,0:T(8,128)(2,1)}, bf16[128,1024]{1,0:T(8,128)(2,1)S(1)}, u32[]{:S(2)}, u32[]{:S(2)}) collective-permute-start(bf16[128,1024]{1,0:T(8,128)(2,1)} %get-tuple-element.43), channel_id=1, source_target_pairs={{0,32},{16,48},{32,64},{48,80},{64,96},{80,112},{96,0},{112,16},{1... | collective-permute-start | bytes 786440 | tf_op jit(solution)/shard_map/ppermute | solution.py:315
  59.9 2.2 %collective-permute-start.4 = (bf16[128,1024]{1,0:T(8,128)(2,1)}, bf16[128,1024]{1,0:T(8,128)(2,1)S(1)}, u32[]{:S(2)}, u32[]{:S(2)}) collective-permute-start(bf16[128,1024]{1,0:T(8,128)(2,1)} %get-tuple-element.47), channel_id=1, source_target_pairs={{0,96},{16,112},{32,0},{48,16},{64,32},{80,48},{96,64},{112,80},{1... | collective-permute-start | bytes 786440 | tf_op jit(solution)/shard_map/ppermute | solution.py:315
  62.1 1.9 %collective-permute-start = (bf16[128,1024]{1,0:T(8,128)(2,1)}, bf16[128,1024]{1,0:T(8,128)(2,1)S(1)}, u32[]{:S(2)}, u32[]{:S(2)}) collective-permute-start(bf16[128,1024]{1,0:T(8,128)(2,1)} %get-tuple-element.41), channel_id=1, source_target_pairs={{0,96},{16,112},{32,0},{48,16},{64,32},{80,48},{96,64},{112,80},{1... | collective-permute-start | bytes 786440 | tf_op jit(solution)/shard_map/ppermute | solution.py:315
  64.1 5.2 %collective-permute-done.1 = bf16[128,1024]{1,0:T(8,128)(2,1)S(1)} collective-permute-done((bf16[128,1024]{1,0:T(8,128)(2,1)}, bf16[128,1024]{1,0:T(8,128)(2,1)S(1)}, u32[]{:S(2)}, u32[]{:S(2)}) %collective-permute-start.1) | collective-permute-done | bytes 262176 | tf_op jit(solution)/shard_map/ppermute | solution.py:315
  69.6 3.3 %collective-permute-start.5 = (bf16[128,1024]{1,0:T(8,128)(2,1)S(1)}, bf16[128,1024]{1,0:T(8,128)(2,1)S(1)}, u32[]{:S(2)}, u32[]{:S(2)}) collective-permute-start(bf16[128,1024]{1,0:T(8,128)(2,1)S(1)} %add_convert_fusion), channel_id=1, source_target_pairs={{0,96},{16,112},{32,0},{48,16},{64,32},{80,48},{96,64},{112,80},{1... | collective-permute-start | bytes 786440 | tf_op jit(solution)/shard_map/ppermute | solution.py:315
  72.8 2.0 %collective-permute-done.f1 = bf16[128,1024]{1,0:T(8,128)(2,1)S(1)} collective-permute-done((bf16[128,1024]{1,0:T(8,128)(2,1)}, bf16[128,1024]{1,0:T(8,128)(2,1)S(1)}, u32[]{:S(2)}, u32[]{:S(2)}) %collective-permute-start) | collective-permute-done | bytes 262176 | tf_op jit(solution)/shard_map/ppermute | solution.py:315
  74.9 5.1 %collective-permute-done.2.f2 = bf16[128,1024]{1,0:T(8,128)(2,1)S(1)} collective-permute-done((bf16[128,1024]{1,0:T(8,128)(2,1)S(1)}, bf16[128,1024]{1,0:T(8,128)(2,1)S(1)}, u32[]{:S(2)}, u32[]{:S(2)}) %collective-permute-start.2) | collective-permute-done | bytes 262176 | tf_op jit(solution)/shard_map/ppermute | solution.py:315
  80.3 2.8 %collective-permute-start.6 = (bf16[256,1024]{1,0:T(8,128)(2,1)S(1)}, bf16[256,1024]{1,0:T(8,128)(2,1)S(1)}, u32[]{:S(2)}, u32[]{:S(2)}) collective-permute-start(bf16[256,1024]{1,0:T(8,128)(2,1)S(1)} %join.1.mine), channel_id=1, source_target_pairs={{0,16},{16,0},{32,48},{48,32},{64,80},{80,64},{96,112},{112,96},{1... | collective-permute-start | bytes 1572872 | tf_op jit(solution)/shard_map/ppermute | solution.py:383
  83.1 4.3 %all-to-all-done.1.r_ref = bf16[16,64,1024]{2,1,0:T(8,128)(2,1)S(1)} async-done(((bf16[16,64,1024]{2,1,0:T(8,128)(2,1)}), bf16[16,64,1024]{2,1,0:T(8,128)(2,1)S(1)}, u32[]{:S(2)}, u32[]{:S(2)}) %all-to-all-start.1) | async-done | bytes 2097184 | tf_op jit(solution)/shard_map/all_to_all | solution.py:311
  87.3 5.0 %square_grads.1.after = bf16[8,64,512]{2,1,0:T(8,128)(2,1)} custom-call(bf16[1024,512]{1,0:T(8,128)(2,1)} %tok_hbm.3, bf16[1024,512]{1,0:T(8,128)(2,1)} %cot_hbm.3, bf16[512,512]{1,0:T(8,128)(2,1)} %get-tuple-element.36.src_hbm, bf16[512,512]{1,0:T(8,128)(2,1)} %get-tuple-element.37.tgt_hbm, bf16[16,64,1024]{2,1,0:T(8,128)(2,1)S(1)} %all-to-all-done.1.r_ref), custom_call_target="tpu_custom_call" | custom-call | flops 1600000000 | bytes 5000000 | tf_op jit(solution)/shard_map/square_grads/pallas_call | solution.py:290
  92.3 7.5 %all-to-all-start.2 = ((bf16[8,64,512]{2,1,0:T(8,128)(2,1)}), bf16[8,64,512]{2,1,0:T(8,128)(2,1)S(1)}, u32[]{:S(2)}, u32[]{:S(2)}) async-start(bf16[8,64,512]{2,1,0:T(8,128)(2,1)} %square_grads.1.after), calls=%async_computation.2 | async-start | bytes 1048576 | tf_op jit(solution)/shard_map/all_to_all | solution.py:311
  100.0 3.3 %collective-permute-start.8 = (bf16[256,1024]{1,0:T(8,128)(2,1)S(1)}, bf16[256,1024]{1,0:T(8,128)(2,1)S(1)}, u32[]{:S(2)}, u32[]{:S(2)}) collective-permute-start(bf16[256,1024]{1,0:T(8,128)(2,1)S(1)} %pair.1.own), channel_id=1, source_target_pairs={{0,96},{16,112},{32,0},{48,16},{64,32},{80,48},{96,64},{112,80},{1... | collective-permute-start | bytes 1572872 | tf_op jit(solution)/shard_map/ppermute | solution.py:315
  104.8 3.5 %outputs.1 = (bf16[1024,512]{1,0:T(8,128)(2,1)}, bf16[1024,512]{1,0:T(8,128)(2,1)}) custom-call(bf16[512,512]{1,0:T(8,128)(2,1)} %get-tuple-element.31.up_hbm, bf16[512,512]{1,0:T(8,128)(2,1)} %get-tuple-element.32.down_hbm, bf16[16,64,1024]{2,1,0:T(8,128)(2,1)S(1)} %copy-done.1, bf16[8,64,512]{2,1,0:T(8,128)(2,1)} %square_grads.1.after), custom_call_target="tpu_custom_call" | custom-call | flops 1000000000 | bytes 5000000 | tf_op jit(solution)/shard_map/outputs/pallas_call | solution.py:290
  108.4 4.0 %all-to-all-done.2.t_ref = bf16[8,64,512]{2,1,0:T(8,128)(2,1)S(1)} async-done(((bf16[8,64,512]{2,1,0:T(8,128)(2,1)}), bf16[8,64,512]{2,1,0:T(8,128)(2,1)S(1)}, u32[]{:S(2)}, u32[]{:S(2)}) %all-to-all-start.2) | async-done | bytes 524320 | tf_op jit(solution)/shard_map/all_to_all | solution.py:311
  113.3 3.5 %all-to-all-start.3 = ((bf16[8,64,512]{2,1,0:T(8,128)(2,1)}), bf16[8,64,512]{2,1,0:T(8,128)(2,1)S(1)}, u32[]{:S(2)}, u32[]{:S(2)}) async-start(bf16[8,64,512]{2,1,0:T(8,128)(2,1)} %total.1), calls=%async_computation.3 | async-start | bytes 1048576 | tf_op jit(solution)/shard_map/all_to_all | solution.py:311
  116.8 3.6 %collective-permute-done.8.right = bf16[256,1024]{1,0:T(8,128)(2,1)S(1)} collective-permute-done((bf16[256,1024]{1,0:T(8,128)(2,1)S(1)}, bf16[256,1024]{1,0:T(8,128)(2,1)S(1)}, u32[]{:S(2)}, u32[]{:S(2)}) %collective-permute-start.8) | collective-permute-done | bytes 524320 | tf_op jit(solution)/shard_map/ppermute | solution.py:315
  122.2 3.2 %collective-permute-start.10 = (bf16[128,1024]{1,0:T(8,128)(2,1)S(1)}, bf16[128,1024]{1,0:T(8,128)(2,1)S(1)}, u32[]{:S(2)}, u32[]{:S(2)}) collective-permute-start(bf16[128,1024]{1,0:T(8,128)(2,1)S(1)} %get-tuple-element.49), channel_id=1, source_target_pairs={{0,96},{16,112},{32,0},{48,16},{64,32},{80,48},{96,64},{112,80},{1... | collective-permute-start | bytes 786440 | tf_op jit(solution)/shard_map/ppermute | solution.py:315
  127.2 5.7 %collective-permute-done.9.f_far = bf16[128,1024]{1,0:T(8,128)(2,1)S(1)} collective-permute-done((bf16[128,1024]{1,0:T(8,128)(2,1)S(1)}, bf16[128,1024]{1,0:T(8,128)(2,1)S(1)}, u32[]{:S(2)}, u32[]{:S(2)}) %collective-permute-start.9) | collective-permute-done | bytes 262176 | tf_op jit(solution)/shard_map/ppermute | solution.py:315
  (41 shorter events, 8.1 us)
Async XLA Ops:
  5.0 5.8 %copy-start.4 = (bf16[2,256,256]{2,1,0:T(8,128)(2,1)S(1)}, bf16[2,256,256]{2,1,0:T(8,128)(2,1)}, u32[]{:S(2)}) copy-start(bf16[2,256,256]{2,1,0:T(8,128)(2,1)} %fu_ref.1) | copy-start | bytes 786436
  5.0 5.8 %copy-start.5 = (bf16[2,256,256]{2,1,0:T(8,128)(2,1)S(1)}, bf16[2,256,256]{2,1,0:T(8,128)(2,1)}, u32[]{:S(2)}) copy-start(bf16[2,256,256]{2,1,0:T(8,128)(2,1)} %sd_ref.1) | copy-start | bytes 786436
  5.0 5.8 %copy-start.6 = (s32[8192]{0:T(1024)S(1)}, s32[8192]{0:T(1024)}, u32[]{:S(2)}) copy-start(s32[8192]{0:T(1024)} %param.13) | copy-start | bytes 98308
  5.0 5.8 %copy-start.7 = (s32[8192]{0:T(1024)S(1)}, s32[8192]{0:T(1024)}, u32[]{:S(2)}) copy-start(s32[8192]{0:T(1024)} %param.14) | copy-start | bytes 98308
  5.0 35.2 %all-to-all-start = ((bf16[16,64,1024]{2,1,0:T(8,128)(2,1)}), bf16[16,64,1024]{2,1,0:T(8,128)(2,1)S(1)}, u32[]{:S(2)}, u32[]{:S(2)}) async-start(bf16[16,64,1024]{2,1,0:T(8,128)(2,1)} %stage_one.1.mark), calls=%async_computation | async-start | bytes 4194304 | tf_op jit(solution)/shard_map/all_to_all | solution.py:311
  52.9 11.2 %copy-start.10 = (bf16[128,1024]{1,0:T(8,128)(2,1)S(1)}, bf16[128,1024]{1,0:T(8,128)(2,1)}, u32[]{:S(2)}) copy-start(bf16[128,1024]{1,0:T(8,128)(2,1)} %get-tuple-element.45) | copy-start | bytes 786436
  52.9 16.4 %copy-start.9 = (bf16[128,1024]{1,0:T(8,128)(2,1)S(1)}, bf16[128,1024]{1,0:T(8,128)(2,1)}, u32[]{:S(2)}) copy-start(bf16[128,1024]{1,0:T(8,128)(2,1)} %get-tuple-element.42) | copy-start | bytes 786436
  52.9 16.6 %copy-start.8 = (bf16[128,1024]{1,0:T(8,128)(2,1)S(1)}, bf16[128,1024]{1,0:T(8,128)(2,1)}, u32[]{:S(2)}) copy-start(bf16[128,1024]{1,0:T(8,128)(2,1)} %get-tuple-element.46) | copy-start | bytes 786436
  52.9 27.2 %copy-start.2 = (bf16[128,1024]{1,0:T(8,128)(2,1)S(1)}, bf16[128,1024]{1,0:T(8,128)(2,1)}, u32[]{:S(2)}) copy-start(bf16[128,1024]{1,0:T(8,128)(2,1)} %get-tuple-element.40.f0) | copy-start | bytes 786436
  52.9 27.2 %copy-start.3 = (bf16[128,1024]{1,0:T(8,128)(2,1)S(1)}, bf16[128,1024]{1,0:T(8,128)(2,1)}, u32[]{:S(2)}) copy-start(bf16[128,1024]{1,0:T(8,128)(2,1)} %get-tuple-element.44.s0) | copy-start | bytes 786436
  52.9 34.4 %all-to-all-start.1 = ((bf16[16,64,1024]{2,1,0:T(8,128)(2,1)}), bf16[16,64,1024]{2,1,0:T(8,128)(2,1)S(1)}, u32[]{:S(2)}, u32[]{:S(2)}) async-start(bf16[16,64,1024]{2,1,0:T(8,128)(2,1)} %get-tuple-element.35), calls=%async_computation.1 | async-start | bytes 4194304 | tf_op jit(solution)/shard_map/all_to_all | solution.py:311
  58.0 11.3 %collective-permute-start.1 = (bf16[128,1024]{1,0:T(8,128)(2,1)}, bf16[128,1024]{1,0:T(8,128)(2,1)S(1)}, u32[]{:S(2)}, u32[]{:S(2)}) collective-permute-start(bf16[128,1024]{1,0:T(8,128)(2,1)} %get-tuple-element.43), channel_id=1, source_target_pairs={{0,32},{16,48},{32,64},{48,80},{64,96},{80,112},{96,0},{112,16},{1... | collective-permute-start | bytes 786440 | tf_op jit(solution)/shard_map/ppermute | solution.py:315
  59.9 9.6 %collective-permute-start.4 = (bf16[128,1024]{1,0:T(8,128)(2,1)}, bf16[128,1024]{1,0:T(8,128)(2,1)S(1)}, u32[]{:S(2)}, u32[]{:S(2)}) collective-permute-start(bf16[128,1024]{1,0:T(8,128)(2,1)} %get-tuple-element.47), channel_id=1, source_target_pairs={{0,96},{16,112},{32,0},{48,16},{64,32},{80,48},{96,64},{112,80},{1... | collective-permute-start | bytes 786440 | tf_op jit(solution)/shard_map/ppermute | solution.py:315
  62.1 12.8 %collective-permute-start = (bf16[128,1024]{1,0:T(8,128)(2,1)}, bf16[128,1024]{1,0:T(8,128)(2,1)S(1)}, u32[]{:S(2)}, u32[]{:S(2)}) collective-permute-start(bf16[128,1024]{1,0:T(8,128)(2,1)} %get-tuple-element.41), channel_id=1, source_target_pairs={{0,96},{16,112},{32,0},{48,16},{64,32},{80,48},{96,64},{112,80},{1... | collective-permute-start | bytes 786440 | tf_op jit(solution)/shard_map/ppermute | solution.py:315
  64.0 10.9 %collective-permute-start.3 = (bf16[128,1024]{1,0:T(8,128)(2,1)S(1)}, bf16[128,1024]{1,0:T(8,128)(2,1)S(1)}, u32[]{:S(2)}, u32[]{:S(2)}) collective-permute-start(bf16[128,1024]{1,0:T(8,128)(2,1)S(1)} %copy-done.10), channel_id=1, source_target_pairs={{0,32},{16,48},{32,64},{48,80},{64,96},{80,112},{96,0},{112,16},{1... | collective-permute-start | bytes 786440 | tf_op jit(solution)/shard_map/ppermute | solution.py:315
  69.4 10.7 %collective-permute-start.2 = (bf16[128,1024]{1,0:T(8,128)(2,1)S(1)}, bf16[128,1024]{1,0:T(8,128)(2,1)S(1)}, u32[]{:S(2)}, u32[]{:S(2)}) collective-permute-start(bf16[128,1024]{1,0:T(8,128)(2,1)S(1)} %add_convert_fusion.1), channel_id=1, source_target_pairs={{0,32},{16,48},{32,64},{48,80},{64,96},{80,112},{96,0},{112,16},{1... | collective-permute-start | bytes 786440 | tf_op jit(solution)/shard_map/ppermute | solution.py:315
  69.6 10.5 %collective-permute-start.5 = (bf16[128,1024]{1,0:T(8,128)(2,1)S(1)}, bf16[128,1024]{1,0:T(8,128)(2,1)S(1)}, u32[]{:S(2)}, u32[]{:S(2)}) collective-permute-start(bf16[128,1024]{1,0:T(8,128)(2,1)S(1)} %add_convert_fusion), channel_id=1, source_target_pairs={{0,96},{16,112},{32,0},{48,16},{64,32},{80,48},{96,64},{112,80},{1... | collective-permute-start | bytes 786440 | tf_op jit(solution)/shard_map/ppermute | solution.py:315
  80.3 19.5 %collective-permute-start.6 = (bf16[256,1024]{1,0:T(8,128)(2,1)S(1)}, bf16[256,1024]{1,0:T(8,128)(2,1)S(1)}, u32[]{:S(2)}, u32[]{:S(2)}) collective-permute-start(bf16[256,1024]{1,0:T(8,128)(2,1)S(1)} %join.1.mine), channel_id=1, source_target_pairs={{0,16},{16,0},{32,48},{48,32},{64,80},{80,64},{96,112},{112,96},{1... | collective-permute-start | bytes 1572872 | tf_op jit(solution)/shard_map/ppermute | solution.py:383
  92.3 20.1 %all-to-all-start.2 = ((bf16[8,64,512]{2,1,0:T(8,128)(2,1)}), bf16[8,64,512]{2,1,0:T(8,128)(2,1)S(1)}, u32[]{:S(2)}, u32[]{:S(2)}) async-start(bf16[8,64,512]{2,1,0:T(8,128)(2,1)} %square_grads.1.after), calls=%async_computation.2 | async-start | bytes 1048576 | tf_op jit(solution)/shard_map/all_to_all | solution.py:311
  100.0 20.4 %collective-permute-start.8 = (bf16[256,1024]{1,0:T(8,128)(2,1)S(1)}, bf16[256,1024]{1,0:T(8,128)(2,1)S(1)}, u32[]{:S(2)}, u32[]{:S(2)}) collective-permute-start(bf16[256,1024]{1,0:T(8,128)(2,1)S(1)} %pair.1.own), channel_id=1, source_target_pairs={{0,96},{16,112},{32,0},{48,16},{64,32},{80,48},{96,64},{112,80},{1... | collective-permute-start | bytes 1572872 | tf_op jit(solution)/shard_map/ppermute | solution.py:315
  103.2 18.8 %collective-permute-start.7 = (bf16[256,1024]{1,0:T(8,128)(2,1)S(1)}, bf16[256,1024]{1,0:T(8,128)(2,1)S(1)}, u32[]{:S(2)}, u32[]{:S(2)}) collective-permute-start(bf16[256,1024]{1,0:T(8,128)(2,1)S(1)} %pair.1.own), channel_id=1, source_target_pairs={{0,32},{16,48},{32,64},{48,80},{64,96},{80,112},{96,0},{112,16},{1... | collective-permute-start | bytes 1572872 | tf_op jit(solution)/shard_map/ppermute | solution.py:315
  113.3 19.6 %all-to-all-start.3 = ((bf16[8,64,512]{2,1,0:T(8,128)(2,1)}), bf16[8,64,512]{2,1,0:T(8,128)(2,1)S(1)}, u32[]{:S(2)}, u32[]{:S(2)}) async-start(bf16[8,64,512]{2,1,0:T(8,128)(2,1)} %total.1), calls=%async_computation.3 | async-start | bytes 1048576 | tf_op jit(solution)/shard_map/all_to_all | solution.py:311
  122.1 10.7 %collective-permute-start.9 = (bf16[128,1024]{1,0:T(8,128)(2,1)S(1)}, bf16[128,1024]{1,0:T(8,128)(2,1)S(1)}, u32[]{:S(2)}, u32[]{:S(2)}) collective-permute-start(bf16[128,1024]{1,0:T(8,128)(2,1)S(1)} %get-tuple-element.48), channel_id=1, source_target_pairs={{0,32},{16,48},{32,64},{48,80},{64,96},{80,112},{96,0},{112,16},{1... | collective-permute-start | bytes 786440 | tf_op jit(solution)/shard_map/ppermute | solution.py:315
  122.2 10.7 %collective-permute-start.10 = (bf16[128,1024]{1,0:T(8,128)(2,1)S(1)}, bf16[128,1024]{1,0:T(8,128)(2,1)S(1)}, u32[]{:S(2)}, u32[]{:S(2)}) collective-permute-start(bf16[128,1024]{1,0:T(8,128)(2,1)S(1)} %get-tuple-element.49), channel_id=1, source_target_pairs={{0,96},{16,112},{32,0},{48,16},{64,32},{80,48},{96,64},{112,80},{1... | collective-permute-start | bytes 786440 | tf_op jit(solution)/shard_map/ppermute | solution.py:315
  (2 other events, 6.6 us)

commit v5 on v4

--- a/solution.py
+++ b/solution.py
@@ -89,26 +89,25 @@
 def stage_one(
     tok_hbm, cot_hbm, fu_hbm, sd_hbm, pu_hbm, pd_hbm, out_hbm, tok, cot, fu, sd, pu, pd, matrix, weight, out, sems, out_sems
 ):
-    pairs = ((pu_hbm, pu), (fu_hbm, fu), (tok_hbm, tok), (pd_hbm, pd), (sd_hbm, sd), (cot_hbm, cot))
-    copies = start(pairs, sems)
+    copies = start(((pu_hbm, pu), (pd_hbm, pd), (fu_hbm, fu), (sd_hbm, sd), (tok_hbm, tok), (cot_hbm, cot)), sems)
     me = lax.axis_index("chan")
     copies[0].wait()
+    copies[1].wait()
+    copies[2].wait()
+    copies[3].wait()
     source_matrix(pu, me, matrix.at[0])
-    copies[1].wait()
+    target_matrix(pd, me, matrix.at[1])
     fold_up(matrix.at[0], fu, weight.at[0])
-    copies[3].wait()
-    target_matrix(pd, me, matrix.at[1])
-    copies[4].wait()
     fold_down(matrix.at[1], sd, weight.at[1])
     sent = []
-    for i, (wait, rows) in enumerate(((copies[2], tok), (copies[5], cot))):
-        wait.wait()
-        for j in range(2):
-            groups = slice(8 * j, 8 * j + 8)
-            part = nt(weight[i, 256 * j : 256 * j + 256, :], rows[...]).astype(BF)
-            out[groups, 32 * i : 32 * i + 32, :] = part.reshape(8, 32, 1024)
-            at = (groups, slice(32 * i, 32 * i + 32))
-            sent.append(send(out.at[at], out_hbm.at[at], out_sems.at[2 * i + j]))
+    copies[4].wait()
+    copies[5].wait()
+    for n, (i, groups) in enumerate(((0, slice(0, 16)), (1, slice(0, 8)), (1, slice(8, 16)))):
+        slots = slice(32 * groups.start, 32 * groups.stop)
+        part = nt(weight[i, slots, :], (tok, cot)[i][...]).astype(BF)
+        out[groups, 32 * i : 32 * i + 32, :] = part.reshape(-1, 32, 1024)
+        at = (groups, slice(32 * i, 32 * i + 32))
+        sent.append(send(out.at[at], out_hbm.at[at], out_sems.at[n]))
     for copy in sent:
         copy.wait()
 
@@ -135,32 +134,40 @@
     copies[2].wait()
     z = lax.shift_right_logical(lax.axis_index("dp"), 1)
     sent = []
-    for k in range(2):
-        mi = mixed_in[256 * k : 256 * k + 256, :]
-        ng = nar_grad[256 * k : 256 * k + 256, :]
-        for c in range(2):
-            units = slice(512 * c, 512 * c + 512)
-            v = tn(su[k, :, units], mi)
-            up = nn(fd[k, units, :], ng)
-            sq = v * v
-            h = 0.5 + 0.5 * jnp.tanh(v * (GELU_C + (GELU_C * GELU_A) * sq))
-            a = (v * h).astype(BF)
-            d = v * ((2 * GELU_C) + (6 * GELU_C * GELU_A) * sq)
-            b = (up * (h * (1.0 + (1.0 - h) * d))).astype(BF)
-            act[k, units, :] = a
-            hg[k, units, :] = b
-            gsu = nt(mi, b).astype(BF)
-            gfd = nt(a, ng).astype(BF)
-            for i in range(2):
-                psu[2 * k + i, :, units] = gsu[128 * i : 128 * i + 128, :]
-            for i in range(4):
-                pfd[2 * k + c, :, 256 * i : 256 * i + 256] = gfd[128 * i : 128 * i + 128, :]
-        if k == 1:
-            for i, (f, s) in enumerate(((f0, s0), (f1, s1), (f2, s2), (f3, s3))):
-                sent.append(send(pfd.at[(z + i) & 3], f, out_sems.at[i]))
-                sent.append(send(psu.at[(z + i) & 3], s, out_sems.at[4 + i]))
-        nar[256 * k : 256 * k + 256, :] = tn(fd[k], act[k]).astype(BF)
-        mix[256 * k : 256 * k + 256, :] = nn(su[k], hg[k]).astype(BF)
+    size = 512
+    steps = [(k, slice(size * c, size * c + size)) for k in range(2) for c in range(1024 // size)]
+
+    def products(k, units):
+        rows = slice(256 * k, 256 * k + 256)
+        return tn(su[k, :, units], mixed_in[rows, :]), nn(fd[k, units, :], nar_grad[rows, :])
+
+    ready = products(*steps[0])
+    for n, (k, units) in enumerate(steps):
+        v, up = ready
+        if n + 1 < len(steps):
+            ready = products(*steps[n + 1])
+        sq = v * v
+        h = 0.5 + 0.5 * jnp.tanh(v * (GELU_C + (GELU_C * GELU_A) * sq))
+        a = (v * h).astype(BF)
+        d = v * ((2 * GELU_C) + (6 * GELU_C * GELU_A) * sq)
+        b = (up * (h * (1.0 + (1.0 - h) * d))).astype(BF)
+        act[k, units, :] = a
+        hg[k, units, :] = b
+        gsu = nt(mixed_in[256 * k : 256 * k + 256, :], b).astype(BF)
+        gfd = nt(a, nar_grad[256 * k : 256 * k + 256, :]).astype(BF)
+        for i in range(2):
+            psu[2 * k + i, :, units] = gsu[128 * i : 128 * i + 128, :]
+        for i in range(size // 128):
+            at = units.start + 128 * i
+            lanes = slice(256 * ((at % 512) // 128), 256 * ((at % 512) // 128) + 256)
+            pfd[2 * k + at // 512, :, lanes] = gfd[128 * i : 128 * i + 128, :]
+        if units.stop == 1024:
+            if k == 1:
+                for i, (f, s) in enumerate(((f0, s0), (f1, s1), (f2, s2), (f3, s3))):
+                    sent.append(send(pfd.at[(z + i) & 3], f, out_sems.at[i]))
+                    sent.append(send(psu.at[(z + i) & 3], s, out_sems.at[4 + i]))
+            nar[256 * k : 256 * k + 256, :] = tn(fd[k], act[k]).astype(BF)
+            mix[256 * k : 256 * k + 256, :] = nn(su[k], hg[k]).astype(BF)
     for i, (matrix, rows) in enumerate(((down_src, nar), (up_tgt, mix))):
         for j in range(4):
             groups = slice(4 * j, 4 * j + 4)
@@ -175,24 +182,12 @@
 def square_grads(
     tok_hbm, cot_hbm, src_hbm, tgt_hbm, r_ref, t_hbm, tok, cot, up_src, down_tgt, t, sems, out_sems
 ):
-    top, low = slice(0, 512), slice(512, 1024)
-    pairs = (
-        (cot_hbm.at[top], cot.at[top]),
-        (cot_hbm.at[low], cot.at[low]),
-        (tgt_hbm, down_tgt),
-        (tok_hbm.at[top], tok.at[top]),
-        (tok_hbm.at[low], tok.at[low]),
-        (src_hbm, up_src),
-    )
-    copies = start(pairs, sems)
+    copies = start(((cot_hbm, cot), (tgt_hbm, down_tgt), (tok_hbm, tok), (src_hbm, up_src)), sems)
     sent = []
     for n, rows in enumerate((cot, tok)):
-        slots = r_ref[:, 32 * n : 32 * n + 32, :].reshape(512, 1024)
-        copies[3 * n].wait()
-        sums = nn(slots[:, top], rows[top, :])
-        copies[3 * n + 1].wait()
-        sums = (sums + nn(slots[:, low], rows[low, :])).astype(BF)
-        copies[3 * n + 2].wait()
+        copies[2 * n].wait()
+        copies[2 * n + 1].wait()
+        sums = nn(r_ref[:, 32 * n : 32 * n + 32, :].reshape(512, 1024), rows[...]).astype(BF)
         for k in range(2):
             cols = slice(256 * k, 256 * k + 256)
             grad = tn(down_tgt[:, cols], sums[:, cols]) if n == 0 else tn(sums[:, cols], up_src[:, cols])

time: 135 us -> 134 us (level)
  transfers between devices with their start and end apart: 15 -> 15, of which waited for: 9 -> 10; matrix products, arithmetic and copies ran while one was open for 0% -> 0% of each run, Pallas kernels for 10% -> 10%
where the time goes in v5:
time: 134 us
  waiting for transfers between devices  58.9 us (44%)
  starting transfers between devices  40.8 us (30%)
  Pallas kernels  31.5 us (24%)
  local copies, waits for them, and re-layouts  1.64 us (1%)
    all_to_all x4, waiting for transfers between devices, exchange(): return lax.all_to_all(values, axis, split_axis=0, concat_axis=0, tiled=True)  35.4 us
    pallas_call x11, Pallas kernels, run(): pl.pallas_call(kernel, out_shape=out_shape, in_specs=placed(pltpu.HBM, hb...  31.5 us
    ppermute x10, waiting for transfers between devices, shifted(): return lax.ppermute(part, 'dp', shift_z(step))  23.4 us
    all_to_all x4, starting transfers between devices, exchange(): return lax.all_to_all(values, axis, split_axis=0, concat_axis=0, tiled=True)  21.8 us
    ppermute x10, starting transfers between devices, shifted(): return lax.ppermute(part, 'dp', shift_z(step))  16.1 us
    ppermute x1, starting transfers between devices, per_device(): other = lax.ppermute(part, 'dp', SWAP_X)  2.81 us
  transfers between devices with their start and end apart: 15, of which 10 were waited for; matrix products, arithmetic and copies ran while one was open for 0% of the time, Pallas kernels for 10%

profile of v5, /device:TPU:24, one launch (start us, length us, event | category | flops | bytes accessed | tf_op | source)
XLA Modules:
  0.0 133.9 jit_solution(13681627998884149650)
XLA Ops:
  0.6 3.9 %stage_one.1.mark = bf16[16,64,1024]{2,1,0:T(8,128)(2,1)} custom-call(bf16[1024,512]{1,0:T(8,128)(2,1)} %tok_hbm.3, bf16[1024,512]{1,0:T(8,128)(2,1)} %cot_hbm.3, bf16[2,256,256]{2,1,0:T(8,128)(2,1)} %fu_ref.1, bf16[2,256,256]{2,1,0:T(8,128)(2,1)} %sd_ref.1, s32[64,128]{1,0:T(8,128)} %bitcast.2, s32[64,128]{1,0:T(8,128)} %bitcast.4), custom_call_target="tpu_custom_call" | custom-call | flops 2000000000 | bytes 5000000 | tf_op jit(solution)/shard_map/stage_one/pallas_call | solution.py:285
  4.6 5.8 %all-to-all-start = ((bf16[16,64,1024]{2,1,0:T(8,128)(2,1)}), bf16[16,64,1024]{2,1,0:T(8,128)(2,1)S(1)}, u32[]{:S(2)}, u32[]{:S(2)}) async-start(bf16[16,64,1024]{2,1,0:T(8,128)(2,1)} %stage_one.1.mark), calls=%async_computation | async-start | bytes 4194304 | tf_op jit(solution)/shard_map/all_to_all | solution.py:306
  10.5 2.1 %prepare.1 = (bf16[512,512]{1,0:T(8,128)(2,1)}, bf16[512,512]{1,0:T(8,128)(2,1)S(1)}, bf16[512,512]{1,0:T(8,128)(2,1)}, bf16[512,512]{1,0:T(8,128)(2,1)}, bf16[5...) custom-call(bf16[2,256,256]{2,1,0:T(8,128)(2,1)S(1)} %copy-done.4, bf16[2,256,256]{2,1,0:T(8,128)(2,1)S(1)} %copy-done.5, ...), custom_call_target="tpu_custom_call" | custom-call | flops 2000000000 | bytes 4000000 | tf_op jit(solution)/shard_map/prepare/pallas_call | solution.py:285
  12.5 27.3 %all-to-all-done.r_ref = bf16[16,64,1024]{2,1,0:T(8,128)(2,1)S(1)} async-done(((bf16[16,64,1024]{2,1,0:T(8,128)(2,1)}), bf16[16,64,1024]{2,1,0:T(8,128)(2,1)S(1)}, u32[]{:S(2)}, u32[]{:S(2)}) %all-to-all-start) | async-done | bytes 2097184 | tf_op jit(solution)/shard_map/all_to_all | solution.py:306
  39.8 12.8 %stage_two.1 = (bf16[16,64,1024]{2,1,0:T(8,128)(2,1)}, bf16[128,1024]{1,0:T(8,128)(2,1)}, bf16[128,1024]{1,0:T(8,128)(2,1)}, bf16[128,1024]{1,0:T(8,128)(2,1)}, ...) custom-call(bf16[512,512]{1,0:T(8,128)(2,1)} %get-tuple-element.33.s, ...), custom_call_target="tpu_custom_call" | custom-call | flops 8499999744 | bytes 9000000 | tf_op jit(solution)/shard_map/stage_two/pallas_call | solution.py:285
  52.6 5.0 %all-to-all-start.1 = ((bf16[16,64,1024]{2,1,0:T(8,128)(2,1)}), bf16[16,64,1024]{2,1,0:T(8,128)(2,1)S(1)}, u32[]{:S(2)}, u32[]{:S(2)}) async-start(bf16[16,64,1024]{2,1,0:T(8,128)(2,1)} %get-tuple-element.35), calls=%async_computation.1 | async-start | bytes 4194304 | tf_op jit(solution)/shard_map/all_to_all | solution.py:306
  57.7 1.9 %collective-permute-start.1 = (bf16[128,1024]{1,0:T(8,128)(2,1)}, bf16[128,1024]{1,0:T(8,128)(2,1)S(1)}, u32[]{:S(2)}, u32[]{:S(2)}) collective-permute-start(bf16[128,1024]{1,0:T(8,128)(2,1)} %get-tuple-element.43), channel_id=1, source_target_pairs={{0,32},{16,48},{32,64},{48,80},{64,96},{80,112},{96,0},{112,16},{1... | collective-permute-start | bytes 786440 | tf_op jit(solution)/shard_map/ppermute | solution.py:310
  59.6 2.3 %collective-permute-start.4 = (bf16[128,1024]{1,0:T(8,128)(2,1)}, bf16[128,1024]{1,0:T(8,128)(2,1)S(1)}, u32[]{:S(2)}, u32[]{:S(2)}) collective-permute-start(bf16[128,1024]{1,0:T(8,128)(2,1)} %get-tuple-element.47), channel_id=1, source_target_pairs={{0,96},{16,112},{32,0},{48,16},{64,32},{80,48},{96,64},{112,80},{1... | collective-permute-start | bytes 786440 | tf_op jit(solution)/shard_map/ppermute | solution.py:310
  61.8 1.9 %collective-permute-start = (bf16[128,1024]{1,0:T(8,128)(2,1)}, bf16[128,1024]{1,0:T(8,128)(2,1)S(1)}, u32[]{:S(2)}, u32[]{:S(2)}) collective-permute-start(bf16[128,1024]{1,0:T(8,128)(2,1)} %get-tuple-element.41), channel_id=1, source_target_pairs={{0,96},{16,112},{32,0},{48,16},{64,32},{80,48},{96,64},{112,80},{1... | collective-permute-start | bytes 786440 | tf_op jit(solution)/shard_map/ppermute | solution.py:310
  63.9 5.2 %collective-permute-done.1 = bf16[128,1024]{1,0:T(8,128)(2,1)S(1)} collective-permute-done((bf16[128,1024]{1,0:T(8,128)(2,1)}, bf16[128,1024]{1,0:T(8,128)(2,1)S(1)}, u32[]{:S(2)}, u32[]{:S(2)}) %collective-permute-start.1) | collective-permute-done | bytes 262176 | tf_op jit(solution)/shard_map/ppermute | solution.py:310
  69.3 3.3 %collective-permute-start.5 = (bf16[128,1024]{1,0:T(8,128)(2,1)S(1)}, bf16[128,1024]{1,0:T(8,128)(2,1)S(1)}, u32[]{:S(2)}, u32[]{:S(2)}) collective-permute-start(bf16[128,1024]{1,0:T(8,128)(2,1)S(1)} %add_convert_fusion), channel_id=1, source_target_pairs={{0,96},{16,112},{32,0},{48,16},{64,32},{80,48},{96,64},{112,80},{1... | collective-permute-start | bytes 786440 | tf_op jit(solution)/shard_map/ppermute | solution.py:310
  72.6 2.0 %collective-permute-done.f1 = bf16[128,1024]{1,0:T(8,128)(2,1)S(1)} collective-permute-done((bf16[128,1024]{1,0:T(8,128)(2,1)}, bf16[128,1024]{1,0:T(8,128)(2,1)S(1)}, u32[]{:S(2)}, u32[]{:S(2)}) %collective-permute-start) | collective-permute-done | bytes 262176 | tf_op jit(solution)/shard_map/ppermute | solution.py:310
  74.7 5.1 %collective-permute-done.2.f2 = bf16[128,1024]{1,0:T(8,128)(2,1)S(1)} collective-permute-done((bf16[128,1024]{1,0:T(8,128)(2,1)S(1)}, bf16[128,1024]{1,0:T(8,128)(2,1)S(1)}, u32[]{:S(2)}, u32[]{:S(2)}) %collective-permute-start.2) | collective-permute-done | bytes 262176 | tf_op jit(solution)/shard_map/ppermute | solution.py:310
  80.0 2.8 %collective-permute-start.6 = (bf16[256,1024]{1,0:T(8,128)(2,1)S(1)}, bf16[256,1024]{1,0:T(8,128)(2,1)S(1)}, u32[]{:S(2)}, u32[]{:S(2)}) collective-permute-start(bf16[256,1024]{1,0:T(8,128)(2,1)S(1)} %join.1.mine), channel_id=1, source_target_pairs={{0,16},{16,0},{32,48},{48,32},{64,80},{80,64},{96,112},{112,96},{1... | collective-permute-start | bytes 1572872 | tf_op jit(solution)/shard_map/ppermute | solution.py:378
  82.9 4.2 %all-to-all-done.1.r_ref = bf16[16,64,1024]{2,1,0:T(8,128)(2,1)S(1)} async-done(((bf16[16,64,1024]{2,1,0:T(8,128)(2,1)}), bf16[16,64,1024]{2,1,0:T(8,128)(2,1)S(1)}, u32[]{:S(2)}, u32[]{:S(2)}) %all-to-all-start.1) | async-done | bytes 2097184 | tf_op jit(solution)/shard_map/all_to_all | solution.py:306
  87.1 4.8 %square_grads.1.after = bf16[8,64,512]{2,1,0:T(8,128)(2,1)} custom-call(bf16[1024,512]{1,0:T(8,128)(2,1)} %tok_hbm.3, bf16[1024,512]{1,0:T(8,128)(2,1)} %cot_hbm.3, bf16[512,512]{1,0:T(8,128)(2,1)} %get-tuple-element.36.src_hbm, bf16[512,512]{1,0:T(8,128)(2,1)} %get-tuple-element.37.tgt_hbm, bf16[16,64,1024]{2,1,0:T(8,128)(2,1)S(1)} %all-to-all-done.1.r_ref), custom_call_target="tpu_custom_call" | custom-call | flops 1600000000 | bytes 5000000 | tf_op jit(solution)/shard_map/square_grads/pallas_call | solution.py:285
  91.9 7.5 %all-to-all-start.2 = ((bf16[8,64,512]{2,1,0:T(8,128)(2,1)}), bf16[8,64,512]{2,1,0:T(8,128)(2,1)S(1)}, u32[]{:S(2)}, u32[]{:S(2)}) async-start(bf16[8,64,512]{2,1,0:T(8,128)(2,1)} %square_grads.1.after), calls=%async_computation.2 | async-start | bytes 1048576 | tf_op jit(solution)/shard_map/all_to_all | solution.py:306
  99.5 3.3 %collective-permute-start.8 = (bf16[256,1024]{1,0:T(8,128)(2,1)S(1)}, bf16[256,1024]{1,0:T(8,128)(2,1)S(1)}, u32[]{:S(2)}, u32[]{:S(2)}) collective-permute-start(bf16[256,1024]{1,0:T(8,128)(2,1)S(1)} %pair.1.own), channel_id=1, source_target_pairs={{0,96},{16,112},{32,0},{48,16},{64,32},{80,48},{96,64},{112,80},{1... | collective-permute-start | bytes 1572872 | tf_op jit(solution)/shard_map/ppermute | solution.py:310
  104.4 3.5 %outputs.1 = (bf16[1024,512]{1,0:T(8,128)(2,1)}, bf16[1024,512]{1,0:T(8,128)(2,1)}) custom-call(bf16[512,512]{1,0:T(8,128)(2,1)} %get-tuple-element.31.up_hbm, bf16[512,512]{1,0:T(8,128)(2,1)} %get-tuple-element.32.down_hbm, bf16[16,64,1024]{2,1,0:T(8,128)(2,1)S(1)} %copy-done.1, bf16[8,64,512]{2,1,0:T(8,128)(2,1)} %square_grads.1.after), custom_call_target="tpu_custom_call" | custom-call | flops 1000000000 | bytes 5000000 | tf_op jit(solution)/shard_map/outputs/pallas_call | solution.py:285
  107.9 4.0 %all-to-all-done.2.t_ref = bf16[8,64,512]{2,1,0:T(8,128)(2,1)S(1)} async-done(((bf16[8,64,512]{2,1,0:T(8,128)(2,1)}), bf16[8,64,512]{2,1,0:T(8,128)(2,1)S(1)}, u32[]{:S(2)}, u32[]{:S(2)}) %all-to-all-start.2) | async-done | bytes 524320 | tf_op jit(solution)/shard_map/all_to_all | solution.py:306
  112.8 3.5 %all-to-all-start.3 = ((bf16[8,64,512]{2,1,0:T(8,128)(2,1)}), bf16[8,64,512]{2,1,0:T(8,128)(2,1)S(1)}, u32[]{:S(2)}, u32[]{:S(2)}) async-start(bf16[8,64,512]{2,1,0:T(8,128)(2,1)} %total.1), calls=%async_computation.3 | async-start | bytes 1048576 | tf_op jit(solution)/shard_map/all_to_all | solution.py:306
  116.3 3.6 %collective-permute-done.8.right = bf16[256,1024]{1,0:T(8,128)(2,1)S(1)} collective-permute-done((bf16[256,1024]{1,0:T(8,128)(2,1)S(1)}, bf16[256,1024]{1,0:T(8,128)(2,1)S(1)}, u32[]{:S(2)}, u32[]{:S(2)}) %collective-permute-start.8) | collective-permute-done | bytes 524320 | tf_op jit(solution)/shard_map/ppermute | solution.py:310
  121.7 3.2 %collective-permute-start.10 = (bf16[128,1024]{1,0:T(8,128)(2,1)S(1)}, bf16[128,1024]{1,0:T(8,128)(2,1)S(1)}, u32[]{:S(2)}, u32[]{:S(2)}) collective-permute-start(bf16[128,1024]{1,0:T(8,128)(2,1)S(1)} %get-tuple-element.49), channel_id=1, source_target_pairs={{0,96},{16,112},{32,0},{48,16},{64,32},{80,48},{96,64},{112,80},{1... | collective-permute-start | bytes 786440 | tf_op jit(solution)/shard_map/ppermute | solution.py:310
  126.7 5.7 %collective-permute-done.9.f_far = bf16[128,1024]{1,0:T(8,128)(2,1)S(1)} collective-permute-done((bf16[128,1024]{1,0:T(8,128)(2,1)S(1)}, bf16[128,1024]{1,0:T(8,128)(2,1)S(1)}, u32[]{:S(2)}, u32[]{:S(2)}) %collective-permute-start.9) | collective-permute-done | bytes 262176 | tf_op jit(solution)/shard_map/ppermute | solution.py:310
  (41 shorter events, 8.2 us)
Async XLA Ops:
  4.6 5.8 %copy-start.4 = (bf16[2,256,256]{2,1,0:T(8,128)(2,1)S(1)}, bf16[2,256,256]{2,1,0:T(8,128)(2,1)}, u32[]{:S(2)}) copy-start(bf16[2,256,256]{2,1,0:T(8,128)(2,1)} %fu_ref.1) | copy-start | bytes 786436
  4.6 5.8 %copy-start.5 = (bf16[2,256,256]{2,1,0:T(8,128)(2,1)S(1)}, bf16[2,256,256]{2,1,0:T(8,128)(2,1)}, u32[]{:S(2)}) copy-start(bf16[2,256,256]{2,1,0:T(8,128)(2,1)} %sd_ref.1) | copy-start | bytes 786436
  4.6 5.8 %copy-start.6 = (s32[8192]{0:T(1024)S(1)}, s32[8192]{0:T(1024)}, u32[]{:S(2)}) copy-start(s32[8192]{0:T(1024)} %param.13) | copy-start | bytes 98308
  4.6 5.8 %copy-start.7 = (s32[8192]{0:T(1024)S(1)}, s32[8192]{0:T(1024)}, u32[]{:S(2)}) copy-start(s32[8192]{0:T(1024)} %param.14) | copy-start | bytes 98308
  4.6 35.2 %all-to-all-start = ((bf16[16,64,1024]{2,1,0:T(8,128)(2,1)}), bf16[16,64,1024]{2,1,0:T(8,128)(2,1)S(1)}, u32[]{:S(2)}, u32[]{:S(2)}) async-start(bf16[16,64,1024]{2,1,0:T(8,128)(2,1)} %stage_one.1.mark), calls=%async_computation | async-start | bytes 4194304 | tf_op jit(solution)/shard_map/all_to_all | solution.py:306
  52.6 11.2 %copy-start.10 = (bf16[128,1024]{1,0:T(8,128)(2,1)S(1)}, bf16[128,1024]{1,0:T(8,128)(2,1)}, u32[]{:S(2)}) copy-start(bf16[128,1024]{1,0:T(8,128)(2,1)} %get-tuple-element.45) | copy-start | bytes 786436
  52.6 16.5 %copy-start.9 = (bf16[128,1024]{1,0:T(8,128)(2,1)S(1)}, bf16[128,1024]{1,0:T(8,128)(2,1)}, u32[]{:S(2)}) copy-start(bf16[128,1024]{1,0:T(8,128)(2,1)} %get-tuple-element.42) | copy-start | bytes 786436
  52.6 16.6 %copy-start.8 = (bf16[128,1024]{1,0:T(8,128)(2,1)S(1)}, bf16[128,1024]{1,0:T(8,128)(2,1)}, u32[]{:S(2)}) copy-start(bf16[128,1024]{1,0:T(8,128)(2,1)} %get-tuple-element.46) | copy-start | bytes 786436
  52.6 27.2 %copy-start.2 = (bf16[128,1024]{1,0:T(8,128)(2,1)S(1)}, bf16[128,1024]{1,0:T(8,128)(2,1)}, u32[]{:S(2)}) copy-start(bf16[128,1024]{1,0:T(8,128)(2,1)} %get-tuple-element.40.f0) | copy-start | bytes 786436
  52.6 27.2 %copy-start.3 = (bf16[128,1024]{1,0:T(8,128)(2,1)S(1)}, bf16[128,1024]{1,0:T(8,128)(2,1)}, u32[]{:S(2)}) copy-start(bf16[128,1024]{1,0:T(8,128)(2,1)} %get-tuple-element.44.s0) | copy-start | bytes 786436
  52.6 34.4 %all-to-all-start.1 = ((bf16[16,64,1024]{2,1,0:T(8,128)(2,1)}), bf16[16,64,1024]{2,1,0:T(8,128)(2,1)S(1)}, u32[]{:S(2)}, u32[]{:S(2)}) async-start(bf16[16,64,1024]{2,1,0:T(8,128)(2,1)} %get-tuple-element.35), calls=%async_computation.1 | async-start | bytes 4194304 | tf_op jit(solution)/shard_map/all_to_all | solution.py:306
  57.7 11.4 %collective-permute-start.1 = (bf16[128,1024]{1,0:T(8,128)(2,1)}, bf16[128,1024]{1,0:T(8,128)(2,1)S(1)}, u32[]{:S(2)}, u32[]{:S(2)}) collective-permute-start(bf16[128,1024]{1,0:T(8,128)(2,1)} %get-tuple-element.43), channel_id=1, source_target_pairs={{0,32},{16,48},{32,64},{48,80},{64,96},{80,112},{96,0},{112,16},{1... | collective-permute-start | bytes 786440 | tf_op jit(solution)/shard_map/ppermute | solution.py:310
  59.6 9.6 %collective-permute-start.4 = (bf16[128,1024]{1,0:T(8,128)(2,1)}, bf16[128,1024]{1,0:T(8,128)(2,1)S(1)}, u32[]{:S(2)}, u32[]{:S(2)}) collective-permute-start(bf16[128,1024]{1,0:T(8,128)(2,1)} %get-tuple-element.47), channel_id=1, source_target_pairs={{0,96},{16,112},{32,0},{48,16},{64,32},{80,48},{96,64},{112,80},{1... | collective-permute-start | bytes 786440 | tf_op jit(solution)/shard_map/ppermute | solution.py:310
  61.8 12.7 %collective-permute-start = (bf16[128,1024]{1,0:T(8,128)(2,1)}, bf16[128,1024]{1,0:T(8,128)(2,1)S(1)}, u32[]{:S(2)}, u32[]{:S(2)}) collective-permute-start(bf16[128,1024]{1,0:T(8,128)(2,1)} %get-tuple-element.41), channel_id=1, source_target_pairs={{0,96},{16,112},{32,0},{48,16},{64,32},{80,48},{96,64},{112,80},{1... | collective-permute-start | bytes 786440 | tf_op jit(solution)/shard_map/ppermute | solution.py:310
  63.8 10.9 %collective-permute-start.3 = (bf16[128,1024]{1,0:T(8,128)(2,1)S(1)}, bf16[128,1024]{1,0:T(8,128)(2,1)S(1)}, u32[]{:S(2)}, u32[]{:S(2)}) collective-permute-start(bf16[128,1024]{1,0:T(8,128)(2,1)S(1)} %copy-done.10), channel_id=1, source_target_pairs={{0,32},{16,48},{32,64},{48,80},{64,96},{80,112},{96,0},{112,16},{1... | collective-permute-start | bytes 786440 | tf_op jit(solution)/shard_map/ppermute | solution.py:310
  69.1 10.7 %collective-permute-start.2 = (bf16[128,1024]{1,0:T(8,128)(2,1)S(1)}, bf16[128,1024]{1,0:T(8,128)(2,1)S(1)}, u32[]{:S(2)}, u32[]{:S(2)}) collective-permute-start(bf16[128,1024]{1,0:T(8,128)(2,1)S(1)} %add_convert_fusion.1), channel_id=1, source_target_pairs={{0,32},{16,48},{32,64},{48,80},{64,96},{80,112},{96,0},{112,16},{1... | collective-permute-start | bytes 786440 | tf_op jit(solution)/shard_map/ppermute | solution.py:310
  69.3 10.5 %collective-permute-start.5 = (bf16[128,1024]{1,0:T(8,128)(2,1)S(1)}, bf16[128,1024]{1,0:T(8,128)(2,1)S(1)}, u32[]{:S(2)}, u32[]{:S(2)}) collective-permute-start(bf16[128,1024]{1,0:T(8,128)(2,1)S(1)} %add_convert_fusion), channel_id=1, source_target_pairs={{0,96},{16,112},{32,0},{48,16},{64,32},{80,48},{96,64},{112,80},{1... | collective-permute-start | bytes 786440 | tf_op jit(solution)/shard_map/ppermute | solution.py:310
  80.0 19.3 %collective-permute-start.6 = (bf16[256,1024]{1,0:T(8,128)(2,1)S(1)}, bf16[256,1024]{1,0:T(8,128)(2,1)S(1)}, u32[]{:S(2)}, u32[]{:S(2)}) collective-permute-start(bf16[256,1024]{1,0:T(8,128)(2,1)S(1)} %join.1.mine), channel_id=1, source_target_pairs={{0,16},{16,0},{32,48},{48,32},{64,80},{80,64},{96,112},{112,96},{1... | collective-permute-start | bytes 1572872 | tf_op jit(solution)/shard_map/ppermute | solution.py:378
  91.9 20.1 %all-to-all-start.2 = ((bf16[8,64,512]{2,1,0:T(8,128)(2,1)}), bf16[8,64,512]{2,1,0:T(8,128)(2,1)S(1)}, u32[]{:S(2)}, u32[]{:S(2)}) async-start(bf16[8,64,512]{2,1,0:T(8,128)(2,1)} %square_grads.1.after), calls=%async_computation.2 | async-start | bytes 1048576 | tf_op jit(solution)/shard_map/all_to_all | solution.py:306
  99.5 20.4 %collective-permute-start.8 = (bf16[256,1024]{1,0:T(8,128)(2,1)S(1)}, bf16[256,1024]{1,0:T(8,128)(2,1)S(1)}, u32[]{:S(2)}, u32[]{:S(2)}) collective-permute-start(bf16[256,1024]{1,0:T(8,128)(2,1)S(1)} %pair.1.own), channel_id=1, source_target_pairs={{0,96},{16,112},{32,0},{48,16},{64,32},{80,48},{96,64},{112,80},{1... | collective-permute-start | bytes 1572872 | tf_op jit(solution)/shard_map/ppermute | solution.py:310
  102.8 18.8 %collective-permute-start.7 = (bf16[256,1024]{1,0:T(8,128)(2,1)S(1)}, bf16[256,1024]{1,0:T(8,128)(2,1)S(1)}, u32[]{:S(2)}, u32[]{:S(2)}) collective-permute-start(bf16[256,1024]{1,0:T(8,128)(2,1)S(1)} %pair.1.own), channel_id=1, source_target_pairs={{0,32},{16,48},{32,64},{48,80},{64,96},{80,112},{96,0},{112,16},{1... | collective-permute-start | bytes 1572872 | tf_op jit(solution)/shard_map/ppermute | solution.py:310
  112.8 19.6 %all-to-all-start.3 = ((bf16[8,64,512]{2,1,0:T(8,128)(2,1)}), bf16[8,64,512]{2,1,0:T(8,128)(2,1)S(1)}, u32[]{:S(2)}, u32[]{:S(2)}) async-start(bf16[8,64,512]{2,1,0:T(8,128)(2,1)} %total.1), calls=%async_computation.3 | async-start | bytes 1048576 | tf_op jit(solution)/shard_map/all_to_all | solution.py:306
  121.6 10.7 %collective-permute-start.9 = (bf16[128,1024]{1,0:T(8,128)(2,1)S(1)}, bf16[128,1024]{1,0:T(8,128)(2,1)S(1)}, u32[]{:S(2)}, u32[]{:S(2)}) collective-permute-start(bf16[128,1024]{1,0:T(8,128)(2,1)S(1)} %get-tuple-element.48), channel_id=1, source_target_pairs={{0,32},{16,48},{32,64},{48,80},{64,96},{80,112},{96,0},{112,16},{1... | collective-permute-start | bytes 786440 | tf_op jit(solution)/shard_map/ppermute | solution.py:310
  121.7 10.7 %collective-permute-start.10 = (bf16[128,1024]{1,0:T(8,128)(2,1)S(1)}, bf16[128,1024]{1,0:T(8,128)(2,1)S(1)}, u32[]{:S(2)}, u32[]{:S(2)}) collective-permute-start(bf16[128,1024]{1,0:T(8,128)(2,1)S(1)} %get-tuple-element.49), channel_id=1, source_target_pairs={{0,96},{16,112},{32,0},{48,16},{64,32},{80,48},{96,64},{112,80},{1... | collective-permute-start | bytes 786440 | tf_op jit(solution)/shard_map/ppermute | solution.py:310
  (2 other events, 6.4 us)

commit v6 on v5

--- a/solution.py
+++ b/solution.py
@@ -208,7 +208,7 @@
     ig_ref[...] = tn(r_ref[:, 32:64, :].reshape(512, 1024), w_up[...]).astype(BF)
 
 
-def total(t_ref, after, out_ref):
+def total(t_ref, out_ref):
     sums = t_ref[0].astype(F32)
     for i in range(1, 8):
         sums = sums + t_ref[i].astype(F32)
@@ -393,20 +393,20 @@
         moved=5 * 10**6,
     )
     tail_parts = exchange(tail, "dp")
+    (tail_sums,) = run(
+        total, (tail_parts,), (far(8, 64, 512),), 20, flops=10**6, moved=10**6
+    )
     mixed, input_grad = run(
         outputs,
         (w_up, w_down, got),
         (like(1024, 512),) * 2,
         20,
         hbm=2,
-        after=(tail,),
+        after=(tail_sums,),
         scratch=[square, square],
         sems=(2,),
         flops=10**9,
         moved=5 * 10**6,
-    )
-    (tail_sums,) = run(
-        total, (tail_parts,), (far(8, 64, 512),), 20, after=(mixed,), flops=10**6, moved=10**6
     )
     tail_all = exchange(tail_sums, "dp")
     wide = (like(2, 1024, 256, dtype=F32), like(2, 256, 1024, dtype=F32))

time: 134 us -> 135 us (level)
  local copies, waits for them, and re-layouts: 1.64 us -> 0.06 us
  waiting for transfers between devices: 58.9 us -> 60.4 us
    all_to_all x4, waiting for transfers between devices: 35.4 us -> 40.6 us  [exchange(): return lax.all_to_all(values, axis, split_axis=0, concat_axis=0, tiled=True)]
    ppermute x10, waiting for transfers between devices: 23.4 us -> 19.8 us  [shifted(): return lax.ppermute(part, 'dp', shift_z(step))]
    unnamed x22, local copies, waits for them, and re-layouts: 1.64 us -> 0.06 us
where the time goes in v6:
time: 135 us; the launch traced here: 134 us
  waiting for transfers between devices  60.4 us (45%)
  starting transfers between devices  40.8 us (30%)
  Pallas kernels  31.5 us (23%)
    all_to_all x4, waiting for transfers between devices, exchange(): return lax.all_to_all(values, axis, split_axis=0, concat_axis=0, tiled=True)  40.6 us
    pallas_call x11, Pallas kernels, run(): pl.pallas_call(kernel, out_shape=out_shape, in_specs=placed(pltpu.HBM, hb...  31.5 us
    all_to_all x4, starting transfers between devices, exchange(): return lax.all_to_all(values, axis, split_axis=0, concat_axis=0, tiled=True)  21.8 us
    ppermute x10, waiting for transfers between devices, shifted(): return lax.ppermute(part, 'dp', shift_z(step))  19.8 us
    ppermute x10, starting transfers between devices, shifted(): return lax.ppermute(part, 'dp', shift_z(step))  16.1 us
    ppermute x1, starting transfers between devices, per_device(): other = lax.ppermute(part, 'dp', SWAP_X)  2.81 us
  transfers between devices with their start and end apart: 15, of which 10 were waited for; matrix products, arithmetic and copies ran while one was open for 0% of the time, Pallas kernels for 10%

profile of v6, /device:TPU:24, one launch (start us, length us, event | category | flops | bytes accessed | tf_op | source)
XLA Modules:
  0.0 133.9 jit_solution(12762496776485776720)
XLA Ops:
  0.6 3.9 %stage_one.1.mark = bf16[16,64,1024]{2,1,0:T(8,128)(2,1)} custom-call(bf16[1024,512]{1,0:T(8,128)(2,1)} %tok_hbm.3, bf16[1024,512]{1,0:T(8,128)(2,1)} %cot_hbm.3, bf16[2,256,256]{2,1,0:T(8,128)(2,1)} %fu_ref.1, bf16[2,256,256]{2,1,0:T(8,128)(2,1)} %sd_ref.1, s32[64,128]{1,0:T(8,128)} %bitcast.2, s32[64,128]{1,0:T(8,128)} %bitcast.4), custom_call_target="tpu_custom_call" | custom-call | flops 2000000000 | bytes 5000000 | tf_op jit(solution)/shard_map/stage_one/pallas_call | solution.py:285
  4.6 5.8 %all-to-all-start = ((bf16[16,64,1024]{2,1,0:T(8,128)(2,1)}), bf16[16,64,1024]{2,1,0:T(8,128)(2,1)S(1)}, u32[]{:S(2)}, u32[]{:S(2)}) async-start(bf16[16,64,1024]{2,1,0:T(8,128)(2,1)} %stage_one.1.mark), calls=%async_computation | async-start | bytes 4194304 | tf_op jit(solution)/shard_map/all_to_all | solution.py:306
  10.5 2.1 %prepare.1 = (bf16[512,512]{1,0:T(8,128)(2,1)}, bf16[512,512]{1,0:T(8,128)(2,1)S(1)}, bf16[512,512]{1,0:T(8,128)(2,1)}, bf16[512,512]{1,0:T(8,128)(2,1)}, bf16[5...) custom-call(bf16[2,256,256]{2,1,0:T(8,128)(2,1)S(1)} %copy-done.4, bf16[2,256,256]{2,1,0:T(8,128)(2,1)S(1)} %copy-done.5, ...), custom_call_target="tpu_custom_call" | custom-call | flops 2000000000 | bytes 4000000 | tf_op jit(solution)/shard_map/prepare/pallas_call | solution.py:285
  12.5 27.3 %all-to-all-done.r_ref = bf16[16,64,1024]{2,1,0:T(8,128)(2,1)S(1)} async-done(((bf16[16,64,1024]{2,1,0:T(8,128)(2,1)}), bf16[16,64,1024]{2,1,0:T(8,128)(2,1)S(1)}, u32[]{:S(2)}, u32[]{:S(2)}) %all-to-all-start) | async-done | bytes 2097184 | tf_op jit(solution)/shard_map/all_to_all | solution.py:306
  39.8 12.8 %stage_two.1 = (bf16[16,64,1024]{2,1,0:T(8,128)(2,1)}, bf16[128,1024]{1,0:T(8,128)(2,1)}, bf16[128,1024]{1,0:T(8,128)(2,1)}, bf16[128,1024]{1,0:T(8,128)(2,1)}, ...) custom-call(bf16[512,512]{1,0:T(8,128)(2,1)} %get-tuple-element.33.s, ...), custom_call_target="tpu_custom_call" | custom-call | flops 8499999744 | bytes 9000000 | tf_op jit(solution)/shard_map/stage_two/pallas_call | solution.py:285
  52.6 5.0 %all-to-all-start.1 = ((bf16[16,64,1024]{2,1,0:T(8,128)(2,1)}), bf16[16,64,1024]{2,1,0:T(8,128)(2,1)S(1)}, u32[]{:S(2)}, u32[]{:S(2)}) async-start(bf16[16,64,1024]{2,1,0:T(8,128)(2,1)} %get-tuple-element.35), calls=%async_computation.1 | async-start | bytes 4194304 | tf_op jit(solution)/shard_map/all_to_all | solution.py:306
  57.7 1.9 %collective-permute-start.1 = (bf16[128,1024]{1,0:T(8,128)(2,1)}, bf16[128,1024]{1,0:T(8,128)(2,1)S(1)}, u32[]{:S(2)}, u32[]{:S(2)}) collective-permute-start(bf16[128,1024]{1,0:T(8,128)(2,1)} %get-tuple-element.43), channel_id=1, source_target_pairs={{0,32},{16,48},{32,64},{48,80},{64,96},{80,112},{96,0},{112,16},{1... | collective-permute-start | bytes 786440 | tf_op jit(solution)/shard_map/ppermute | solution.py:310
  59.6 2.3 %collective-permute-start.4 = (bf16[128,1024]{1,0:T(8,128)(2,1)}, bf16[128,1024]{1,0:T(8,128)(2,1)S(1)}, u32[]{:S(2)}, u32[]{:S(2)}) collective-permute-start(bf16[128,1024]{1,0:T(8,128)(2,1)} %get-tuple-element.47), channel_id=1, source_target_pairs={{0,96},{16,112},{32,0},{48,16},{64,32},{80,48},{96,64},{112,80},{1... | collective-permute-start | bytes 786440 | tf_op jit(solution)/shard_map/ppermute | solution.py:310
  61.8 1.9 %collective-permute-start = (bf16[128,1024]{1,0:T(8,128)(2,1)}, bf16[128,1024]{1,0:T(8,128)(2,1)S(1)}, u32[]{:S(2)}, u32[]{:S(2)}) collective-permute-start(bf16[128,1024]{1,0:T(8,128)(2,1)} %get-tuple-element.41), channel_id=1, source_target_pairs={{0,96},{16,112},{32,0},{48,16},{64,32},{80,48},{96,64},{112,80},{1... | collective-permute-start | bytes 786440 | tf_op jit(solution)/shard_map/ppermute | solution.py:310
  63.9 5.2 %collective-permute-done.1 = bf16[128,1024]{1,0:T(8,128)(2,1)S(1)} collective-permute-done((bf16[128,1024]{1,0:T(8,128)(2,1)}, bf16[128,1024]{1,0:T(8,128)(2,1)S(1)}, u32[]{:S(2)}, u32[]{:S(2)}) %collective-permute-start.1) | collective-permute-done | bytes 262176 | tf_op jit(solution)/shard_map/ppermute | solution.py:310
  69.3 3.3 %collective-permute-start.5 = (bf16[128,1024]{1,0:T(8,128)(2,1)S(1)}, bf16[128,1024]{1,0:T(8,128)(2,1)S(1)}, u32[]{:S(2)}, u32[]{:S(2)}) collective-permute-start(bf16[128,1024]{1,0:T(8,128)(2,1)S(1)} %add_convert_fusion), channel_id=1, source_target_pairs={{0,96},{16,112},{32,0},{48,16},{64,32},{80,48},{96,64},{112,80},{1... | collective-permute-start | bytes 786440 | tf_op jit(solution)/shard_map/ppermute | solution.py:310
  72.6 2.0 %collective-permute-done.f1 = bf16[128,1024]{1,0:T(8,128)(2,1)S(1)} collective-permute-done((bf16[128,1024]{1,0:T(8,128)(2,1)}, bf16[128,1024]{1,0:T(8,128)(2,1)S(1)}, u32[]{:S(2)}, u32[]{:S(2)}) %collective-permute-start) | collective-permute-done | bytes 262176 | tf_op jit(solution)/shard_map/ppermute | solution.py:310
  74.7 5.1 %collective-permute-done.2.f2 = bf16[128,1024]{1,0:T(8,128)(2,1)S(1)} collective-permute-done((bf16[128,1024]{1,0:T(8,128)(2,1)S(1)}, bf16[128,1024]{1,0:T(8,128)(2,1)S(1)}, u32[]{:S(2)}, u32[]{:S(2)}) %collective-permute-start.2) | collective-permute-done | bytes 262176 | tf_op jit(solution)/shard_map/ppermute | solution.py:310
  80.0 2.8 %collective-permute-start.6 = (bf16[256,1024]{1,0:T(8,128)(2,1)S(1)}, bf16[256,1024]{1,0:T(8,128)(2,1)S(1)}, u32[]{:S(2)}, u32[]{:S(2)}) collective-permute-start(bf16[256,1024]{1,0:T(8,128)(2,1)S(1)} %join.1.mine), channel_id=1, source_target_pairs={{0,16},{16,0},{32,48},{48,32},{64,80},{80,64},{96,112},{112,96},{1... | collective-permute-start | bytes 1572872 | tf_op jit(solution)/shard_map/ppermute | solution.py:378
  82.9 4.2 %all-to-all-done.1.r_ref = bf16[16,64,1024]{2,1,0:T(8,128)(2,1)S(1)} async-done(((bf16[16,64,1024]{2,1,0:T(8,128)(2,1)}), bf16[16,64,1024]{2,1,0:T(8,128)(2,1)S(1)}, u32[]{:S(2)}, u32[]{:S(2)}) %all-to-all-start.1) | async-done | bytes 2097184 | tf_op jit(solution)/shard_map/all_to_all | solution.py:306
  87.1 4.8 %square_grads.1 = bf16[8,64,512]{2,1,0:T(8,128)(2,1)} custom-call(bf16[1024,512]{1,0:T(8,128)(2,1)} %tok_hbm.3, bf16[1024,512]{1,0:T(8,128)(2,1)} %cot_hbm.3, bf16[512,512]{1,0:T(8,128)(2,1)} %get-tuple-element.36.src_hbm, bf16[512,512]{1,0:T(8,128)(2,1)} %get-tuple-element.37.tgt_hbm, bf16[16,64,1024]{2,1,0:T(8,128)(2,1)S(1)} %all-to-all-done.1.r_ref), custom_call_target="tpu_custom_call" | custom-call | flops 1600000000 | bytes 5000000 | tf_op jit(solution)/shard_map/square_grads/pallas_call | solution.py:285
  91.8 7.5 %all-to-all-start.2 = ((bf16[8,64,512]{2,1,0:T(8,128)(2,1)}), bf16[8,64,512]{2,1,0:T(8,128)(2,1)S(1)}, u32[]{:S(2)}, u32[]{:S(2)}) async-start(bf16[8,64,512]{2,1,0:T(8,128)(2,1)} %square_grads.1), calls=%async_computation.2 | async-start | bytes 1048576 | tf_op jit(solution)/shard_map/all_to_all | solution.py:306
  99.5 3.3 %collective-permute-start.8 = (bf16[256,1024]{1,0:T(8,128)(2,1)S(1)}, bf16[256,1024]{1,0:T(8,128)(2,1)S(1)}, u32[]{:S(2)}, u32[]{:S(2)}) collective-permute-start(bf16[256,1024]{1,0:T(8,128)(2,1)S(1)} %pair.1.own), channel_id=1, source_target_pairs={{0,96},{16,112},{32,0},{48,16},{64,32},{80,48},{96,64},{112,80},{1... | collective-permute-start | bytes 1572872 | tf_op jit(solution)/shard_map/ppermute | solution.py:310
  102.8 9.1 %all-to-all-done.2.t_ref = bf16[8,64,512]{2,1,0:T(8,128)(2,1)S(1)} async-done(((bf16[8,64,512]{2,1,0:T(8,128)(2,1)}), bf16[8,64,512]{2,1,0:T(8,128)(2,1)S(1)}, u32[]{:S(2)}, u32[]{:S(2)}) %all-to-all-start.2) | async-done | bytes 524320 | tf_op jit(solution)/shard_map/all_to_all | solution.py:306
  112.8 3.5 %all-to-all-start.3 = ((bf16[8,64,512]{2,1,0:T(8,128)(2,1)}), bf16[8,64,512]{2,1,0:T(8,128)(2,1)S(1)}, u32[]{:S(2)}, u32[]{:S(2)}) async-start(bf16[8,64,512]{2,1,0:T(8,128)(2,1)} %total.1.after), calls=%async_computation.3 | async-start | bytes 1048576 | tf_op jit(solution)/shard_map/all_to_all | solution.py:306
  116.3 3.6 %collective-permute-done.8.right = bf16[256,1024]{1,0:T(8,128)(2,1)S(1)} collective-permute-done((bf16[256,1024]{1,0:T(8,128)(2,1)S(1)}, bf16[256,1024]{1,0:T(8,128)(2,1)S(1)}, u32[]{:S(2)}, u32[]{:S(2)}) %collective-permute-start.8) | collective-permute-done | bytes 524320 | tf_op jit(solution)/shard_map/ppermute | solution.py:310
  121.7 3.2 %collective-permute-start.10 = (bf16[128,1024]{1,0:T(8,128)(2,1)S(1)}, bf16[128,1024]{1,0:T(8,128)(2,1)S(1)}, u32[]{:S(2)}, u32[]{:S(2)}) collective-permute-start(bf16[128,1024]{1,0:T(8,128)(2,1)S(1)} %get-tuple-element.49), channel_id=1, source_target_pairs={{0,96},{16,112},{32,0},{48,16},{64,32},{80,48},{96,64},{112,80},{1... | collective-permute-start | bytes 786440 | tf_op jit(solution)/shard_map/ppermute | solution.py:310
  126.7 3.5 %outputs.1 = (bf16[1024,512]{1,0:T(8,128)(2,1)}, bf16[1024,512]{1,0:T(8,128)(2,1)}) custom-call(bf16[512,512]{1,0:T(8,128)(2,1)} %get-tuple-element.31.up_hbm, bf16[512,512]{1,0:T(8,128)(2,1)} %get-tuple-element.32.down_hbm, bf16[16,64,1024]{2,1,0:T(8,128)(2,1)S(1)} %copy-done.1, bf16[8,64,512]{2,1,0:T(8,128)(2,1)} %total.1.after), custom_call_target="tpu_custom_call" | custom-call | flops 1000000000 | bytes 5000000 | tf_op jit(solution)/shard_map/outputs/pallas_call | solution.py:285
  130.2 2.1 %collective-permute-done.9.f_far = bf16[128,1024]{1,0:T(8,128)(2,1)S(1)} collective-permute-done((bf16[128,1024]{1,0:T(8,128)(2,1)S(1)}, bf16[128,1024]{1,0:T(8,128)(2,1)S(1)}, u32[]{:S(2)}, u32[]{:S(2)}) %collective-permute-start.9) | collective-permute-done | bytes 262176 | tf_op jit(solution)/shard_map/ppermute | solution.py:310
  (41 shorter events, 6.6 us)
Async XLA Ops:
  4.6 5.8 %copy-start.4 = (bf16[2,256,256]{2,1,0:T(8,128)(2,1)S(1)}, bf16[2,256,256]{2,1,0:T(8,128)(2,1)}, u32[]{:S(2)}) copy-start(bf16[2,256,256]{2,1,0:T(8,128)(2,1)} %fu_ref.1) | copy-start | bytes 786436
  4.6 5.8 %copy-start.5 = (bf16[2,256,256]{2,1,0:T(8,128)(2,1)S(1)}, bf16[2,256,256]{2,1,0:T(8,128)(2,1)}, u32[]{:S(2)}) copy-start(bf16[2,256,256]{2,1,0:T(8,128)(2,1)} %sd_ref.1) | copy-start | bytes 786436
  4.6 5.8 %copy-start.6 = (s32[8192]{0:T(1024)S(1)}, s32[8192]{0:T(1024)}, u32[]{:S(2)}) copy-start(s32[8192]{0:T(1024)} %param.13) | copy-start | bytes 98308
  4.6 35.2 %all-to-all-start = ((bf16[16,64,1024]{2,1,0:T(8,128)(2,1)}), bf16[16,64,1024]{2,1,0:T(8,128)(2,1)S(1)}, u32[]{:S(2)}, u32[]{:S(2)}) async-start(bf16[16,64,1024]{2,1,0:T(8,128)(2,1)} %stage_one.1.mark), calls=%async_computation | async-start | bytes 4194304 | tf_op jit(solution)/shard_map/all_to_all | solution.py:306
  52.6 11.2 %copy-start.10 = (bf16[128,1024]{1,0:T(8,128)(2,1)S(1)}, bf16[128,1024]{1,0:T(8,128)(2,1)}, u32[]{:S(2)}) copy-start(bf16[128,1024]{1,0:T(8,128)(2,1)} %get-tuple-element.45) | copy-start | bytes 786436
  52.6 16.5 %copy-start.9 = (bf16[128,1024]{1,0:T(8,128)(2,1)S(1)}, bf16[128,1024]{1,0:T(8,128)(2,1)}, u32[]{:S(2)}) copy-start(bf16[128,1024]{1,0:T(8,128)(2,1)} %get-tuple-element.42) | copy-start | bytes 786436
  52.6 16.6 %copy-start.8 = (bf16[128,1024]{1,0:T(8,128)(2,1)S(1)}, bf16[128,1024]{1,0:T(8,128)(2,1)}, u32[]{:S(2)}) copy-start(bf16[128,1024]{1,0:T(8,128)(2,1)} %get-tuple-element.46) | copy-start | bytes 786436
  52.6 27.2 %copy-start.2 = (bf16[128,1024]{1,0:T(8,128)(2,1)S(1)}, bf16[128,1024]{1,0:T(8,128)(2,1)}, u32[]{:S(2)}) copy-start(bf16[128,1024]{1,0:T(8,128)(2,1)} %get-tuple-element.40.f0) | copy-start | bytes 786436
  52.6 27.2 %copy-start.3 = (bf16[128,1024]{1,0:T(8,128)(2,1)S(1)}, bf16[128,1024]{1,0:T(8,128)(2,1)}, u32[]{:S(2)}) copy-start(bf16[128,1024]{1,0:T(8,128)(2,1)} %get-tuple-element.44.s0) | copy-start | bytes 786436
  52.6 34.4 %all-to-all-start.1 = ((bf16[16,64,1024]{2,1,0:T(8,128)(2,1)}), bf16[16,64,1024]{2,1,0:T(8,128)(2,1)S(1)}, u32[]{:S(2)}, u32[]{:S(2)}) async-start(bf16[16,64,1024]{2,1,0:T(8,128)(2,1)} %get-tuple-element.35), calls=%async_computation.1 | async-start | bytes 4194304 | tf_op jit(solution)/shard_map/all_to_all | solution.py:306
  57.7 11.4 %collective-permute-start.1 = (bf16[128,1024]{1,0:T(8,128)(2,1)}, bf16[128,1024]{1,0:T(8,128)(2,1)S(1)}, u32[]{:S(2)}, u32[]{:S(2)}) collective-permute-start(bf16[128,1024]{1,0:T(8,128)(2,1)} %get-tuple-element.43), channel_id=1, source_target_pairs={{0,32},{16,48},{32,64},{48,80},{64,96},{80,112},{96,0},{112,16},{1... | collective-permute-start | bytes 786440 | tf_op jit(solution)/shard_map/ppermute | solution.py:310
  59.6 9.6 %collective-permute-start.4 = (bf16[128,1024]{1,0:T(8,128)(2,1)}, bf16[128,1024]{1,0:T(8,128)(2,1)S(1)}, u32[]{:S(2)}, u32[]{:S(2)}) collective-permute-start(bf16[128,1024]{1,0:T(8,128)(2,1)} %get-tuple-element.47), channel_id=1, source_target_pairs={{0,96},{16,112},{32,0},{48,16},{64,32},{80,48},{96,64},{112,80},{1... | collective-permute-start | bytes 786440 | tf_op jit(solution)/shard_map/ppermute | solution.py:310
  61.8 12.7 %collective-permute-start = (bf16[128,1024]{1,0:T(8,128)(2,1)}, bf16[128,1024]{1,0:T(8,128)(2,1)S(1)}, u32[]{:S(2)}, u32[]{:S(2)}) collective-permute-start(bf16[128,1024]{1,0:T(8,128)(2,1)} %get-tuple-element.41), channel_id=1, source_target_pairs={{0,96},{16,112},{32,0},{48,16},{64,32},{80,48},{96,64},{112,80},{1... | collective-permute-start | bytes 786440 | tf_op jit(solution)/shard_map/ppermute | solution.py:310
  63.8 10.9 %collective-permute-start.3 = (bf16[128,1024]{1,0:T(8,128)(2,1)S(1)}, bf16[128,1024]{1,0:T(8,128)(2,1)S(1)}, u32[]{:S(2)}, u32[]{:S(2)}) collective-permute-start(bf16[128,1024]{1,0:T(8,128)(2,1)S(1)} %copy-done.10), channel_id=1, source_target_pairs={{0,32},{16,48},{32,64},{48,80},{64,96},{80,112},{96,0},{112,16},{1... | collective-permute-start | bytes 786440 | tf_op jit(solution)/shard_map/ppermute | solution.py:310
  69.1 10.7 %collective-permute-start.2 = (bf16[128,1024]{1,0:T(8,128)(2,1)S(1)}, bf16[128,1024]{1,0:T(8,128)(2,1)S(1)}, u32[]{:S(2)}, u32[]{:S(2)}) collective-permute-start(bf16[128,1024]{1,0:T(8,128)(2,1)S(1)} %add_convert_fusion.1), channel_id=1, source_target_pairs={{0,32},{16,48},{32,64},{48,80},{64,96},{80,112},{96,0},{112,16},{1... | collective-permute-start | bytes 786440 | tf_op jit(solution)/shard_map/ppermute | solution.py:310
  69.3 10.5 %collective-permute-start.5 = (bf16[128,1024]{1,0:T(8,128)(2,1)S(1)}, bf16[128,1024]{1,0:T(8,128)(2,1)S(1)}, u32[]{:S(2)}, u32[]{:S(2)}) collective-permute-start(bf16[128,1024]{1,0:T(8,128)(2,1)S(1)} %add_convert_fusion), channel_id=1, source_target_pairs={{0,96},{16,112},{32,0},{48,16},{64,32},{80,48},{96,64},{112,80},{1... | collective-permute-start | bytes 786440 | tf_op jit(solution)/shard_map/ppermute | solution.py:310
  80.0 19.3 %collective-permute-start.6 = (bf16[256,1024]{1,0:T(8,128)(2,1)S(1)}, bf16[256,1024]{1,0:T(8,128)(2,1)S(1)}, u32[]{:S(2)}, u32[]{:S(2)}) collective-permute-start(bf16[256,1024]{1,0:T(8,128)(2,1)S(1)} %join.1.mine), channel_id=1, source_target_pairs={{0,16},{16,0},{32,48},{48,32},{64,80},{80,64},{96,112},{112,96},{1... | collective-permute-start | bytes 1572872 | tf_op jit(solution)/shard_map/ppermute | solution.py:378
  91.8 20.1 %all-to-all-start.2 = ((bf16[8,64,512]{2,1,0:T(8,128)(2,1)}), bf16[8,64,512]{2,1,0:T(8,128)(2,1)S(1)}, u32[]{:S(2)}, u32[]{:S(2)}) async-start(bf16[8,64,512]{2,1,0:T(8,128)(2,1)} %square_grads.1), calls=%async_computation.2 | async-start | bytes 1048576 | tf_op jit(solution)/shard_map/all_to_all | solution.py:306
  99.5 20.4 %collective-permute-start.8 = (bf16[256,1024]{1,0:T(8,128)(2,1)S(1)}, bf16[256,1024]{1,0:T(8,128)(2,1)S(1)}, u32[]{:S(2)}, u32[]{:S(2)}) collective-permute-start(bf16[256,1024]{1,0:T(8,128)(2,1)S(1)} %pair.1.own), channel_id=1, source_target_pairs={{0,96},{16,112},{32,0},{48,16},{64,32},{80,48},{96,64},{112,80},{1... | collective-permute-start | bytes 1572872 | tf_op jit(solution)/shard_map/ppermute | solution.py:310
  102.8 18.8 %collective-permute-start.7 = (bf16[256,1024]{1,0:T(8,128)(2,1)S(1)}, bf16[256,1024]{1,0:T(8,128)(2,1)S(1)}, u32[]{:S(2)}, u32[]{:S(2)}) collective-permute-start(bf16[256,1024]{1,0:T(8,128)(2,1)S(1)} %pair.1.own), channel_id=1, source_target_pairs={{0,32},{16,48},{32,64},{48,80},{64,96},{80,112},{96,0},{112,16},{1... | collective-permute-start | bytes 1572872 | tf_op jit(solution)/shard_map/ppermute | solution.py:310
  112.8 19.6 %all-to-all-start.3 = ((bf16[8,64,512]{2,1,0:T(8,128)(2,1)}), bf16[8,64,512]{2,1,0:T(8,128)(2,1)S(1)}, u32[]{:S(2)}, u32[]{:S(2)}) async-start(bf16[8,64,512]{2,1,0:T(8,128)(2,1)} %total.1.after), calls=%async_computation.3 | async-start | bytes 1048576 | tf_op jit(solution)/shard_map/all_to_all | solution.py:306
  116.3 10.4 %copy-start.1 = (bf16[16,64,1024]{2,1,0:T(8,128)(2,1)S(1)}, bf16[16,64,1024]{2,1,0:T(8,128)(2,1)}, u32[]{:S(2)}) copy-start(bf16[16,64,1024]{2,1,0:T(8,128)(2,1)} %copy-done) | copy-start | bytes 6291460
  121.6 10.7 %collective-permute-start.9 = (bf16[128,1024]{1,0:T(8,128)(2,1)S(1)}, bf16[128,1024]{1,0:T(8,128)(2,1)S(1)}, u32[]{:S(2)}, u32[]{:S(2)}) collective-permute-start(bf16[128,1024]{1,0:T(8,128)(2,1)S(1)} %get-tuple-element.48), channel_id=1, source_target_pairs={{0,32},{16,48},{32,64},{48,80},{64,96},{80,112},{96,0},{112,16},{1... | collective-permute-start | bytes 786440 | tf_op jit(solution)/shard_map/ppermute | solution.py:310
  121.7 10.7 %collective-permute-start.10 = (bf16[128,1024]{1,0:T(8,128)(2,1)S(1)}, bf16[128,1024]{1,0:T(8,128)(2,1)S(1)}, u32[]{:S(2)}, u32[]{:S(2)}) collective-permute-start(bf16[128,1024]{1,0:T(8,128)(2,1)S(1)} %get-tuple-element.49), channel_id=1, source_target_pairs={{0,96},{16,112},{32,0},{48,16},{64,32},{80,48},{96,64},{112,80},{1... | collective-permute-start | bytes 786440 | tf_op jit(solution)/shard_map/ppermute | solution.py:310
  (2 other events, 10.6 us)
